TPU v7x, 512 devices: a whole 4x4x16 slice. The times are simulated.
512 devices in a mesh: tm: 16 (over z_hi, y, core), rows: 32 (over x, z_lo).
Axes of the slice: x: 4, y: 4, z: 16 (z_hi: 2, z_lo: 8; z = z_hi * 8 + z_lo), core: 2. Of those that a mesh axis runs over, the one named last changes fastest.
Arguments:
- video_clip: bfloat16 [32, 64, 64, 128], P('tm', 'rows'), may hold values from -6 to 6
- first_kernel: bfloat16 [3, 3, 3, 128, 128], replicated, may hold values from -0.109375 to 0.109375
- second_kernel: bfloat16 [3, 3, 3, 128, 128], replicated, may hold values from -0.109375 to 0.109375
- cotangent: bfloat16 [32, 64, 64, 128], P('tm', 'rows'), may hold values from -6 to 6
Outputs:
- input_grad: bfloat16 [32, 64, 64, 128], P('tm', 'rows')
- weight_grads: float32 [2, 442368], P(None, ('tm', 'rows'))
All inputs are finite; a program needn't handle non-finite values.
Results may differ from a plain program's by a relative error of at most 0.0046.
Values may be sent and summed in bfloat16 or wider, within the bound.
No kernel may reach another device: no remote copies, remote signals or barrier semaphores. Data moves between devices by JAX's collectives and lax.ppermute only.
A program may use at most 64 MiB of HBM per device.

v0:
```python
import math

import jax
import jax.numpy as jnp
from jax import lax
from jax.sharding import PartitionSpec as P


def passed_along(shard, axis, by):
    size = lax.axis_size(axis)
    pairs = [(i, i + by) for i in range(size) if 0 <= i + by < size]
    return lax.ppermute(shard, axis, pairs)


def padded(shard, sides, width):
    for axis, dim in sides:
        size, length = (lax.axis_size(axis), shard.shape[dim])
        up = [(i, (i + 1) % size) for i in range(size - 1)]
        down = [(j, i) for i, j in up]
        last = lax.slice_in_dim(shard, length - width, length, axis=dim)
        initial = lax.slice_in_dim(shard, 0, width, axis=dim)
        before = lax.ppermute(last, axis, up)
        after = lax.ppermute(initial, axis, down)
        shard = jnp.concatenate([before, shard, after], axis=dim)
    return shard


def pad_columns(volume):
    return jnp.pad(volume, ((0, 0), (0, 0), (1, 1), (0, 0)))


def correlate(source, kernel, frames, row_count):
    columns = source.shape[2] - 2
    time_taps = kernel.shape[0]
    out_chans = kernel.shape[-1]
    running = jnp.zeros((frames * row_count * columns, out_chans), jnp.float32)
    for tap_t in range(time_taps):
        for tap_h in range(3):
            stripe = source[tap_t : tap_t + frames, tap_h : tap_h + row_count]
            triple = jnp.concatenate(
                [stripe[:, :, tap_w : tap_w + columns] for tap_w in range(3)], axis=-1
            )
            triple = triple.reshape(frames * row_count * columns, -1)
            running = running + jnp.dot(
                triple,
                kernel[tap_t, tap_h].reshape(-1, out_chans),
                preferred_element_type=jnp.float32,
            )
    return running.reshape(frames, row_count, columns, out_chans)


def weight_terms(source, gradient, frames, row_count):
    columns = source.shape[2] - 2
    flat_grad = gradient.reshape(frames * row_count * columns, -1)
    pieces = []
    for tap_t in range(3):
        for tap_h in range(3):
            stripe = source[tap_t : tap_t + frames, tap_h : tap_h + row_count]
            triple = jnp.concatenate(
                [stripe[:, :, tap_w : tap_w + columns] for tap_w in range(3)], axis=-1
            )
            triple = triple.reshape(frames * row_count * columns, -1)
            pieces.append(
                lax.dot_general(
                    triple, flat_grad, (((0,), (0,)), ((), ())), preferred_element_type=jnp.float32
                )
            )
    return jnp.stack(pieces).reshape(-1)


def flipped(kernel):
    return jnp.flip(kernel, (0, 1, 2)).transpose(0, 1, 2, 4, 3)


def fold_first(source, turned, row_count):
    leading = jnp.stack([source[0], source[0], source[1]])
    taps = jnp.stack([turned[2], turned[1], turned[2]])
    return correlate(leading, taps, 1, row_count)[0]


def silu_slope(values):
    sig_value = jax.nn.sigmoid(values)
    return sig_value * (1.0 + values * (1.0 - sig_value))


def extend_past(volume):
    recent = passed_along(volume, "tm", 1)
    leading = jnp.broadcast_to(volume[:1], recent.shape)
    recent = jnp.where(lax.axis_index("tm") == 0, leading, recent)
    stacked = jnp.concatenate([recent, volume], axis=0)
    rimmed = padded(stacked, (("rows", 1),), 1)
    return pad_columns(rimmed)


def extend_future(gradient):
    coming = passed_along(gradient, "tm", -1)
    stacked = jnp.concatenate([gradient, coming], axis=0)
    rimmed = padded(stacked, (("rows", 1),), 1)
    return pad_columns(rimmed)


def transpose_conv(source, kernel, frames, row_count):
    turned = flipped(kernel)
    result = correlate(source, turned, frames, row_count)
    first_fold = lax.cond(
        lax.axis_index("tm") == 0,
        lambda: fold_first(source, turned, row_count),
        lambda: jnp.zeros(result.shape[1:], jnp.float32),
    )
    return result.at[0].add(first_fold)


def per_device(video_clip, first_kernel, second_kernel, cotangent):
    frames, row_count, columns, channels = video_clip.shape
    clip_ext = extend_past(video_clip)
    pre_act = correlate(clip_ext, first_kernel, frames, row_count).astype(jnp.bfloat16)
    hidden = jax.nn.silu(pre_act.astype(jnp.float32)).astype(jnp.bfloat16)
    hidden_ext = extend_past(hidden)
    back_grad = transpose_conv(extend_future(cotangent), second_kernel, frames, row_count)
    act_grad = (back_grad * silu_slope(pre_act.astype(jnp.float32))).astype(jnp.bfloat16)
    second_terms = weight_terms(hidden_ext, cotangent, frames, row_count)
    branch_grad = transpose_conv(extend_future(act_grad), first_kernel, frames, row_count)
    input_grad = (cotangent.astype(jnp.float32) + branch_grad).astype(jnp.bfloat16)
    first_terms = weight_terms(clip_ext, act_grad, frames, row_count)
    shares = lax.psum_scatter(
        jnp.stack([first_terms, second_terms]), ("tm", "rows"), scatter_dimension=1, tiled=True
    )
    cell_total = frames * lax.axis_size("tm") * row_count * lax.axis_size("rows") * columns
    grad_scale = 1.0 / math.sqrt(cell_total)
    return (input_grad, shares * grad_scale)


def solution(mesh):
    return jax.shard_map(
        per_device,
        mesh=mesh,
        in_specs=(P("tm", "rows", None, None), P(), P(), P("tm", "rows", None, None)),
        out_specs=(P("tm", "rows", None, None), P(None, ("tm", "rows"))),
        check_vma=False,
    )
```

profile of v0, /device:TPU:1, one launch (start us, length us, event | category | flops | bytes accessed | tf_op | source)
XLA Modules:
  0.0 623.3 jit_solution(18075216522846448185)
XLA Ops:
  7.2 4.7 collective-permute-start.3
  12.0 6.1 collective-permute-start
  18.8 2.2 fusion.121
  21.1 1.4 copy.9
  22.5 1.4 copy.8
  24.0 1.0 fusion.122
  26.0 1.3 collective-permute-start.2
  27.3 4.0 collective-permute-start.1
  32.2 1.3 collective-permute-start.5
  33.5 4.0 collective-permute-start.4
  37.8 2.1 collective-permute-done.4
  48.2 0.9 add_dynamic-update-slice_fusion.1
  49.2 0.9 fusion.96
  50.1 4.0 collective-permute-start.6
  54.1 1.1 fusion.17
  55.3 2.1 collective-permute-start.9
  57.4 1.1 fusion.16
  60.5 1.3 collective-permute-start.8
  61.8 4.9 collective-permute-start.7
  66.7 1.3 collective-permute-start.11
  68.0 4.0 collective-permute-start.10
  77.2 4.3 pad_maximum_fusion.12
  85.5 529.6 %all-reduce.7.cloned.1.call-done = f32[2,442368]{1,0:T(2,128)} async-done(((f32[2,442368]{1,0:T(2,128)}), f32[2,442368]{1,0:T(2,128)}) %all-reduce.7.cloned.1.call-update) | async-done | bytes 3538960
  615.1 1.4 dynamic-slice_multiply_fusion
  (270 shorter events, 21.6 us)
Async XLA Ops:
  7.2 13.9 %copy-start = (bf16[3,3,3,128,128]{4,3,2,1,0:T(8,128)(2,1)S(1)}, bf16[3,3,3,128,128]{4,3,2,1,0:T(8,128)(2,1)}, u32[]{:S(2)}) copy-start(bf16[3,3,3,128,128]{4,3,2,1,0:T(8,128)(2,1)} %param.13) | copy-start | bytes 2654212
  7.2 607.9 %all-reduce.7.cloned.1.call-start = ((), (), s32[]{:S(2)}) async-start(), calls=%async_computation | async-start | bytes 7077888
  7.2 24.0 %collective-permute-start.3 = (bf16[2,2,64,128]{3,2,1,0:T(8,128)(2,1)}, bf16[2,2,64,128]{3,2,1,0:T(8,128)(2,1)}, u32[]{:S(2)}, u32[]{:S(2)}) collective-permute-start(bf16[2,2,64,128]{3,2,1,0:T(8,128)(2,1)} %param.12), channel_id=1, source_target_pairs={{0,32},{32,64},{64,96},{96,128},{128,160},{160,192},{192,224},{224... | collective-permute-start | bytes 196616 | tf_op jit(solution)/shard_map/ppermute | solution.py:12
  12.0 13.9 %collective-permute-start = (bf16[2,2,64,128]{3,2,1,0:T(8,128)(2,1)}, bf16[2,2,64,128]{3,2,1,0:T(8,128)(2,1)S(1)}, u32[]{:S(2)}, u32[]{:S(2)}) collective-permute-start(bf16[2,2,64,128]{3,2,1,0:T(8,128)(2,1)} %param.15), channel_id=1, source_target_pairs={{32,0},{64,32},{96,64},{128,96},{160,128},{192,160},{224,192},{256... | collective-permute-start | bytes 196616 | tf_op jit(solution)/shard_map/ppermute | solution.py:12
  25.9 11.6 %copy-start.52 = (bf16[2,2,64,128]{3,2,1,0:T(8,128)(2,1)}, bf16[2,2,64,128]{3,2,1,0:T(8,128)(2,1)S(1)}, u32[]{:S(2)}) copy-start(bf16[2,2,64,128]{3,2,1,0:T(8,128)(2,1)S(1)} %collective-permute-done) | copy-start | bytes 196612
  26.0 11.5 %collective-permute-start.2 = (bf16[4,1,64,128]{3,2,1,0:T(8,128)(2,1)S(1)}, bf16[4,1,64,128]{3,2,1,0:T(8,128)(2,1)S(1)}, u32[]{:S(2)}, u32[]{:S(2)}) collective-permute-start(bf16[4,1,64,128]{3,2,1,0:T(8,128)(2,1)S(1)} %get-tuple-element.245), channel_id=1, source_target_pairs={{1,0},{2,1},{3,2},{4,3},{5,4},{6,5},{7,6},{8,7},{9,8},{10,9},{11,1... | collective-permute-start | bytes 196616 | tf_op jit(solution)/shard_map/ppermute | solution.py:23
  27.3 10.2 %collective-permute-start.1 = (bf16[4,1,64,128]{3,2,1,0:T(8,128)(2,1)S(1)}, bf16[4,1,64,128]{3,2,1,0:T(8,128)(2,1)S(1)}, u32[]{:S(2)}, u32[]{:S(2)}) collective-permute-start(bf16[4,1,64,128]{3,2,1,0:T(8,128)(2,1)S(1)} %get-tuple-element.244), channel_id=1, source_target_pairs={{0,1},{1,2},{2,3},{3,4},{4,5},{5,6},{6,7},{7,8},{8,9},{9,10},{10,1... | collective-permute-start | bytes 196616 | tf_op jit(solution)/shard_map/ppermute | solution.py:22
  32.2 5.7 collective-permute-start.5
  33.5 6.5 %collective-permute-start.4 = (bf16[4,1,64,128]{3,2,1,0:T(8,128)(2,1)S(1)}, bf16[4,1,64,128]{3,2,1,0:T(8,128)(2,1)S(1)}, u32[]{:S(2)}, u32[]{:S(2)}) collective-permute-start(bf16[4,1,64,128]{3,2,1,0:T(8,128)(2,1)S(1)} %get-tuple-element.237), channel_id=1, source_target_pairs={{0,1},{1,2},{2,3},{3,4},{4,5},{5,6},{6,7},{7,8},{8,9},{9,10},{10,1... | collective-permute-start | bytes 196616 | tf_op jit(solution)/shard_map/ppermute | solution.py:22
  48.2 10.3 %copy-start.45 = (bf16[2,2,64,128]{3,2,1,0:T(8,128)(2,1)S(1)}, bf16[2,2,64,128]{3,2,1,0:T(8,128)(2,1)}, u32[]{:S(2)}) copy-start(bf16[2,2,64,128]{3,2,1,0:T(8,128)(2,1)} %copy-done.44) | copy-start | bytes 196612
  48.2 10.3 %copy-start.47 = (bf16[2,2,64,128]{3,2,1,0:T(8,128)(2,1)S(1)}, bf16[2,2,64,128]{3,2,1,0:T(8,128)(2,1)}, u32[]{:S(2)}) copy-start(bf16[2,2,64,128]{3,2,1,0:T(8,128)(2,1)} %copy-done.46) | copy-start | bytes 196612
  48.2 10.3 %copy-start.65 = (bf16[2,2,64,128]{3,2,1,0:T(8,128)(2,1)S(1)}, bf16[2,2,64,128]{3,2,1,0:T(8,128)(2,1)}, u32[]{:S(2)}) copy-start(bf16[2,2,64,128]{3,2,1,0:T(8,128)(2,1)} %copy-done.64) | copy-start | bytes 196612
  48.2 10.6 %copy-start.41 = (bf16[2,2,64,128]{3,2,1,0:T(8,128)(2,1)S(1)}, bf16[2,2,64,128]{3,2,1,0:T(8,128)(2,1)}, u32[]{:S(2)}) copy-start(bf16[2,2,64,128]{3,2,1,0:T(8,128)(2,1)} %copy-done.40) | copy-start | bytes 196612
  48.2 10.6 %copy-start.43 = (bf16[2,2,64,128]{3,2,1,0:T(8,128)(2,1)S(1)}, bf16[2,2,64,128]{3,2,1,0:T(8,128)(2,1)}, u32[]{:S(2)}) copy-start(bf16[2,2,64,128]{3,2,1,0:T(8,128)(2,1)} %copy-done.42) | copy-start | bytes 196612
  48.2 10.6 %copy-start.63 = (bf16[2,2,64,128]{3,2,1,0:T(8,128)(2,1)S(1)}, bf16[2,2,64,128]{3,2,1,0:T(8,128)(2,1)}, u32[]{:S(2)}) copy-start(bf16[2,2,64,128]{3,2,1,0:T(8,128)(2,1)} %copy-done.62) | copy-start | bytes 196612
  50.1 9.2 %copy-start.37 = (bf16[2,2,64,128]{3,2,1,0:T(8,128)(2,1)S(1)}, bf16[2,2,64,128]{3,2,1,0:T(8,128)(2,1)}, u32[]{:S(2)}) copy-start(bf16[2,2,64,128]{3,2,1,0:T(8,128)(2,1)} %copy-done.36) | copy-start | bytes 196612
  50.1 9.2 %copy-start.39 = (bf16[2,2,64,128]{3,2,1,0:T(8,128)(2,1)S(1)}, bf16[2,2,64,128]{3,2,1,0:T(8,128)(2,1)}, u32[]{:S(2)}) copy-start(bf16[2,2,64,128]{3,2,1,0:T(8,128)(2,1)} %copy-done.38) | copy-start | bytes 196612
  50.1 9.2 %copy-start.61 = (bf16[2,2,64,128]{3,2,1,0:T(8,128)(2,1)S(1)}, bf16[2,2,64,128]{3,2,1,0:T(8,128)(2,1)}, u32[]{:S(2)}) copy-start(bf16[2,2,64,128]{3,2,1,0:T(8,128)(2,1)} %copy-done.60) | copy-start | bytes 196612
  50.1 10.3 %collective-permute-start.6 = (bf16[2,2,64,128]{3,2,1,0:T(8,128)(2,1)S(1)}, bf16[2,2,64,128]{3,2,1,0:T(8,128)(2,1)S(1)}, u32[]{:S(2)}, u32[]{:S(2)}) collective-permute-start(bf16[2,2,64,128]{3,2,1,0:T(8,128)(2,1)S(1)} %get-tuple-element.247), channel_id=1, source_target_pairs={{32,0},{64,32},{96,64},{128,96},{160,128},{192,160},{224,192},{256... | collective-permute-start | bytes 196616 | tf_op jit(solution)/shard_map/ppermute | solution.py:12
  55.3 11.4 %collective-permute-start.9 = (bf16[2,2,64,128]{3,2,1,0:T(8,128)(2,1)S(1)}, bf16[2,2,64,128]{3,2,1,0:T(8,128)(2,1)S(1)}, u32[]{:S(2)}, u32[]{:S(2)}) collective-permute-start(bf16[2,2,64,128]{3,2,1,0:T(8,128)(2,1)S(1)} %get-tuple-element.246), channel_id=1, source_target_pairs={{0,32},{32,64},{64,96},{96,128},{128,160},{160,192},{192,224},{224... | collective-permute-start | bytes 196616 | tf_op jit(solution)/shard_map/ppermute | solution.py:12
  60.5 11.5 %collective-permute-start.8 = (bf16[4,1,64,128]{3,2,1,0:T(8,128)(2,1)S(1)}, bf16[4,1,64,128]{3,2,1,0:T(8,128)(2,1)S(1)}, u32[]{:S(2)}, u32[]{:S(2)}) collective-permute-start(bf16[4,1,64,128]{3,2,1,0:T(8,128)(2,1)S(1)} %get-tuple-element.234), channel_id=1, source_target_pairs={{1,0},{2,1},{3,2},{4,3},{5,4},{6,5},{7,6},{8,7},{9,8},{10,9},{11,1... | collective-permute-start | bytes 196616 | tf_op jit(solution)/shard_map/ppermute | solution.py:23
  61.8 10.3 %collective-permute-start.7 = (bf16[4,1,64,128]{3,2,1,0:T(8,128)(2,1)S(1)}, bf16[4,1,64,128]{3,2,1,0:T(8,128)(2,1)S(1)}, u32[]{:S(2)}, u32[]{:S(2)}) collective-permute-start(bf16[4,1,64,128]{3,2,1,0:T(8,128)(2,1)S(1)} %get-tuple-element.233), channel_id=1, source_target_pairs={{0,1},{1,2},{2,3},{3,4},{4,5},{5,6},{6,7},{7,8},{8,9},{9,10},{10,1... | collective-permute-start | bytes 196616 | tf_op jit(solution)/shard_map/ppermute | solution.py:22
  66.7 7.7 %collective-permute-start.11 = (bf16[4,1,64,128]{3,2,1,0:T(8,128)(2,1)S(1)}, bf16[4,1,64,128]{3,2,1,0:T(8,128)(2,1)S(1)}, u32[]{:S(2)}, u32[]{:S(2)}) collective-permute-start(bf16[4,1,64,128]{3,2,1,0:T(8,128)(2,1)S(1)} %get-tuple-element.230), channel_id=1, source_target_pairs={{1,0},{2,1},{3,2},{4,3},{5,4},{6,5},{7,6},{8,7},{9,8},{10,9},{11,1... | collective-permute-start | bytes 196616 | tf_op jit(solution)/shard_map/ppermute | solution.py:23
  68.0 6.4 %collective-permute-start.10 = (bf16[4,1,64,128]{3,2,1,0:T(8,128)(2,1)S(1)}, bf16[4,1,64,128]{3,2,1,0:T(8,128)(2,1)S(1)}, u32[]{:S(2)}, u32[]{:S(2)}) collective-permute-start(bf16[4,1,64,128]{3,2,1,0:T(8,128)(2,1)S(1)} %get-tuple-element.229), channel_id=1, source_target_pairs={{0,1},{1,2},{2,3},{3,4},{4,5},{5,6},{6,7},{7,8},{8,9},{9,10},{10,1... | collective-permute-start | bytes 196616 | tf_op jit(solution)/shard_map/ppermute | solution.py:22
  (69 other events, 178.1 us)
Sparse Core Ops, SparseCore 0:
  81.7 533.3 all-reduce.6
where the time goes:
time: 625 us; the launch traced here: 623 us
  waiting for transfers between devices  532 us (85%)
  starting transfers between devices  38.9 us (6%)
  between operations  16 us (3%)
  local copies, waits for them, and re-layouts  14.1 us (2%)
  matrix products  12.1 us (2%)
  other arithmetic  10.4 us (2%)
    unnamed x2, waiting for transfers between devices  530 us
    ppermute x4, starting transfers between devices, passed_along(): return lax.ppermute(shard, axis, pairs)  16.9 us
    ppermute x4, starting transfers between devices, padded(): before = lax.ppermute(last, axis, up)  16.9 us
  transfers between devices with their start and end apart: 13, of which 2 were waited for; matrix products, arithmetic and copies ran while one was open for 3% of the time, Pallas kernels for 0%

commit v1 on v0

v1 whole, which is shorter than its diff:
```python
import math

import jax
import jax.numpy as jnp
import numpy as np
from jax import lax
from jax.experimental import pallas as pl
from jax.experimental.pallas import tpu as pltpu
from jax.sharding import Mesh, PartitionSpec as P

TM = ("zh", "y", "c")
ROWS = ("x", "zl")
VMEM = pl.BlockSpec(memory_space=pltpu.VMEM)
PARAMS = pltpu.CompilerParams(vmem_limit_bytes=48 * 1024 * 1024)


def contract_first(lhs, rhs):
    return lax.dot_general(lhs, rhs, (((0,), (0,)), ((), ())), preferred_element_type=jnp.float32)


def fill_triples(src_ref, up_ref, dn_ref, triples_ref, frames):
    columns = src_ref.shape[2]
    chans = src_ref.shape[3]
    col = lax.broadcasted_iota(jnp.int32, (columns, chans), 0)
    for f in range(frames):
        for r in range(4):
            cells = up_ref[f] if r == 0 else dn_ref[f] if r == 3 else src_ref[f, r - 1]
            wide = cells.astype(jnp.float32)
            before = jnp.where(col == 0, 0.0, pltpu.roll(wide, 1, 0))
            after = jnp.where(col == columns - 1, 0.0, pltpu.roll(wide, columns - 1, 0))
            triples_ref[f, r, :, 0:chans] = before.astype(cells.dtype)
            triples_ref[f, r, :, chans : 2 * chans] = cells
            triples_ref[f, r, :, 2 * chans : 3 * chans] = after.astype(cells.dtype)


def stripe(triples_ref, f, count, b):
    part = triples_ref[f : f + count, b : b + 2]
    return part.reshape(count * 2 * part.shape[2], part.shape[3])


def conv_all(triples_ref, kernel_ref, frames):
    total = None
    for a in range(3):
        for b in range(3):
            term = jnp.dot(
                stripe(triples_ref, a, frames, b),
                kernel_ref[a * 3 + b],
                preferred_element_type=jnp.float32,
            )
            total = term if total is None else total + term
    return total


def fold_all(triples_ref, kernel_ref):
    total = None
    for f, a in ((0, 2), (0, 1), (1, 2)):
        for b in range(3):
            term = jnp.dot(
                stripe(triples_ref, f, 1, b),
                kernel_ref[a * 3 + b],
                preferred_element_type=jnp.float32,
            )
            total = term if total is None else total + term
    return total


def first_conv_kernel(src_ref, up_ref, dn_ref, kernel_ref, out_ref, triples_ref):
    fill_triples(src_ref, up_ref, dn_ref, triples_ref, 6)
    out_ref[...] = conv_all(triples_ref, kernel_ref, 4)

    @pl.when((lax.axis_index("c") == 1) & (lax.axis_index("zh") == 0) & (lax.axis_index("y") == 0))
    def _():
        out_ref[0:128, :] += fold_all(triples_ref, kernel_ref)


def input_conv_kernel(src_ref, up_ref, dn_ref, kernel_ref, cot_ref, out_ref, triples_ref, sum_ref):
    fill_triples(src_ref, up_ref, dn_ref, triples_ref, 4)
    sum_ref[...] = conv_all(triples_ref, kernel_ref, 2)

    @pl.when((lax.axis_index("c") == 0) & (lax.axis_index("zh") == 0) & (lax.axis_index("y") == 0))
    def _():
        sum_ref[0:128, :] += fold_all(triples_ref, kernel_ref)

    cot = cot_ref[...].reshape(256, 128).astype(jnp.float32)
    out_ref[...] = (cot + sum_ref[...]).astype(jnp.bfloat16).reshape(out_ref.shape)


def grads_kernel(own_ref, other_ref, triples_ref, send_ref, act_ref, terms_ref):
    core = lax.axis_index("c")
    own, other = own_ref[...], other_ref[...]
    pre_act = jnp.where(core == 0, own, other).astype(jnp.bfloat16).astype(jnp.float32)
    back_grad = jnp.where(core == 0, other, own)
    sig = 1.0 / (1.0 + jnp.exp(-pre_act))
    act_grad = (back_grad * (sig * (1.0 + pre_act * (1.0 - sig)))).astype(jnp.bfloat16)
    hidden = (pre_act * sig).astype(jnp.bfloat16)
    act_ref[...] = act_grad.reshape(act_ref.shape)

    @pl.when(core == 0)
    def _():
        for a in range(3):
            for b in range(3):
                start = (a * 3 + b) * 384
                terms_ref[start : start + 384, :] = contract_first(stripe(triples_ref, a, 4, b), act_grad)

    @pl.when(core == 1)
    def _():
        for a in range(3):
            for b in range(3):
                part = contract_first(hidden, stripe(triples_ref, a, 4, b))
                for d in range(3):
                    start = ((2 - a) * 9 + (2 - b) * 3 + (2 - d)) * 128
                    terms_ref[start : start + 128, :] = part[:, d * 128 : (d + 1) * 128]

    @pl.when((core == 1) & (lax.axis_index("zh") == 0) & (lax.axis_index("y") == 0))
    def _():
        for f, a in ((0, 2), (0, 1), (1, 2)):
            for b in range(3):
                part = contract_first(hidden[0:128], stripe(triples_ref, f, 1, b))
                for d in range(3):
                    start = ((2 - a) * 9 + (2 - b) * 3 + (2 - d)) * 128
                    terms_ref[start : start + 128, :] += part[:, d * 128 : (d + 1) * 128]

    for y in range(4):
        for x in range(4):
            blocks = []
            for zh in range(2):
                for c in range(2):
                    start = 54 * (((zh * 4 + y) * 2 + c) * 4 + x)
                    blocks.append(terms_ref[start : start + 54, :])
            blocks.append(jnp.zeros((8, 128), jnp.float32))
            send_ref[y * 4 + x] = jnp.concatenate(blocks, axis=0).astype(jnp.bfloat16)


def plane_sum_kernel(got_ref, send_ref, sum_ref):
    total = got_ref[0].astype(jnp.float32)
    for k in range(1, 16):
        total = total + got_ref[k].astype(jnp.float32)
    sum_ref[...] = total
    lane = lax.broadcasted_iota(jnp.int32, (8, 128), 1)
    for zh in range(2):
        for c in range(2):
            for zl in range(8):
                value = (zh * 2 + c) * 54 * 128 + zl * 864
                row, shift = value // 128, value % 128
                piece = sum_ref[row : row + 8, :]
                if shift:
                    after = sum_ref[row + 1 : row + 9, :]
                    piece = jnp.where(
                        lane < 128 - shift,
                        pltpu.roll(piece, 128 - shift, 1),
                        pltpu.roll(after, 128 - shift, 1),
                    )
                send_ref[zh * 8 + zl, c] = piece


def line_sum_kernel(got_ref, own_ref, send_ref):
    core = lax.axis_index("c")
    total = got_ref[0]
    for k in range(1, 16):
        total = total + got_ref[k]
    own_ref[...] = jnp.where(core == 0, total[0], total[1])
    send_ref[...] = jnp.where(core == 0, total[1], total[0])


def place_kernel(scale, own_ref, other_ref, out_ref):
    core = lax.axis_index("c")
    own, other = own_ref[...] * scale, other_ref[...] * scale
    shares = (jnp.where(core == 0, own, other), jnp.where(core == 0, other, own))
    for k in range(2):
        for r in range(7):
            width = min(128, 864 - 128 * r)
            out_ref[k : k + 1, 128 * r : 128 * r + width] = shares[k][r : r + 1, :width]


def call(kernel, out_shape, *args, scratch=()):
    many = isinstance(out_shape, (list, tuple))
    return pl.pallas_call(
        kernel,
        out_shape=out_shape,
        in_specs=[VMEM] * len(args),
        out_specs=[VMEM] * len(out_shape) if many else VMEM,
        scratch_shapes=scratch,
        compiler_params=PARAMS,
    )(*args)


def shaped(shape, dtype):
    return jax.ShapeDtypeStruct(shape, dtype)


def flipped(kernel):
    return jnp.flip(kernel, (0, 1, 2)).transpose(0, 1, 2, 4, 3)


def exchange_rows(source):
    count = lax.axis_size(ROWS)
    up = lax.ppermute(source[:, 1], ROWS, [(i, i + 1) for i in range(count - 1)])
    down = lax.ppermute(source[:, 0], ROWS, [(i + 1, i) for i in range(count - 1)])
    return up, down


SWAP = [(0, 1), (1, 0)]


def per_device(video_clip, first_kernel, second_kernel, cotangent):
    bf16, f32 = jnp.bfloat16, jnp.float32
    core = lax.axis_index("c")
    chip = lax.axis_index(("zh", "y"))
    other_cores = lax.ppermute(jnp.where(core == 0, cotangent, video_clip), "c", SWAP)
    beyond_pairs = [(2 * k + 1, 2 * k + 2) for k in range(7)] + [(2 * k + 2, 2 * k + 1) for k in range(7)]
    beyond = lax.ppermute(jnp.where(core == 0, cotangent, video_clip), TM, beyond_pairs)
    kernel = jnp.where(core == 0, first_kernel, flipped(second_kernel)).reshape(9, 384, 128)
    first_back = flipped(first_kernel).reshape(9, 384, 128)
    repeated = jnp.broadcast_to(video_clip[:1], video_clip.shape)
    beyond = jnp.where((core == 0) & (chip == 0), repeated, beyond)
    source = jnp.where(
        core == 0,
        jnp.concatenate([beyond, video_clip, other_cores], 0),
        jnp.concatenate([other_cores, cotangent, beyond], 0),
    )
    up, down = exchange_rows(source)
    own, triples = call(
        first_conv_kernel,
        (shaped((512, 128), f32), shaped((6, 4, 64, 384), bf16)),
        source, up, down, kernel,
    )
    other = lax.ppermute(own, "c", SWAP)
    send, act_grad = call(
        grads_kernel,
        (shaped((16, 224, 128), bf16), shaped((4, 2, 64, 128), bf16)),
        own, other, triples,
        scratch=[pltpu.VMEM((3456, 128), f32)],
    )
    got = lax.all_to_all(send, ("y", "x"), 0, 0, tiled=True)
    send = call(plane_sum_kernel, shaped((16, 2, 8, 128), f32), got, scratch=[pltpu.VMEM((224, 128), f32)])
    got = lax.all_to_all(send, ("zh", "zl"), 0, 0, tiled=True)
    own_share, send_share = call(line_sum_kernel, (shaped((8, 128), f32),) * 2, got)
    other_share = lax.ppermute(send_share, "c", SWAP)
    scale = 1.0 / math.sqrt(131072)
    weight_grads = call(
        lambda *refs: place_kernel(scale, *refs), shaped((2, 864), f32), own_share, other_share
    )
    later = lax.ppermute(act_grad[:2], TM, [(2 * k + 2, 2 * k + 1) for k in range(7)])
    grad_source = jnp.where(core == 0, act_grad, jnp.concatenate([act_grad[2:], later], 0))
    up, down = exchange_rows(grad_source)
    input_grad = call(
        input_conv_kernel,
        shaped((2, 2, 64, 128), bf16),
        grad_source, up, down, first_back, cotangent,
        scratch=[pltpu.VMEM((4, 4, 64, 384), bf16), pltpu.VMEM((256, 128), f32)],
    )
    return input_grad, weight_grads


def solution(mesh):
    fine = Mesh(np.asarray(mesh.devices).reshape(2, 4, 2, 4, 8), TM + ROWS)
    return jax.shard_map(
        per_device,
        mesh=fine,
        in_specs=(P(TM, ROWS, None, None), P(), P(), P(TM, ROWS, None, None)),
        out_specs=(P(TM, ROWS, None, None), P(None, TM + ROWS)),
        check_vma=False,
    )
```

time: 625 us -> 101 us (0.16)
  waiting for transfers between devices: 532 us -> 24.8 us
  starting transfers between devices: 38.9 us -> 60.9 us
  between operations: 16 us -> 0.93 us
  matrix products: 12.1 us -> 0 us
  other arithmetic: 10.4 us -> 1.33 us
  local copies, waits for them, and re-layouts: 14.1 us -> 5.77 us
  Pallas kernels: 0 us -> 6.73 us
    unnamed x2 -> x0, waiting for transfers between devices: 530 us -> none
    all_to_all x0 -> x2, starting transfers between devices: none -> 33.5 us  [the longest x1 22.7 us: per_device(): got = lax.all_to_all(send, ('y', 'x'), 0, 0, tiled=True)]
    all_to_all x0 -> x2, waiting for transfers between devices: none -> 20.5 us  [the longest x1 13.1 us: per_device(): got = lax.all_to_all(send, ('y', 'x'), 0, 0, tiled=True)]
    dot_general x45 -> x0, matrix products: 12.1 us -> none  [the longest x18 6.15 us: weight_terms(): lax.dot_general(triple, flat_grad, (((0,), (0,)), ((), ())), preferred_el...]
    ppermute x12 -> x9, starting transfers between devices: 38.9 us -> 27.5 us  [the longest x1 7.03 us: per_device(): other_share = lax.ppermute(send_share, 'c', SWAP)]
    slice x14 -> x1, local copies, waits for them, and re-layouts: 7.17 us -> 0.01 us  [per_device(): act_grad[2:]]
    pallas_call x0 -> x6, Pallas kernels: none -> 6.73 us  [call(): pl.pallas_call(kernel, out_shape=out_shape, in_specs=[VMEM] * len(args),...]
  transfers between devices with their start and end apart: 13 -> 11, of which waited for: 2 -> 4; matrix products, arithmetic and copies ran while one was open for 3% -> 6% of each run, Pallas kernels for 0% -> 2%
where the time goes in v1:
time: 101 us; the launch traced here: 100 us
  starting transfers between devices  60.9 us (60%)
  waiting for transfers between devices  24.8 us (25%)
  Pallas kernels  6.73 us (7%)
  local copies, waits for them, and re-layouts  5.77 us (6%)
  other arithmetic  1.33 us (1%)
    all_to_all x1, starting transfers between devices, per_device(): got = lax.all_to_all(send, ('y', 'x'), 0, 0, tiled=True)  22.7 us
    all_to_all x1, waiting for transfers between devices, per_device(): got = lax.all_to_all(send, ('y', 'x'), 0, 0, tiled=True)  13.1 us
    all_to_all x1, starting transfers between devices, per_device(): got = lax.all_to_all(send, ('zh', 'zl'), 0, 0, tiled=True)  10.7 us
    all_to_all x1, waiting for transfers between devices, per_device(): got = lax.all_to_all(send, ('zh', 'zl'), 0, 0, tiled=True)  7.38 us
    ppermute x1, starting transfers between devices, per_device(): other_share = lax.ppermute(send_share, 'c', SWAP)  7.03 us
    pallas_call x6, Pallas kernels, call(): pl.pallas_call(kernel, out_shape=out_shape, in_specs=[VMEM] * len(args),...  6.73 us
    ppermute x1, starting transfers between devices, per_device(): lax.ppermute(jnp.where(core == 0, cotangent, video_clip), 'c', SWAP)  4.86 us
    ppermute x1, starting transfers between devices, per_device(): lax.ppermute(jnp.where(core == 0, cotangent, video_clip), TM, beyond_pairs)  4.59 us
  transfers between devices with their start and end apart: 11, of which 4 were waited for; matrix products, arithmetic and copies ran while one was open for 6% of the time, Pallas kernels for 2%

profile of v1, /device:TPU:1, one launch (start us, length us, event | category | flops | bytes accessed | tf_op | source)
XLA Modules:
  0.0 100.5 jit_solution(18395160154093697346)
XLA Ops:
  0.6 0.9 fusion.1
  1.5 4.6 %collective-permute-start = (bf16[2,2,64,128]{3,2,0,1:T(8,128)(2,1)S(1)}, bf16[2,2,64,128]{3,2,0,1:T(8,128)(2,1)S(1)}, u32[]{:S(2)}, u32[]{:S(2)}) collective-permute-start(bf16[2,2,64,128]{3,2,0,1:T(8,128)(2,1)S(1)} %get-tuple-element.21), channel_id=1, source_target_pairs={{32,64},{96,128},{160,192},{224,256},{288,320},{352,384},{416,448}... | collective-permute-start | bytes 196616 | tf_op jit(solution)/shard_map/ppermute | solution.py:211
  6.1 4.9 %collective-permute-start.1 = (bf16[2,2,64,128]{3,2,0,1:T(8,128)(2,1)S(1)}, bf16[2,2,64,128]{3,2,0,1:T(8,128)(2,1)S(1)}, u32[]{:S(2)}, u32[]{:S(2)}) collective-permute-start(bf16[2,2,64,128]{3,2,0,1:T(8,128)(2,1)S(1)} %get-tuple-element.21), channel_id=1, source_target_pairs={{0,32},{32,0},{1,33},{33,1},{2,34},{34,2},{3,35},{35,3},{4,36},{36... | collective-permute-start | bytes 196616 | tf_op jit(solution)/shard_map/ppermute | solution.py:209
  11.0 0.8 slice_bitcast_fusion.4
  11.8 2.1 %copy.10 = bf16[3,3,3,128,128]{3,4,2,1,0:T(8,128)(2,1)S(1)} copy(bf16[3,3,3,128,128]{4,3,2,1,0:T(8,128)(2,1)} %param.5) | data formatting | bytes 1769472 | tf_op args[1]
  14.0 1.3 %collective-permute-start.2 = (bf16[6,64,128]{2,1,0:T(8,128)(2,1)S(1)}, bf16[6,64,128]{2,1,0:T(8,128)(2,1)S(1)}, u32[]{:S(2)}, u32[]{:S(2)}) collective-permute-start(bf16[6,64,128]{2,1,0:T(8,128)(2,1)S(1)} %get-tuple-element.15), channel_id=1, source_target_pairs={{0,1},{1,2},{2,3},{3,4},{4,5},{5,6},{6,7},{7,8},{8,9},{9,10},{10,1... | collective-permute-start | bytes 294920 | tf_op jit(solution)/shard_map/ppermute | solution.py:197
  15.3 1.3 %collective-permute-start.3 = (bf16[6,64,128]{2,1,0:T(8,128)(2,1)S(1)}, bf16[6,64,128]{2,1,0:T(8,128)(2,1)S(1)}, u32[]{:S(2)}, u32[]{:S(2)}) collective-permute-start(bf16[6,64,128]{2,1,0:T(8,128)(2,1)S(1)} %get-tuple-element.14), channel_id=1, source_target_pairs={{1,0},{2,1},{3,2},{4,3},{5,4},{6,5},{7,6},{8,7},{9,8},{10,9},{11,1... | collective-permute-start | bytes 294920 | tf_op jit(solution)/shard_map/ppermute | solution.py:198
  16.9 1.4 %copy.11 = bf16[3,3,3,128,128]{4,3,2,1,0:T(8,128)(2,1)S(1)} copy(bf16[3,3,3,128,128]{3,4,2,1,0:T(8,128)(2,1)S(1)} %bitcast_select_fusion) | data formatting | bytes 1769472 | tf_op jit(solution)/shard_map/jit(_where)/select_n | solution.py:212
  18.4 3.1 %collective-permute-done.3.dn_ref = bf16[6,64,128]{2,1,0:T(8,128)(2,1)S(1)} collective-permute-done((bf16[6,64,128]{2,1,0:T(8,128)(2,1)S(1)}, bf16[6,64,128]{2,1,0:T(8,128)(2,1)S(1)}, u32[]{:S(2)}, u32[]{:S(2)}) %collective-permute-start.3) | collective-permute-done | bytes 98336 | tf_op jit(solution)/shard_map/ppermute | solution.py:198
  21.5 1.5 %shard_map.59 = (f32[512,128]{1,0:T(8,128)S(1)}, bf16[6,4,64,384]{3,2,1,0:T(8,128)(2,1)S(1)}) custom-call(bf16[6,2,64,128]{3,2,1,0:T(8,128)(2,1)S(1)} %copy.12.src_ref, bf16[6,64,128]{2,1,0:T(8,128)(2,1)S(1)} %collective-permute-done.2.up_ref, bf16[6,64,128]{2,1,0:T(8,128)(2,1)S(1)} %collective-permute-done.3.dn_ref, bf16[9,384,128]{2,1,0:T(8,128)(2,1)S(1)} %bitcast.16), custom_call_target="tpu_custom_call" | custom-call | tf_op jit(solution)/shard_map/pallas_call | solution.py:177
  23.0 2.4 %collective-permute-start.4 = (f32[512,128]{1,0:T(8,128)S(1)}, f32[512,128]{1,0:T(8,128)S(1)}, u32[]{:S(2)}, u32[]{:S(2)}) collective-permute-start(f32[512,128]{1,0:T(8,128)S(1)} %get-tuple-element.8.own_ref), channel_id=1, source_target_pairs={{0,32},{32,0},{1,33},{33,1},{2,34},{34,2},{3,35},{35,3},{4,36},{36... | collective-permute-start | bytes 786440 | tf_op jit(solution)/shard_map/ppermute | solution.py:227
  25.4 1.1 %collective-permute-done.4.other_ref = f32[512,128]{1,0:T(8,128)S(1)} collective-permute-done((f32[512,128]{1,0:T(8,128)S(1)}, f32[512,128]{1,0:T(8,128)S(1)}, u32[]{:S(2)}, u32[]{:S(2)}) %collective-permute-start.4) | collective-permute-done | bytes 262176 | tf_op jit(solution)/shard_map/ppermute | solution.py:227
  26.5 2.5 %shard_map.60 = (bf16[16,224,128]{2,1,0:T(8,128)(2,1)}, bf16[4,2,64,128]{3,2,1,0:T(8,128)(2,1)S(1)}) custom-call(f32[512,128]{1,0:T(8,128)S(1)} %get-tuple-element.8.own_ref, f32[512,128]{1,0:T(8,128)S(1)} %collective-permute-done.4.other_ref, bf16[6,4,64,384]{3,2,1,0:T(8,128)(2,1)S(1)} %get-tuple-element.9.triples_ref), custom_call_target="tpu_custom_call" | custom-call | tf_op jit(solution)/shard_map/pallas_call | solution.py:177
  29.0 22.7 %all-to-all-start = ((bf16[16,224,128]{2,1,0:T(8,128)(2,1)}), bf16[16,224,128]{2,1,0:T(8,128)(2,1)S(1)}, u32[]{:S(2)}, u32[]{:S(2)}) async-start(bf16[16,224,128]{2,1,0:T(8,128)(2,1)} %get-tuple-element.11), calls=%async_computation | async-start | bytes 1835008 | tf_op jit(solution)/shard_map/all_to_all | solution.py:234
  51.8 1.4 %collective-permute-start.5 = (bf16[2,2,64,128]{3,2,0,1:T(8,128)(2,1)S(1)}, bf16[2,2,64,128]{3,2,0,1:T(8,128)(2,1)S(1)}, u32[]{:S(2)}, u32[]{:S(2)}) collective-permute-start(bf16[2,2,64,128]{3,2,0,1:T(8,128)(2,1)S(1)} %get-tuple-element.19), channel_id=1, source_target_pairs={{64,32},{128,96},{192,160},{256,224},{320,288},{384,352},{448,416}... | collective-permute-start | bytes 196616 | tf_op jit(solution)/shard_map/ppermute | solution.py:243
  53.2 13.1 %all-to-all-done.got_ref = bf16[16,224,128]{2,1,0:T(8,128)(2,1)S(1)} async-done(((bf16[16,224,128]{2,1,0:T(8,128)(2,1)}), bf16[16,224,128]{2,1,0:T(8,128)(2,1)S(1)}, u32[]{:S(2)}, u32[]{:S(2)}) %all-to-all-start) | async-done | bytes 917536 | tf_op jit(solution)/shard_map/all_to_all | solution.py:234
  66.3 0.9 shard_map.62
  67.2 10.7 %all-to-all-start.1 = ((f32[16,2,8,128]{3,2,1,0:T(8,128)}), f32[16,2,8,128]{3,2,1,0:T(8,128)S(1)}, u32[]{:S(2)}, u32[]{:S(2)}) async-start(f32[16,2,8,128]{3,2,1,0:T(8,128)} %shard_map.62), calls=%async_computation.1 | async-start | bytes 262144 | tf_op jit(solution)/shard_map/all_to_all | solution.py:236
  78.0 3.3 %collective-permute-start.6 = (bf16[4,64,128]{2,1,0:T(8,128)(2,1)S(1)}, bf16[4,64,128]{2,1,0:T(8,128)(2,1)S(1)}, u32[]{:S(2)}, u32[]{:S(2)}) collective-permute-start(bf16[4,64,128]{2,1,0:T(8,128)(2,1)S(1)} %get-tuple-element.17), channel_id=1, source_target_pairs={{0,1},{1,2},{2,3},{3,4},{4,5},{5,6},{6,7},{7,8},{8,9},{9,10},{10,1... | collective-permute-start | bytes 196616 | tf_op jit(solution)/shard_map/ppermute | solution.py:197
  81.3 1.3 %collective-permute-start.7 = (bf16[4,64,128]{2,1,0:T(8,128)(2,1)S(1)}, bf16[4,64,128]{2,1,0:T(8,128)(2,1)S(1)}, u32[]{:S(2)}, u32[]{:S(2)}) collective-permute-start(bf16[4,64,128]{2,1,0:T(8,128)(2,1)S(1)} %get-tuple-element.16), channel_id=1, source_target_pairs={{1,0},{2,1},{3,2},{4,3},{5,4},{6,5},{7,6},{8,7},{9,8},{10,9},{11,1... | collective-permute-start | bytes 196616 | tf_op jit(solution)/shard_map/ppermute | solution.py:198
  82.6 7.4 %all-to-all-done.1.got_ref = f32[16,2,8,128]{3,2,1,0:T(8,128)S(1)} async-done(((f32[16,2,8,128]{3,2,1,0:T(8,128)}), f32[16,2,8,128]{3,2,1,0:T(8,128)S(1)}, u32[]{:S(2)}, u32[]{:S(2)}) %all-to-all-start.1) | async-done | bytes 131104 | tf_op jit(solution)/shard_map/all_to_all | solution.py:236
  90.0 7.0 %collective-permute-start.8 = (f32[8,128]{1,0:T(8,128)S(1)}, f32[8,128]{1,0:T(8,128)S(1)}, u32[]{:S(2)}, u32[]{:S(2)}) collective-permute-start(f32[8,128]{1,0:T(8,128)S(1)} %get-tuple-element.13), channel_id=1, source_target_pairs={{0,32},{32,0},{1,33},{33,1},{2,34},{34,2},{3,35},{35,3},{4,36},{36... | collective-permute-start | bytes 12296 | tf_op jit(solution)/shard_map/ppermute | solution.py:238
  97.2 1.4 %copy.16 = bf16[3,3,3,128,128]{4,3,2,1,0:T(8,128)(2,1)S(1)} copy(bf16[3,3,3,128,128]{3,4,2,1,0:T(8,128)(2,1)S(1)} %reverse_bitcast_fusion) | data formatting | bytes 1769472 | tf_op jit(solution)/shard_map/transpose | solution.py:192
  98.6 1.3 %shard_map.61 = bf16[2,2,64,128]{3,2,1,0:T(8,128)(2,1)} custom-call(bf16[4,2,64,128]{3,2,1,0:T(8,128)(2,1)S(1)} %copy.17.src_ref, bf16[4,64,128]{2,1,0:T(8,128)(2,1)S(1)} %collective-permute-done.6.up_ref, bf16[4,64,128]{2,1,0:T(8,128)(2,1)S(1)} %collective-permute-done.7.dn_ref, bf16[9,384,128]{2,1,0:T(8,128)(2,1)S(1)} %bitcast.17, ...), custom_call_target="tpu_custom_call" | custom-call | tf_op jit(solution)/shard_map/pallas_call | solution.py:177
  (25 shorter events, 1.2 us)
Async XLA Ops:
  1.5 12.3 %collective-permute-start = (bf16[2,2,64,128]{3,2,0,1:T(8,128)(2,1)S(1)}, bf16[2,2,64,128]{3,2,0,1:T(8,128)(2,1)S(1)}, u32[]{:S(2)}, u32[]{:S(2)}) collective-permute-start(bf16[2,2,64,128]{3,2,0,1:T(8,128)(2,1)S(1)} %get-tuple-element.21), channel_id=1, source_target_pairs={{32,64},{96,128},{160,192},{224,256},{288,320},{352,384},{416,448}... | collective-permute-start | bytes 196616 | tf_op jit(solution)/shard_map/ppermute | solution.py:211
  6.1 7.7 %collective-permute-start.1 = (bf16[2,2,64,128]{3,2,0,1:T(8,128)(2,1)S(1)}, bf16[2,2,64,128]{3,2,0,1:T(8,128)(2,1)S(1)}, u32[]{:S(2)}, u32[]{:S(2)}) collective-permute-start(bf16[2,2,64,128]{3,2,0,1:T(8,128)(2,1)S(1)} %get-tuple-element.21), channel_id=1, source_target_pairs={{0,32},{32,0},{1,33},{33,1},{2,34},{34,2},{3,35},{35,3},{4,36},{36... | collective-permute-start | bytes 196616 | tf_op jit(solution)/shard_map/ppermute | solution.py:209
  11.8 4.8 %copy-start.2 = (bf16[3,3,3,128,128]{4,3,2,1,0:T(8,128)(2,1)S(1)}, bf16[3,3,3,128,128]{4,3,2,1,0:T(8,128)(2,1)}, u32[]{:S(2)}) copy-start(bf16[3,3,3,128,128]{4,3,2,1,0:T(8,128)(2,1)} %param.6) | copy-start | bytes 2654212
  14.0 4.4 %collective-permute-start.2 = (bf16[6,64,128]{2,1,0:T(8,128)(2,1)S(1)}, bf16[6,64,128]{2,1,0:T(8,128)(2,1)S(1)}, u32[]{:S(2)}, u32[]{:S(2)}) collective-permute-start(bf16[6,64,128]{2,1,0:T(8,128)(2,1)S(1)} %get-tuple-element.15), channel_id=1, source_target_pairs={{0,1},{1,2},{2,3},{3,4},{4,5},{5,6},{6,7},{7,8},{8,9},{9,10},{10,1... | collective-permute-start | bytes 294920 | tf_op jit(solution)/shard_map/ppermute | solution.py:197
  15.3 6.2 %collective-permute-start.3 = (bf16[6,64,128]{2,1,0:T(8,128)(2,1)S(1)}, bf16[6,64,128]{2,1,0:T(8,128)(2,1)S(1)}, u32[]{:S(2)}, u32[]{:S(2)}) collective-permute-start(bf16[6,64,128]{2,1,0:T(8,128)(2,1)S(1)} %get-tuple-element.14), channel_id=1, source_target_pairs={{1,0},{2,1},{3,2},{4,3},{5,4},{6,5},{7,6},{8,7},{9,8},{10,9},{11,1... | collective-permute-start | bytes 294920 | tf_op jit(solution)/shard_map/ppermute | solution.py:198
  23.0 3.5 %collective-permute-start.4 = (f32[512,128]{1,0:T(8,128)S(1)}, f32[512,128]{1,0:T(8,128)S(1)}, u32[]{:S(2)}, u32[]{:S(2)}) collective-permute-start(f32[512,128]{1,0:T(8,128)S(1)} %get-tuple-element.8.own_ref), channel_id=1, source_target_pairs={{0,32},{32,0},{1,33},{33,1},{2,34},{34,2},{3,35},{35,3},{4,36},{36... | collective-permute-start | bytes 786440 | tf_op jit(solution)/shard_map/ppermute | solution.py:227
  29.0 37.3 %all-to-all-start = ((bf16[16,224,128]{2,1,0:T(8,128)(2,1)}), bf16[16,224,128]{2,1,0:T(8,128)(2,1)S(1)}, u32[]{:S(2)}, u32[]{:S(2)}) async-start(bf16[16,224,128]{2,1,0:T(8,128)(2,1)} %get-tuple-element.11), calls=%async_computation | async-start | bytes 1835008 | tf_op jit(solution)/shard_map/all_to_all | solution.py:234
  51.8 45.3 %copy-start.1 = (bf16[3,3,3,128,128]{4,3,2,1,0:T(8,128)(2,1)S(1)}, bf16[3,3,3,128,128]{4,3,2,1,0:T(8,128)(2,1)}, u32[]{:S(2)}) copy-start(bf16[3,3,3,128,128]{4,3,2,1,0:T(8,128)(2,1)} %param.5) | copy-start | bytes 2654212
  51.8 26.2 %collective-permute-start.5 = (bf16[2,2,64,128]{3,2,0,1:T(8,128)(2,1)S(1)}, bf16[2,2,64,128]{3,2,0,1:T(8,128)(2,1)S(1)}, u32[]{:S(2)}, u32[]{:S(2)}) collective-permute-start(bf16[2,2,64,128]{3,2,0,1:T(8,128)(2,1)S(1)} %get-tuple-element.19), channel_id=1, source_target_pairs={{64,32},{128,96},{192,160},{256,224},{320,288},{384,352},{448,416}... | collective-permute-start | bytes 196616 | tf_op jit(solution)/shard_map/ppermute | solution.py:243
  67.2 22.8 %all-to-all-start.1 = ((f32[16,2,8,128]{3,2,1,0:T(8,128)}), f32[16,2,8,128]{3,2,1,0:T(8,128)S(1)}, u32[]{:S(2)}, u32[]{:S(2)}) async-start(f32[16,2,8,128]{3,2,1,0:T(8,128)} %shard_map.62), calls=%async_computation.1 | async-start | bytes 262144 | tf_op jit(solution)/shard_map/all_to_all | solution.py:236
  78.0 20.6 %collective-permute-start.6 = (bf16[4,64,128]{2,1,0:T(8,128)(2,1)S(1)}, bf16[4,64,128]{2,1,0:T(8,128)(2,1)S(1)}, u32[]{:S(2)}, u32[]{:S(2)}) collective-permute-start(bf16[4,64,128]{2,1,0:T(8,128)(2,1)S(1)} %get-tuple-element.17), channel_id=1, source_target_pairs={{0,1},{1,2},{2,3},{3,4},{4,5},{5,6},{6,7},{7,8},{8,9},{9,10},{10,1... | collective-permute-start | bytes 196616 | tf_op jit(solution)/shard_map/ppermute | solution.py:197
  81.3 17.3 %collective-permute-start.7 = (bf16[4,64,128]{2,1,0:T(8,128)(2,1)S(1)}, bf16[4,64,128]{2,1,0:T(8,128)(2,1)S(1)}, u32[]{:S(2)}, u32[]{:S(2)}) collective-permute-start(bf16[4,64,128]{2,1,0:T(8,128)(2,1)S(1)} %get-tuple-element.16), channel_id=1, source_target_pairs={{1,0},{2,1},{3,2},{4,3},{5,4},{6,5},{7,6},{8,7},{9,8},{10,9},{11,1... | collective-permute-start | bytes 196616 | tf_op jit(solution)/shard_map/ppermute | solution.py:198
  90.0 9.9 %collective-permute-start.8 = (f32[8,128]{1,0:T(8,128)S(1)}, f32[8,128]{1,0:T(8,128)S(1)}, u32[]{:S(2)}, u32[]{:S(2)}) collective-permute-start(f32[8,128]{1,0:T(8,128)S(1)} %get-tuple-element.13), channel_id=1, source_target_pairs={{0,32},{32,0},{1,33},{33,1},{2,34},{34,2},{3,35},{35,3},{4,36},{36... | collective-permute-start | bytes 12296 | tf_op jit(solution)/shard_map/ppermute | solution.py:238
  97.1 1.4 %copy-start = (bf16[2,2,64,128]{3,2,1,0:T(8,128)(2,1)S(1)}, bf16[2,2,64,128]{3,2,1,0:T(8,128)(2,1)}, u32[]{:S(2)}) copy-start(bf16[2,2,64,128]{3,2,1,0:T(8,128)(2,1)} %cot_ref.1) | copy-start | bytes 196612

commit v2 on v1

--- a/solution.py
+++ b/solution.py
@@ -14,17 +14,38 @@
 PARAMS = pltpu.CompilerParams(vmem_limit_bytes=48 * 1024 * 1024)
 
 
+SWAP = [(0, 1), (1, 0)]
+NEAR_ROWS = [(r, r ^ 1) for r in range(32)]
+FAR_GROUPS = [
+    [t * 32 + r for t in (2 * k + 1, (2 * k + 2) % 16) for r in (2 * s + 1, (2 * s + 2) % 32)]
+    for k in range(8)
+    for s in range(16)
+]
+
+
+def place():
+    core = lax.axis_index("c")
+    chip = lax.axis_index("zh") * 4 + lax.axis_index("y")
+    slab = lax.axis_index("x") * 8 + lax.axis_index("zl")
+    odd = slab & 1
+    return core, chip, slab, odd, 2 * (1 - core) + (1 - odd)
+
+
 def contract_first(lhs, rhs):
     return lax.dot_general(lhs, rhs, (((0,), (0,)), ((), ())), preferred_element_type=jnp.float32)
 
 
-def fill_triples(src_ref, up_ref, dn_ref, triples_ref, frames):
+def fill_triples(src_ref, far_ref, near_ref, triples_ref, frames):
+    odd = place()[3]
     columns = src_ref.shape[2]
     chans = src_ref.shape[3]
     col = lax.broadcasted_iota(jnp.int32, (columns, chans), 0)
     for f in range(frames):
         for r in range(4):
-            cells = up_ref[f] if r == 0 else dn_ref[f] if r == 3 else src_ref[f, r - 1]
+            if r in (0, 3):
+                cells = jnp.where(odd == (r == 3), far_ref[f], near_ref[f])
+            else:
+                cells = src_ref[f, r - 1]
             wide = cells.astype(jnp.float32)
             before = jnp.where(col == 0, 0.0, pltpu.roll(wide, 1, 0))
             after = jnp.where(col == columns - 1, 0.0, pltpu.roll(wide, columns - 1, 0))
@@ -64,8 +85,89 @@
     return total
 
 
-def first_conv_kernel(src_ref, up_ref, dn_ref, kernel_ref, out_ref, triples_ref):
-    fill_triples(src_ref, up_ref, dn_ref, triples_ref, 6)
+def pack_kernel(clip_ref, cot_ref, other_ref, send_ref):
+    core, _, _, odd, spot = place()
+
+    def pack(across_ref, first_ref, second_ref):
+        send_ref[spot ^ 2] = across_ref[...].reshape(4, 64, 128)
+        send_ref[spot ^ 1, 0:2] = first_ref[:, odd]
+        send_ref[spot ^ 1, 2:4] = second_ref[:, odd]
+        send_ref[spot ^ 3, 0:2] = across_ref[:, odd]
+
+    @pl.when(core == 0)
+    def _():
+        pack(cot_ref, clip_ref, other_ref)
+
+    @pl.when(core == 1)
+    def _():
+        pack(clip_ref, other_ref, cot_ref)
+
+
+def unpack_kernel(clip_ref, cot_ref, other_ref, got_ref, src_ref, far_ref, inner_ref):
+    core, chip, slab, odd, spot = place()
+
+    @pl.when(core == 0)
+    def _():
+        src_ref[0:2] = got_ref[spot ^ 2].reshape(2, 2, 64, 128)
+        src_ref[2:4] = clip_ref[...]
+        src_ref[4:6] = other_ref[...]
+        far_ref[0:2] = got_ref[spot ^ 3, 0:2]
+        far_ref[2:6] = got_ref[spot ^ 1]
+
+        @pl.when(chip == 0)
+        def _():
+            for f in range(2):
+                src_ref[f] = clip_ref[0]
+                far_ref[f] = got_ref[spot ^ 1, 0]
+
+    @pl.when(core == 1)
+    def _():
+        src_ref[0:2] = other_ref[...]
+        src_ref[2:4] = cot_ref[...]
+        src_ref[4:6] = got_ref[spot ^ 2].reshape(2, 2, 64, 128)
+        far_ref[0:4] = got_ref[spot ^ 1]
+        far_ref[4:6] = got_ref[spot ^ 3, 0:2]
+
+        @pl.when(chip == 7)
+        def _():
+            src_ref[4:6] = jnp.zeros((2, 2, 64, 128), jnp.bfloat16)
+            far_ref[4:6] = jnp.zeros((2, 64, 128), jnp.bfloat16)
+
+    @pl.when((slab == 0) | (slab == 31))
+    def _():
+        far_ref[...] = jnp.zeros(far_ref.shape, jnp.bfloat16)
+
+    inner_ref[...] = src_ref[:, 1 - odd]
+
+
+def unpack_grad_kernel(act_ref, got_ref, src_ref, far_ref, inner_ref):
+    core, chip, slab, odd, spot = place()
+    far_ref[...] = got_ref[spot ^ 1]
+
+    @pl.when(core == 0)
+    def _():
+        src_ref[...] = act_ref[...]
+
+    @pl.when(core == 1)
+    def _():
+        src_ref[0:2] = act_ref[2:4]
+        src_ref[2:4] = got_ref[spot ^ 2].reshape(2, 2, 64, 128)
+        far_ref[2:4] = got_ref[spot ^ 3, 0:2]
+
+        @pl.when(chip == 7)
+        def _():
+            src_ref[2:4] = jnp.zeros((2, 2, 64, 128), jnp.bfloat16)
+            far_ref[2:4] = jnp.zeros((2, 64, 128), jnp.bfloat16)
+
+    @pl.when((slab == 0) | (slab == 31))
+    def _():
+        far_ref[...] = jnp.zeros(far_ref.shape, jnp.bfloat16)
+
+    inner_ref[...] = src_ref[:, 1 - odd]
+
+
+def first_conv_kernel(src_ref, far_ref, near_ref, kernel_ref, out_ref, triples_ref):
+    fill_triples(src_ref, far_ref, near_ref, triples_ref, 6)
     out_ref[...] = conv_all(triples_ref, kernel_ref, 4)
 
     @pl.when((lax.axis_index("c") == 1) & (lax.axis_index("zh") == 0) & (lax.axis_index("y") == 0))
@@ -73,8 +175,8 @@
         out_ref[0:128, :] += fold_all(triples_ref, kernel_ref)
 
 
-def input_conv_kernel(src_ref, up_ref, dn_ref, kernel_ref, cot_ref, out_ref, triples_ref, sum_ref):
-    fill_triples(src_ref, up_ref, dn_ref, triples_ref, 4)
+def input_conv_kernel(src_ref, far_ref, near_ref, kernel_ref, cot_ref, out_ref, triples_ref, sum_ref):
+    fill_triples(src_ref, far_ref, near_ref, triples_ref, 4)
     sum_ref[...] = conv_all(triples_ref, kernel_ref, 2)
 
     @pl.when((lax.axis_index("c") == 0) & (lax.axis_index("zh") == 0) & (lax.axis_index("y") == 0))
@@ -85,8 +187,8 @@
     out_ref[...] = (cot + sum_ref[...]).astype(jnp.bfloat16).reshape(out_ref.shape)
 
 
-def grads_kernel(own_ref, other_ref, triples_ref, send_ref, act_ref, terms_ref):
-    core = lax.axis_index("c")
+def grads_kernel(own_ref, other_ref, triples_ref, send_ref, act_ref, halo_ref, terms_ref):
+    core, _, _, odd, spot = place()
     own, other = own_ref[...], other_ref[...]
     pre_act = jnp.where(core == 0, own, other).astype(jnp.bfloat16).astype(jnp.float32)
     back_grad = jnp.where(core == 0, other, own)
@@ -94,6 +196,10 @@
     act_grad = (back_grad * (sig * (1.0 + pre_act * (1.0 - sig)))).astype(jnp.bfloat16)
     hidden = (pre_act * sig).astype(jnp.bfloat16)
     act_ref[...] = act_grad.reshape(act_ref.shape)
+    halo_ref[spot ^ 2] = act_ref[0:2].reshape(4, 64, 128)
+    halo_ref[spot ^ 3, 0:2] = act_ref[0:2, odd]
+    halo_ref[spot ^ 1, 0:2] = act_ref[pl.ds(2 * core, 2), odd]
+    halo_ref[spot ^ 1, 2:4] = act_ref[2:4, odd]
 
     @pl.when(core == 0)
     def _():
@@ -192,62 +298,59 @@
     return jnp.flip(kernel, (0, 1, 2)).transpose(0, 1, 2, 4, 3)
 
 
-def exchange_rows(source):
-    count = lax.axis_size(ROWS)
-    up = lax.ppermute(source[:, 1], ROWS, [(i, i + 1) for i in range(count - 1)])
-    down = lax.ppermute(source[:, 0], ROWS, [(i + 1, i) for i in range(count - 1)])
-    return up, down
-
-
-SWAP = [(0, 1), (1, 0)]
+def far_exchange(blocks):
+    return lax.all_to_all(blocks, TM + ROWS, 0, 0, axis_index_groups=FAR_GROUPS, tiled=True)
 
 
 def per_device(video_clip, first_kernel, second_kernel, cotangent):
     bf16, f32 = jnp.bfloat16, jnp.float32
     core = lax.axis_index("c")
-    chip = lax.axis_index(("zh", "y"))
-    other_cores = lax.ppermute(jnp.where(core == 0, cotangent, video_clip), "c", SWAP)
-    beyond_pairs = [(2 * k + 1, 2 * k + 2) for k in range(7)] + [(2 * k + 2, 2 * k + 1) for k in range(7)]
-    beyond = lax.ppermute(jnp.where(core == 0, cotangent, video_clip), TM, beyond_pairs)
+    other_frames = lax.ppermute(jnp.where(core == 0, cotangent, video_clip), "c", SWAP)
+    blocks = call(pack_kernel, shaped((4, 4, 64, 128), bf16), video_clip, cotangent, other_frames)
+    got = far_exchange(blocks)
     kernel = jnp.where(core == 0, first_kernel, flipped(second_kernel)).reshape(9, 384, 128)
     first_back = flipped(first_kernel).reshape(9, 384, 128)
-    repeated = jnp.broadcast_to(video_clip[:1], video_clip.shape)
-    beyond = jnp.where((core == 0) & (chip == 0), repeated, beyond)
-    source = jnp.where(
-        core == 0,
-        jnp.concatenate([beyond, video_clip, other_cores], 0),
-        jnp.concatenate([other_cores, cotangent, beyond], 0),
-    )
-    up, down = exchange_rows(source)
+    kernel, first_back = lax.optimization_barrier((kernel, first_back))
+    source, far, inner = call(
+        unpack_kernel,
+        (shaped((6, 2, 64, 128), bf16), shaped((6, 64, 128), bf16), shaped((6, 64, 128), bf16)),
+        video_clip, cotangent, other_frames, got,
+    )
+    near = lax.ppermute(inner, ROWS, NEAR_ROWS)
     own, triples = call(
         first_conv_kernel,
         (shaped((512, 128), f32), shaped((6, 4, 64, 384), bf16)),
-        source, up, down, kernel,
+        source, far, near, kernel,
     )
     other = lax.ppermute(own, "c", SWAP)
-    send, act_grad = call(
+    send, act_grad, blocks = call(
         grads_kernel,
-        (shaped((16, 224, 128), bf16), shaped((4, 2, 64, 128), bf16)),
+        (shaped((16, 224, 128), bf16), shaped((4, 2, 64, 128), bf16), shaped((4, 4, 64, 128), bf16)),
         own, other, triples,
         scratch=[pltpu.VMEM((3456, 128), f32)],
     )
     got = lax.all_to_all(send, ("y", "x"), 0, 0, tiled=True)
+    got_grad = far_exchange(blocks)
     send = call(plane_sum_kernel, shaped((16, 2, 8, 128), f32), got, scratch=[pltpu.VMEM((224, 128), f32)])
     got = lax.all_to_all(send, ("zh", "zl"), 0, 0, tiled=True)
+    source, far, inner = call(
+        unpack_grad_kernel,
+        (shaped((4, 2, 64, 128), bf16), shaped((4, 64, 128), bf16), shaped((4, 64, 128), bf16)),
+        act_grad, got_grad,
+    )
+    near = lax.ppermute(inner, ROWS, NEAR_ROWS)
+    input_grad = call(
+        input_conv_kernel,
+        shaped((2, 2, 64, 128), bf16),
+        source, far, near, first_back, cotangent,
+        scratch=[pltpu.VMEM((4, 4, 64, 384), bf16), pltpu.VMEM((256, 128), f32)],
+    )
+    got, input_grad = lax.optimization_barrier((got, input_grad))
     own_share, send_share = call(line_sum_kernel, (shaped((8, 128), f32),) * 2, got)
     other_share = lax.ppermute(send_share, "c", SWAP)
     scale = 1.0 / math.sqrt(131072)
     weight_grads = call(
         lambda *refs: place_kernel(scale, *refs), shaped((2, 864), f32), own_share, other_share
-    )
-    later = lax.ppermute(act_grad[:2], TM, [(2 * k + 2, 2 * k + 1) for k in range(7)])
-    grad_source = jnp.where(core == 0, act_grad, jnp.concatenate([act_grad[2:], later], 0))
-    up, down = exchange_rows(grad_source)
-    input_grad = call(
-        input_conv_kernel,
-        shaped((2, 2, 64, 128), bf16),
-        grad_source, up, down, first_back, cotangent,
-        scratch=[pltpu.VMEM((4, 4, 64, 384), bf16), pltpu.VMEM((256, 128), f32)],
     )
     return input_grad, weight_grads
 

time: 101 us -> 124 us (1.23)
  blocking collectives: 0 us -> 19.5 us
  starting transfers between devices: 60.9 us -> 70.3 us
  waiting for transfers between devices: 24.8 us -> 17.3 us
    all_to_all x0 -> x1, blocking collectives: none -> 19.5 us  [per_device(): got = lax.all_to_all(send, ('y', 'x'), 0, 0, tiled=True)]
    ppermute x1, starting transfers between devices: 2.4 us -> 13 us  [per_device(): other = lax.ppermute(own, 'c', SWAP)]
    ppermute x6 -> x2, starting transfers between devices: 13.2 us -> 5.16 us  [per_device(): near = lax.ppermute(inner, ROWS, NEAR_ROWS)]
    all_to_all x1 -> x2, waiting for transfers between devices: 13.1 us -> 5.78 us  [far_exchange(): lax.all_to_all(blocks, TM + ROWS, 0, 0, axis_index_groups=FAR_GROUPS, til...]
    ppermute x1, starting transfers between devices: 7.03 us -> 12.8 us  [per_device(): other_share = lax.ppermute(send_share, 'c', SWAP)]
    ppermute x1, starting transfers between devices: 4.86 us -> 8.78 us  [per_device(): lax.ppermute(jnp.where(core == 0, cotangent, video_clip), 'c', SWAP)]
    all_to_all x1, starting transfers between devices: 10.7 us -> 7.34 us  [per_device(): got = lax.all_to_all(send, ('zh', 'zl'), 0, 0, tiled=True)]
    all_to_all x1, waiting for transfers between devices: 7.38 us -> 5.16 us  [per_device(): got = lax.all_to_all(send, ('zh', 'zl'), 0, 0, tiled=True)]
  transfers between devices with their start and end apart: 11 -> 8, of which waited for: 4 -> 8; matrix products, arithmetic and copies ran while one was open for 6% -> 5% of each run, Pallas kernels for 2% -> 2%
where the time goes in v2:
time: 124 us; the launch traced here: 123 us
  starting transfers between devices  70.3 us (57%)
  blocking collectives  19.5 us (16%)
  waiting for transfers between devices  17.3 us (14%)
  Pallas kernels  7.26 us (6%)
  local copies, waits for them, and re-layouts  5.92 us (5%)
  other arithmetic  2.36 us (2%)
    all_to_all x2, starting transfers between devices, far_exchange(): lax.all_to_all(blocks, TM + ROWS, 0, 0, axis_index_groups=FAR_GROUPS, til...  23.3 us
    all_to_all x1, blocking collectives, per_device(): got = lax.all_to_all(send, ('y', 'x'), 0, 0, tiled=True)  19.5 us
    ppermute x1, starting transfers between devices, per_device(): other = lax.ppermute(own, 'c', SWAP)  13 us
    ppermute x1, starting transfers between devices, per_device(): other_share = lax.ppermute(send_share, 'c', SWAP)  12.8 us
    ppermute x1, starting transfers between devices, per_device(): lax.ppermute(jnp.where(core == 0, cotangent, video_clip), 'c', SWAP)  8.78 us
    all_to_all x1, starting transfers between devices, per_device(): got = lax.all_to_all(send, ('zh', 'zl'), 0, 0, tiled=True)  7.34 us
    pallas_call x9, Pallas kernels, call(): pl.pallas_call(kernel, out_shape=out_shape, in_specs=[VMEM] * len(args),...  7.26 us
    all_to_all x2, waiting for transfers between devices, far_exchange(): lax.all_to_all(blocks, TM + ROWS, 0, 0, axis_index_groups=FAR_GROUPS, til...  5.78 us
  transfers between devices with their start and end apart: 8, of which 8 were waited for; matrix products, arithmetic and copies ran while one was open for 5% of the time, Pallas kernels for 2%

profile of v2, /device:TPU:1, one launch (start us, length us, event | category | flops | bytes accessed | tf_op | source)
XLA Modules:
  0.0 123.5 jit_solution(17865301388195244900)
XLA Ops:
  1.5 8.8 %collective-permute-start = (bf16[2,2,64,128]{3,2,1,0:T(8,128)(2,1)S(1)}, bf16[2,2,64,128]{3,2,1,0:T(8,128)(2,1)S(1)}, u32[]{:S(2)}, u32[]{:S(2)}) collective-permute-start(bf16[2,2,64,128]{3,2,1,0:T(8,128)(2,1)S(1)} %broadcast_select_fusion), channel_id=1, source_target_pairs={{0,32},{32,0},{1,33},{33,1},{2,34},{34,2},{3,35},{35,3},{4,36},{36... | collective-permute-start | bytes 196616 | tf_op jit(solution)/shard_map/ppermute | solution.py:308
  10.3 0.9 collective-permute-done.other_ref
  13.6 11.4 %all-to-all-start = ((bf16[4,4,64,128]{3,2,1,0:T(8,128)(2,1)}), bf16[4,4,64,128]{3,2,1,0:T(8,128)(2,1)S(1)}, u32[]{:S(2)}, u32[]{:S(2)}) async-start(bf16[4,4,64,128]{3,2,1,0:T(8,128)(2,1)} %shard_map.59), calls=%async_computation | async-start | bytes 524288 | tf_op jit(solution)/shard_map/all_to_all | solution.py:302
  25.0 1.4 %copy.6 = bf16[3,3,3,128,128]{3,4,2,1,0:T(8,128)(2,1)S(1)} copy(bf16[3,3,3,128,128]{4,3,2,1,0:T(8,128)(2,1)S(1)} %copy-done.4) | data formatting | bytes 1769472 | tf_op args[1]
  26.4 1.5 %bitcast_select_fusion = bf16[3,3,3,128,128]{3,4,2,1,0:T(8,128)(2,1)S(1)} fusion(bf16[3,3,3,128,128]{3,4,2,1,0:T(8,128)(2,1)S(1)} %copy.6, bf16[3,3,3,128,128]{4,3,2,1,0:T(8,128)(2,1)} %param.6, pred[]{:T(512)S(6)} %eq.4), kind=kLoop, calls=%fused_computation | loop fusion | flops 442368 | bytes 2654209 | tf_op jit(solution)/shard_map/jit(_where)/select_n | solution.py:311
  27.9 2.0 %all-to-all-done.got_ref = bf16[4,4,64,128]{3,2,1,0:T(8,128)(2,1)S(1)} async-done(((bf16[4,4,64,128]{3,2,1,0:T(8,128)(2,1)}), bf16[4,4,64,128]{3,2,1,0:T(8,128)(2,1)S(1)}, u32[]{:S(2)}, u32[]{:S(2)}) %all-to-all-start) | async-done | bytes 262176 | tf_op jit(solution)/shard_map/all_to_all | solution.py:302
  29.9 1.9 %collective-permute-start.1 = (bf16[6,64,128]{2,1,0:T(8,128)(2,1)S(1)}, bf16[6,64,128]{2,1,0:T(8,128)(2,1)S(1)}, u32[]{:S(2)}, u32[]{:S(2)}) collective-permute-start(bf16[6,64,128]{2,1,0:T(8,128)(2,1)S(1)} %get-tuple-element.21), channel_id=1, source_target_pairs={{0,1},{1,0},{2,3},{3,2},{4,5},{5,4},{6,7},{7,6},{8,9},{9,8},{10,11... | collective-permute-start | bytes 294920 | tf_op jit(solution)/shard_map/ppermute | solution.py:319
  32.0 1.4 %copy.8 = bf16[3,3,3,128,128]{4,3,2,1,0:T(8,128)(2,1)S(1)} copy(bf16[3,3,3,128,128]{3,4,2,1,0:T(8,128)(2,1)S(1)} %reverse_bitcast_fusion) | data formatting | bytes 1769472 | tf_op jit(solution)/shard_map/transpose | solution.py:298
  33.4 1.4 %copy.7 = bf16[3,3,3,128,128]{4,3,2,1,0:T(8,128)(2,1)S(1)} copy(bf16[3,3,3,128,128]{3,4,2,1,0:T(8,128)(2,1)S(1)} %bitcast_select_fusion) | data formatting | bytes 1769472 | tf_op jit(solution)/shard_map/jit(_where)/select_n | solution.py:311
  34.7 1.3 %collective-permute-done.1.near_ref = bf16[6,64,128]{2,1,0:T(8,128)(2,1)S(1)} collective-permute-done((bf16[6,64,128]{2,1,0:T(8,128)(2,1)S(1)}, bf16[6,64,128]{2,1,0:T(8,128)(2,1)S(1)}, u32[]{:S(2)}, u32[]{:S(2)}) %collective-permute-start.1) | collective-permute-done | bytes 98336 | tf_op jit(solution)/shard_map/ppermute | solution.py:319
  36.1 1.5 %shard_map.61 = (f32[512,128]{1,0:T(8,128)S(1)}, bf16[6,4,64,384]{3,2,1,0:T(8,128)(2,1)S(1)}) custom-call(bf16[6,2,64,128]{3,2,1,0:T(8,128)(2,1)S(1)} %get-tuple-element.19.src_ref, bf16[6,64,128]{2,1,0:T(8,128)(2,1)S(1)} %get-tuple-element.20.far_ref, bf16[6,64,128]{2,1,0:T(8,128)(2,1)S(1)} %collective-permute-done.1.near_ref, bf16[9,384,128]{2,1,0:T(8,128)(2,1)S(1)} %bitcast.7), custom_call_target="tpu_custom_call" | custom-call | tf_op jit(solution)/shard_map/pallas_call | solution.py:283
  37.6 13.0 %collective-permute-start.2 = (f32[512,128]{1,0:T(8,128)S(1)}, f32[512,128]{1,0:T(8,128)S(1)}, u32[]{:S(2)}, u32[]{:S(2)}) collective-permute-start(f32[512,128]{1,0:T(8,128)S(1)} %get-tuple-element.23.own_ref), channel_id=1, source_target_pairs={{0,32},{32,0},{1,33},{33,1},{2,34},{34,2},{3,35},{35,3},{4,36},{36... | collective-permute-start | bytes 786440 | tf_op jit(solution)/shard_map/ppermute | solution.py:325
  50.6 1.1 collective-permute-done.2.other_ref
  51.7 2.2 %shard_map.62 = (bf16[16,224,128]{2,1,0:T(8,128)(2,1)S(1)}, bf16[4,2,64,128]{3,2,1,0:T(8,128)(2,1)S(1)}, bf16[4,4,64,128]{3,2,1,0:T(8,128)(2,1)}) custom-call(f32[512,128]{1,0:T(8,128)S(1)} %get-tuple-element.23.own_ref, f32[512,128]{1,0:T(8,128)S(1)} %collective-permute-done.2.other_ref, bf16[6,4,64,384]{3,2,1,0:T(8,128)(2,1)S(1)} %get-tuple-element.24.triples_ref), custom_call_target="tpu_custom_call" | custom-call | tf_op jit(solution)/shard_map/pallas_call | solution.py:283
  53.9 19.5 %all_to_all.20.got_ref = bf16[16,224,128]{2,1,0:T(8,128)(2,1)S(1)} all-to-all(bf16[16,224,128]{2,1,0:T(8,128)(2,1)S(1)} %get-tuple-element.25), channel_id=1, replica_groups=mesh['zh'=2,'y'=4,'c'=2,'x'=4,'zl'=8] {'y','x'}, dimensions={0} | all-to-all | bytes 1835008 | tf_op jit(solution)/shard_map/all_to_all | solution.py:332
  73.4 11.8 %all-to-all-start.3 = ((bf16[4,4,64,128]{3,2,1,0:T(8,128)(2,1)}), bf16[4,4,64,128]{3,2,1,0:T(8,128)(2,1)S(1)}, u32[]{:S(2)}, u32[]{:S(2)}) async-start(bf16[4,4,64,128]{3,2,1,0:T(8,128)(2,1)} %get-tuple-element.27), calls=%async_computation.3 | async-start | bytes 524288 | tf_op jit(solution)/shard_map/all_to_all | solution.py:302
  85.2 0.9 shard_map.63
  86.1 3.8 %all-to-all-done.3.got_ref = bf16[4,4,64,128]{3,2,1,0:T(8,128)(2,1)S(1)} async-done(((bf16[4,4,64,128]{3,2,1,0:T(8,128)(2,1)}), bf16[4,4,64,128]{3,2,1,0:T(8,128)(2,1)S(1)}, u32[]{:S(2)}, u32[]{:S(2)}) %all-to-all-start.3) | async-done | bytes 262176 | tf_op jit(solution)/shard_map/all_to_all | solution.py:302
  89.9 7.3 %all-to-all-start.2 = ((f32[16,2,8,128]{3,2,1,0:T(8,128)}), f32[16,2,8,128]{3,2,1,0:T(8,128)S(1)}, u32[]{:S(2)}, u32[]{:S(2)}) async-start(f32[16,2,8,128]{3,2,1,0:T(8,128)} %shard_map.63), calls=%async_computation.2 | async-start | bytes 262144 | tf_op jit(solution)/shard_map/all_to_all | solution.py:335
  97.3 3.2 %collective-permute-start.3 = (bf16[4,64,128]{2,1,0:T(8,128)(2,1)S(1)}, bf16[4,64,128]{2,1,0:T(8,128)(2,1)S(1)}, u32[]{:S(2)}, u32[]{:S(2)}) collective-permute-start(bf16[4,64,128]{2,1,0:T(8,128)(2,1)S(1)} %get-tuple-element.30), channel_id=1, source_target_pairs={{0,1},{1,0},{2,3},{3,2},{4,5},{5,4},{6,7},{7,6},{8,9},{9,8},{10,11... | collective-permute-start | bytes 196616 | tf_op jit(solution)/shard_map/ppermute | solution.py:341
  100.6 2.2 %collective-permute-done.3.near_ref = bf16[4,64,128]{2,1,0:T(8,128)(2,1)S(1)} collective-permute-done((bf16[4,64,128]{2,1,0:T(8,128)(2,1)S(1)}, bf16[4,64,128]{2,1,0:T(8,128)(2,1)S(1)}, u32[]{:S(2)}, u32[]{:S(2)}) %collective-permute-start.3) | collective-permute-done | bytes 65568 | tf_op jit(solution)/shard_map/ppermute | solution.py:341
  102.8 1.3 %shard_map.65 = bf16[2,2,64,128]{3,2,1,0:T(8,128)(2,1)} custom-call(bf16[4,2,64,128]{3,2,1,0:T(8,128)(2,1)S(1)} %get-tuple-element.28.src_ref, bf16[4,64,128]{2,1,0:T(8,128)(2,1)S(1)} %get-tuple-element.29.far_ref, bf16[4,64,128]{2,1,0:T(8,128)(2,1)S(1)} %collective-permute-done.3.near_ref, bf16[9,384,128]{2,1,0:T(8,128)(2,1)S(1)} %bitcast.6, ...), custom_call_target="tpu_custom_call" | custom-call | tf_op jit(solution)/shard_map/pallas_call | solution.py:283
  104.1 5.2 %all-to-all-done.2.got_ref = f32[16,2,8,128]{3,2,1,0:T(8,128)S(1)} async-done(((f32[16,2,8,128]{3,2,1,0:T(8,128)}), f32[16,2,8,128]{3,2,1,0:T(8,128)S(1)}, u32[]{:S(2)}, u32[]{:S(2)}) %all-to-all-start.2) | async-done | bytes 131104 | tf_op jit(solution)/shard_map/all_to_all | solution.py:335
  109.3 12.8 %collective-permute-start.4 = (f32[8,128]{1,0:T(8,128)S(1)}, f32[8,128]{1,0:T(8,128)S(1)}, u32[]{:S(2)}, u32[]{:S(2)}) collective-permute-start(f32[8,128]{1,0:T(8,128)S(1)} %get-tuple-element.35), channel_id=1, source_target_pairs={{0,32},{32,0},{1,33},{33,1},{2,34},{34,2},{3,35},{35,3},{4,36},{36... | collective-permute-start | bytes 12296 | tf_op jit(solution)/shard_map/ppermute | solution.py:350
  (18 shorter events, 4.9 us)
Async XLA Ops:
  1.5 9.7 %collective-permute-start = (bf16[2,2,64,128]{3,2,1,0:T(8,128)(2,1)S(1)}, bf16[2,2,64,128]{3,2,1,0:T(8,128)(2,1)S(1)}, u32[]{:S(2)}, u32[]{:S(2)}) collective-permute-start(bf16[2,2,64,128]{3,2,1,0:T(8,128)(2,1)S(1)} %broadcast_select_fusion), channel_id=1, source_target_pairs={{0,32},{32,0},{1,33},{33,1},{2,34},{34,2},{3,35},{35,3},{4,36},{36... | collective-permute-start | bytes 196616 | tf_op jit(solution)/shard_map/ppermute | solution.py:308
  11.2 0.8 copy-start
  12.0 0.8 copy-start.2
  12.9 12.2 %copy-start.4 = (bf16[3,3,3,128,128]{4,3,2,1,0:T(8,128)(2,1)S(1)}, bf16[3,3,3,128,128]{4,3,2,1,0:T(8,128)(2,1)}, u32[]{:S(2)}) copy-start(bf16[3,3,3,128,128]{4,3,2,1,0:T(8,128)(2,1)} %param.5) | copy-start | bytes 2654212
  13.6 16.3 %all-to-all-start = ((bf16[4,4,64,128]{3,2,1,0:T(8,128)(2,1)}), bf16[4,4,64,128]{3,2,1,0:T(8,128)(2,1)S(1)}, u32[]{:S(2)}, u32[]{:S(2)}) async-start(bf16[4,4,64,128]{3,2,1,0:T(8,128)(2,1)} %shard_map.59), calls=%async_computation | async-start | bytes 524288 | tf_op jit(solution)/shard_map/all_to_all | solution.py:302
  26.4 3.5 %copy-start.1 = (bf16[2,2,64,128]{3,2,1,0:T(8,128)(2,1)S(1)}, bf16[2,2,64,128]{3,2,1,0:T(8,128)(2,1)}, u32[]{:S(2)}) copy-start(bf16[2,2,64,128]{3,2,1,0:T(8,128)(2,1)} %cot_ref.5) | copy-start | bytes 196612
  26.4 3.5 %copy-start.3 = (bf16[2,2,64,128]{3,2,1,0:T(8,128)(2,1)S(1)}, bf16[2,2,64,128]{3,2,1,0:T(8,128)(2,1)}, u32[]{:S(2)}) copy-start(bf16[2,2,64,128]{3,2,1,0:T(8,128)(2,1)} %clip_ref.3) | copy-start | bytes 196612
  29.9 6.1 %collective-permute-start.1 = (bf16[6,64,128]{2,1,0:T(8,128)(2,1)S(1)}, bf16[6,64,128]{2,1,0:T(8,128)(2,1)S(1)}, u32[]{:S(2)}, u32[]{:S(2)}) collective-permute-start(bf16[6,64,128]{2,1,0:T(8,128)(2,1)S(1)} %get-tuple-element.21), channel_id=1, source_target_pairs={{0,1},{1,0},{2,3},{3,2},{4,5},{5,4},{6,7},{7,6},{8,9},{9,8},{10,11... | collective-permute-start | bytes 294920 | tf_op jit(solution)/shard_map/ppermute | solution.py:319
  37.6 14.1 %collective-permute-start.2 = (f32[512,128]{1,0:T(8,128)S(1)}, f32[512,128]{1,0:T(8,128)S(1)}, u32[]{:S(2)}, u32[]{:S(2)}) collective-permute-start(f32[512,128]{1,0:T(8,128)S(1)} %get-tuple-element.23.own_ref), channel_id=1, source_target_pairs={{0,32},{32,0},{1,33},{33,1},{2,34},{34,2},{3,35},{35,3},{4,36},{36... | collective-permute-start | bytes 786440 | tf_op jit(solution)/shard_map/ppermute | solution.py:325
  73.4 16.5 %all-to-all-start.3 = ((bf16[4,4,64,128]{3,2,1,0:T(8,128)(2,1)}), bf16[4,4,64,128]{3,2,1,0:T(8,128)(2,1)S(1)}, u32[]{:S(2)}, u32[]{:S(2)}) async-start(bf16[4,4,64,128]{3,2,1,0:T(8,128)(2,1)} %get-tuple-element.27), calls=%async_computation.3 | async-start | bytes 524288 | tf_op jit(solution)/shard_map/all_to_all | solution.py:302
  89.9 19.3 %all-to-all-start.2 = ((f32[16,2,8,128]{3,2,1,0:T(8,128)}), f32[16,2,8,128]{3,2,1,0:T(8,128)S(1)}, u32[]{:S(2)}, u32[]{:S(2)}) async-start(f32[16,2,8,128]{3,2,1,0:T(8,128)} %shard_map.63), calls=%async_computation.2 | async-start | bytes 262144 | tf_op jit(solution)/shard_map/all_to_all | solution.py:335
  97.3 5.5 %collective-permute-start.3 = (bf16[4,64,128]{2,1,0:T(8,128)(2,1)S(1)}, bf16[4,64,128]{2,1,0:T(8,128)(2,1)S(1)}, u32[]{:S(2)}, u32[]{:S(2)}) collective-permute-start(bf16[4,64,128]{2,1,0:T(8,128)(2,1)S(1)} %get-tuple-element.30), channel_id=1, source_target_pairs={{0,1},{1,0},{2,3},{3,2},{4,5},{5,4},{6,7},{7,6},{8,9},{9,8},{10,11... | collective-permute-start | bytes 196616 | tf_op jit(solution)/shard_map/ppermute | solution.py:341
  109.3 13.6 %collective-permute-start.4 = (f32[8,128]{1,0:T(8,128)S(1)}, f32[8,128]{1,0:T(8,128)S(1)}, u32[]{:S(2)}, u32[]{:S(2)}) collective-permute-start(f32[8,128]{1,0:T(8,128)S(1)} %get-tuple-element.35), channel_id=1, source_target_pairs={{0,32},{32,0},{1,33},{33,1},{2,34},{34,2},{3,35},{35,3},{4,36},{36... | collective-permute-start | bytes 12296 | tf_op jit(solution)/shard_map/ppermute | solution.py:350

commit v3 on v2

--- a/solution.py
+++ b/solution.py
@@ -16,10 +16,10 @@
 
 SWAP = [(0, 1), (1, 0)]
 NEAR_ROWS = [(r, r ^ 1) for r in range(32)]
-FAR_GROUPS = [
-    [t * 32 + r for t in (2 * k + 1, (2 * k + 2) % 16) for r in (2 * s + 1, (2 * s + 2) % 32)]
-    for k in range(8)
-    for s in range(16)
+FAR_ROWS = [(r, r + 1) for r in range(1, 31, 2)] + [(r + 1, r) for r in range(1, 31, 2)]
+BEYOND = [(2 * k + 1, 2 * k + 2) for k in range(7)] + [(2 * k + 2, 2 * k + 1) for k in range(7)]
+BEFORE = [((2 * k + 2) * 32 + r, (2 * k + 1) * 32 + r) for k in range(7) for r in range(32)] + [
+    ((2 * k + 3) * 32 + r, 2 * k * 32 + q) for k in range(7) for r, q in FAR_ROWS
 ]
 
 
@@ -28,7 +28,7 @@
     chip = lax.axis_index("zh") * 4 + lax.axis_index("y")
     slab = lax.axis_index("x") * 8 + lax.axis_index("zl")
     odd = slab & 1
-    return core, chip, slab, odd, 2 * (1 - core) + (1 - odd)
+    return core, chip, slab, odd
 
 
 def contract_first(lhs, rhs):
@@ -85,64 +85,33 @@
     return total
 
 
-def pack_kernel(clip_ref, cot_ref, other_ref, send_ref):
-    core, _, _, odd, spot = place()
-
-    def pack(across_ref, first_ref, second_ref):
-        send_ref[spot ^ 2] = across_ref[...].reshape(4, 64, 128)
-        send_ref[spot ^ 1, 0:2] = first_ref[:, odd]
-        send_ref[spot ^ 1, 2:4] = second_ref[:, odd]
-        send_ref[spot ^ 3, 0:2] = across_ref[:, odd]
+def assemble_kernel(clip_ref, cot_ref, other_ref, beyond_ref, src_ref, edge_ref, inner_ref):
+    core, chip, _, odd = place()
 
     @pl.when(core == 0)
     def _():
-        pack(cot_ref, clip_ref, other_ref)
-
-    @pl.when(core == 1)
-    def _():
-        pack(clip_ref, other_ref, cot_ref)
-
-
-def unpack_kernel(clip_ref, cot_ref, other_ref, got_ref, src_ref, far_ref, inner_ref):
-    core, chip, slab, odd, spot = place()
-
-    @pl.when(core == 0)
-    def _():
-        src_ref[0:2] = got_ref[spot ^ 2].reshape(2, 2, 64, 128)
+        src_ref[0:2] = beyond_ref[...]
         src_ref[2:4] = clip_ref[...]
         src_ref[4:6] = other_ref[...]
-        far_ref[0:2] = got_ref[spot ^ 3, 0:2]
-        far_ref[2:6] = got_ref[spot ^ 1]
 
         @pl.when(chip == 0)
         def _():
-            for f in range(2):
-                src_ref[f] = clip_ref[0]
-                far_ref[f] = got_ref[spot ^ 1, 0]
+            src_ref[0] = clip_ref[0]
+            src_ref[1] = clip_ref[0]
 
     @pl.when(core == 1)
     def _():
         src_ref[0:2] = other_ref[...]
         src_ref[2:4] = cot_ref[...]
-        src_ref[4:6] = got_ref[spot ^ 2].reshape(2, 2, 64, 128)
-        far_ref[0:4] = got_ref[spot ^ 1]
-        far_ref[4:6] = got_ref[spot ^ 3, 0:2]
-
-        @pl.when(chip == 7)
-        def _():
-            src_ref[4:6] = jnp.zeros((2, 2, 64, 128), jnp.bfloat16)
-            far_ref[4:6] = jnp.zeros((2, 64, 128), jnp.bfloat16)
-
-    @pl.when((slab == 0) | (slab == 31))
-    def _():
-        far_ref[...] = jnp.zeros(far_ref.shape, jnp.bfloat16)
-
+        src_ref[4:6] = beyond_ref[...]
+
+    edge_ref[...] = src_ref[:, odd]
     inner_ref[...] = src_ref[:, 1 - odd]
 
 
-def unpack_grad_kernel(act_ref, got_ref, src_ref, far_ref, inner_ref):
-    core, chip, slab, odd, spot = place()
-    far_ref[...] = got_ref[spot ^ 1]
+def assemble_grad_kernel(act_ref, before_ref, src_ref, inner_ref, corner_ref):
+    core, _, _, odd = place()
+    corner_ref[...] = before_ref[:, 0]
 
     @pl.when(core == 0)
     def _():
@@ -151,17 +120,7 @@
     @pl.when(core == 1)
     def _():
         src_ref[0:2] = act_ref[2:4]
-        src_ref[2:4] = got_ref[spot ^ 2].reshape(2, 2, 64, 128)
-        far_ref[2:4] = got_ref[spot ^ 3, 0:2]
-
-        @pl.when(chip == 7)
-        def _():
-            src_ref[2:4] = jnp.zeros((2, 2, 64, 128), jnp.bfloat16)
-            far_ref[2:4] = jnp.zeros((2, 64, 128), jnp.bfloat16)
-
-    @pl.when((slab == 0) | (slab == 31))
-    def _():
-        far_ref[...] = jnp.zeros(far_ref.shape, jnp.bfloat16)
+        src_ref[2:4] = before_ref[...]
 
     inner_ref[...] = src_ref[:, 1 - odd]
 
@@ -175,7 +134,15 @@
         out_ref[0:128, :] += fold_all(triples_ref, kernel_ref)
 
 
-def input_conv_kernel(src_ref, far_ref, near_ref, kernel_ref, cot_ref, out_ref, triples_ref, sum_ref):
+def input_conv_kernel(
+    src_ref, edge_ref, corner_ref, near_ref, kernel_ref, cot_ref, out_ref, far_ref, triples_ref, sum_ref
+):
+    far_ref[...] = edge_ref[...]
+
+    @pl.when(lax.axis_index("c") == 1)
+    def _():
+        far_ref[2:4] = corner_ref[...]
+
     fill_triples(src_ref, far_ref, near_ref, triples_ref, 4)
     sum_ref[...] = conv_all(triples_ref, kernel_ref, 2)
 
@@ -187,8 +154,8 @@
     out_ref[...] = (cot + sum_ref[...]).astype(jnp.bfloat16).reshape(out_ref.shape)
 
 
-def grads_kernel(own_ref, other_ref, triples_ref, send_ref, act_ref, halo_ref, terms_ref):
-    core, _, _, odd, spot = place()
+def grads_kernel(own_ref, other_ref, triples_ref, send_ref, act_ref, edge_ref, before_ref, terms_ref):
+    core, _, _, odd = place()
     own, other = own_ref[...], other_ref[...]
     pre_act = jnp.where(core == 0, own, other).astype(jnp.bfloat16).astype(jnp.float32)
     back_grad = jnp.where(core == 0, other, own)
@@ -196,10 +163,17 @@
     act_grad = (back_grad * (sig * (1.0 + pre_act * (1.0 - sig)))).astype(jnp.bfloat16)
     hidden = (pre_act * sig).astype(jnp.bfloat16)
     act_ref[...] = act_grad.reshape(act_ref.shape)
-    halo_ref[spot ^ 2] = act_ref[0:2].reshape(4, 64, 128)
-    halo_ref[spot ^ 3, 0:2] = act_ref[0:2, odd]
-    halo_ref[spot ^ 1, 0:2] = act_ref[pl.ds(2 * core, 2), odd]
-    halo_ref[spot ^ 1, 2:4] = act_ref[2:4, odd]
+    edge_ref[0:2] = act_ref[pl.ds(2 * core, 2), odd]
+    edge_ref[2:4] = act_ref[2:4, odd]
+
+    @pl.when(core == 0)
+    def _():
+        before_ref[...] = act_ref[0:2]
+
+    @pl.when(core == 1)
+    def _():
+        before_ref[:, 0] = act_ref[0:2, odd]
+        before_ref[:, 1] = act_ref[0:2, odd]
 
     @pl.when(core == 0)
     def _():
@@ -256,26 +230,20 @@
                         pltpu.roll(piece, 128 - shift, 1),
                         pltpu.roll(after, 128 - shift, 1),
                     )
-                send_ref[zh * 8 + zl, c] = piece
-
-
-def line_sum_kernel(got_ref, own_ref, send_ref):
-    core = lax.axis_index("c")
-    total = got_ref[0]
-    for k in range(1, 16):
-        total = total + got_ref[k]
-    own_ref[...] = jnp.where(core == 0, total[0], total[1])
-    send_ref[...] = jnp.where(core == 0, total[1], total[0])
-
-
-def place_kernel(scale, own_ref, other_ref, out_ref):
-    core = lax.axis_index("c")
-    own, other = own_ref[...] * scale, other_ref[...] * scale
-    shares = (jnp.where(core == 0, own, other), jnp.where(core == 0, other, own))
+                send_ref[zh * 16 + c * 8 + zl] = piece
+
+
+def line_sum_kernel(scale, got_ref, out_ref):
     for k in range(2):
+        total = None
+        for zh in range(2):
+            for zl in range(8):
+                term = got_ref[zh * 16 + k * 8 + zl]
+                total = term if total is None else total + term
+        total = total * scale
         for r in range(7):
             width = min(128, 864 - 128 * r)
-            out_ref[k : k + 1, 128 * r : 128 * r + width] = shares[k][r : r + 1, :width]
+            out_ref[k : k + 1, 128 * r : 128 * r + width] = total[r : r + 1, :width]
 
 
 def call(kernel, out_shape, *args, scratch=()):
@@ -298,24 +266,21 @@
     return jnp.flip(kernel, (0, 1, 2)).transpose(0, 1, 2, 4, 3)
 
 
-def far_exchange(blocks):
-    return lax.all_to_all(blocks, TM + ROWS, 0, 0, axis_index_groups=FAR_GROUPS, tiled=True)
-
-
 def per_device(video_clip, first_kernel, second_kernel, cotangent):
     bf16, f32 = jnp.bfloat16, jnp.float32
     core = lax.axis_index("c")
-    other_frames = lax.ppermute(jnp.where(core == 0, cotangent, video_clip), "c", SWAP)
-    blocks = call(pack_kernel, shaped((4, 4, 64, 128), bf16), video_clip, cotangent, other_frames)
-    got = far_exchange(blocks)
+    given = jnp.where(core == 0, cotangent, video_clip)
+    beyond = lax.ppermute(given, TM, BEYOND)
+    other_frames = lax.ppermute(given, "c", SWAP)
     kernel = jnp.where(core == 0, first_kernel, flipped(second_kernel)).reshape(9, 384, 128)
     first_back = flipped(first_kernel).reshape(9, 384, 128)
     kernel, first_back = lax.optimization_barrier((kernel, first_back))
-    source, far, inner = call(
-        unpack_kernel,
+    source, edge, inner = call(
+        assemble_kernel,
         (shaped((6, 2, 64, 128), bf16), shaped((6, 64, 128), bf16), shaped((6, 64, 128), bf16)),
-        video_clip, cotangent, other_frames, got,
-    )
+        video_clip, cotangent, other_frames, beyond,
+    )
+    far = lax.ppermute(edge, ROWS, FAR_ROWS)
     near = lax.ppermute(inner, ROWS, NEAR_ROWS)
     own, triples = call(
         first_conv_kernel,
@@ -323,35 +288,38 @@
         source, far, near, kernel,
     )
     other = lax.ppermute(own, "c", SWAP)
-    send, act_grad, blocks = call(
+    send, act_grad, edge, before = call(
         grads_kernel,
-        (shaped((16, 224, 128), bf16), shaped((4, 2, 64, 128), bf16), shaped((4, 4, 64, 128), bf16)),
+        (
+            shaped((16, 224, 128), bf16), shaped((4, 2, 64, 128), bf16),
+            shaped((4, 64, 128), bf16), shaped((2, 2, 64, 128), bf16),
+        ),
         own, other, triples,
         scratch=[pltpu.VMEM((3456, 128), f32)],
     )
     got = lax.all_to_all(send, ("y", "x"), 0, 0, tiled=True)
-    got_grad = far_exchange(blocks)
-    send = call(plane_sum_kernel, shaped((16, 2, 8, 128), f32), got, scratch=[pltpu.VMEM((224, 128), f32)])
-    got = lax.all_to_all(send, ("zh", "zl"), 0, 0, tiled=True)
-    source, far, inner = call(
-        unpack_grad_kernel,
-        (shaped((4, 2, 64, 128), bf16), shaped((4, 64, 128), bf16), shaped((4, 64, 128), bf16)),
-        act_grad, got_grad,
+    before = lax.ppermute(before, TM + ROWS, BEFORE)
+    far = lax.ppermute(edge, ROWS, FAR_ROWS)
+    send = call(plane_sum_kernel, shaped((32, 8, 128), f32), got, scratch=[pltpu.VMEM((224, 128), f32)])
+    got = lax.all_to_all(send, ("zh", "c", "zl"), 0, 0, tiled=True)
+    source, inner, corner = call(
+        assemble_grad_kernel,
+        (shaped((4, 2, 64, 128), bf16), shaped((4, 64, 128), bf16), shaped((2, 64, 128), bf16)),
+        act_grad, before,
     )
     near = lax.ppermute(inner, ROWS, NEAR_ROWS)
+    corner = lax.ppermute(corner, "c", [(0, 1)])
     input_grad = call(
         input_conv_kernel,
         shaped((2, 2, 64, 128), bf16),
-        source, far, near, first_back, cotangent,
-        scratch=[pltpu.VMEM((4, 4, 64, 384), bf16), pltpu.VMEM((256, 128), f32)],
+        source, far, corner, near, first_back, cotangent,
+        scratch=[
+            pltpu.VMEM((4, 64, 128), bf16), pltpu.VMEM((4, 4, 64, 384), bf16), pltpu.VMEM((256, 128), f32)
+        ],
     )
     got, input_grad = lax.optimization_barrier((got, input_grad))
-    own_share, send_share = call(line_sum_kernel, (shaped((8, 128), f32),) * 2, got)
-    other_share = lax.ppermute(send_share, "c", SWAP)
     scale = 1.0 / math.sqrt(131072)
-    weight_grads = call(
-        lambda *refs: place_kernel(scale, *refs), shaped((2, 864), f32), own_share, other_share
-    )
+    weight_grads = call(lambda *refs: line_sum_kernel(scale, *refs), shaped((2, 864), f32), got)
     return input_grad, weight_grads
 
 

time: 124 us -> 103 us (0.83)
  the two profiles are of different devices: /device:TPU:1 before, /device:TPU:25 now
where the time goes in v3:
time: 103 us
  starting transfers between devices  43.4 us (42%)
  blocking collectives  25.6 us (25%)
  waiting for transfers between devices  20.4 us (20%)
  Pallas kernels  5.15 us (5%)
  local copies, waits for them, and re-layouts  4.87 us (5%)
  other arithmetic  2.41 us (2%)
    all_to_all x1, blocking collectives, per_device(): got = lax.all_to_all(send, ('y', 'x'), 0, 0, tiled=True)  25.6 us
    ppermute x1, waiting for transfers between devices, per_device(): before = lax.ppermute(before, TM + ROWS, BEFORE)  17.4 us
    ppermute x1, starting transfers between devices, per_device(): beyond = lax.ppermute(given, TM, BEYOND)  15.7 us
    ppermute x2, starting transfers between devices, per_device(): near = lax.ppermute(inner, ROWS, NEAR_ROWS)  10.2 us
    all_to_all x1, starting transfers between devices, per_device(): got = lax.all_to_all(send, ('zh', 'c', 'zl'), 0, 0, tiled=True)  8.74 us
    pallas_call x7, Pallas kernels, call(): pl.pallas_call(kernel, out_shape=out_shape, in_specs=[VMEM] * len(args),...  5.15 us
    ppermute x1, starting transfers between devices, per_device(): other = lax.ppermute(own, 'c', SWAP)  2.97 us
  transfers between devices with their start and end apart: 10, of which 3 were waited for; matrix products, arithmetic and copies ran while one was open for 6% of the time, Pallas kernels for 1%

profile of v3, /device:TPU:25, one launch (start us, length us, event | category | flops | bytes accessed | tf_op | source)
XLA Modules:
  0.0 102.7 jit_solution(4759770154961782440)
XLA Ops:
  0.6 0.9 broadcast_select_fusion
  1.5 15.7 %collective-permute-start.1 = (bf16[2,2,64,128]{3,2,1,0:T(8,128)(2,1)S(1)}, bf16[2,2,64,128]{3,2,1,0:T(8,128)(2,1)S(1)}, u32[]{:S(2)}, u32[]{:S(2)}) collective-permute-start(bf16[2,2,64,128]{3,2,1,0:T(8,128)(2,1)S(1)} %broadcast_select_fusion), channel_id=1, source_target_pairs={{32,64},{96,128},{160,192},{224,256},{288,320},{352,384},{416,448}... | collective-permute-start | bytes 196616 | tf_op jit(solution)/shard_map/ppermute | solution.py:273
  17.2 1.9 %collective-permute-start = (bf16[2,2,64,128]{3,2,1,0:T(8,128)(2,1)S(1)}, bf16[2,2,64,128]{3,2,1,0:T(8,128)(2,1)S(1)}, u32[]{:S(2)}, u32[]{:S(2)}) collective-permute-start(bf16[2,2,64,128]{3,2,1,0:T(8,128)(2,1)S(1)} %broadcast_select_fusion), channel_id=1, source_target_pairs={{0,32},{32,0},{1,33},{33,1},{2,34},{34,2},{3,35},{35,3},{4,36},{36... | collective-permute-start | bytes 196616 | tf_op jit(solution)/shard_map/ppermute | solution.py:274
  19.1 2.0 %copy.6 = bf16[3,3,3,128,128]{3,4,2,1,0:T(8,128)(2,1)S(1)} copy(bf16[3,3,3,128,128]{4,3,2,1,0:T(8,128)(2,1)} %param.5) | data formatting | bytes 1769472 | tf_op args[1]
  21.1 1.5 %bitcast_select_fusion = bf16[3,3,3,128,128]{3,4,2,1,0:T(8,128)(2,1)S(1)} fusion(bf16[3,3,3,128,128]{3,4,2,1,0:T(8,128)(2,1)S(1)} %copy.6, bf16[3,3,3,128,128]{4,3,2,1,0:T(8,128)(2,1)} %param.6, pred[]{:T(512)S(6)} %eq.4), kind=kLoop, calls=%fused_computation | loop fusion | flops 442368 | bytes 2654209 | tf_op jit(solution)/shard_map/jit(_where)/select_n | solution.py:275
  22.8 0.7 collective-permute-start.2
  23.5 4.6 %collective-permute-start.3 = (bf16[6,64,128]{2,1,0:T(8,128)(2,1)S(1)}, bf16[6,64,128]{2,1,0:T(8,128)(2,1)S(1)}, u32[]{:S(2)}, u32[]{:S(2)}) collective-permute-start(bf16[6,64,128]{2,1,0:T(8,128)(2,1)S(1)} %get-tuple-element.20), channel_id=1, source_target_pairs={{0,1},{1,0},{2,3},{3,2},{4,5},{5,4},{6,7},{7,6},{8,9},{9,8},{10,11... | collective-permute-start | bytes 294920 | tf_op jit(solution)/shard_map/ppermute | solution.py:284
  28.2 1.4 %copy.8 = bf16[3,3,3,128,128]{4,3,2,1,0:T(8,128)(2,1)S(1)} copy(bf16[3,3,3,128,128]{3,4,2,1,0:T(8,128)(2,1)S(1)} %reverse_bitcast_fusion) | data formatting | bytes 1769472 | tf_op jit(solution)/shard_map/transpose | solution.py:266
  29.6 1.4 %copy.7 = bf16[3,3,3,128,128]{4,3,2,1,0:T(8,128)(2,1)S(1)} copy(bf16[3,3,3,128,128]{3,4,2,1,0:T(8,128)(2,1)S(1)} %bitcast_select_fusion) | data formatting | bytes 1769472 | tf_op jit(solution)/shard_map/jit(_where)/select_n | solution.py:275
  31.0 1.1 %shard_map.60 = (f32[512,128]{1,0:T(8,128)S(1)}, bf16[6,4,64,384]{3,2,1,0:T(8,128)(2,1)S(1)}) custom-call(bf16[6,2,64,128]{3,2,1,0:T(8,128)(2,1)S(1)} %get-tuple-element.18.src_ref, bf16[6,64,128]{2,1,0:T(8,128)(2,1)S(1)} %collective-permute-done.2.far_ref, bf16[6,64,128]{2,1,0:T(8,128)(2,1)S(1)} %collective-permute-done.3.near_ref, ...), custom_call_target="tpu_custom_call" | custom-call | tf_op jit(solution)/shard_map/pallas_call | solution.py:251
  32.1 3.0 %collective-permute-start.4 = (f32[512,128]{1,0:T(8,128)S(1)}, f32[512,128]{1,0:T(8,128)S(1)}, u32[]{:S(2)}, u32[]{:S(2)}) collective-permute-start(f32[512,128]{1,0:T(8,128)S(1)} %get-tuple-element.22.own_ref), channel_id=1, source_target_pairs={{0,32},{32,0},{1,33},{33,1},{2,34},{34,2},{3,35},{35,3},{4,36},{36... | collective-permute-start | bytes 786440 | tf_op jit(solution)/shard_map/ppermute | solution.py:290
  35.1 1.1 %collective-permute-done.4.other_ref = f32[512,128]{1,0:T(8,128)S(1)} collective-permute-done((f32[512,128]{1,0:T(8,128)S(1)}, f32[512,128]{1,0:T(8,128)S(1)}, u32[]{:S(2)}, u32[]{:S(2)}) %collective-permute-start.4) | collective-permute-done | bytes 262176 | tf_op jit(solution)/shard_map/ppermute | solution.py:290
  36.2 1.2 %shard_map.61 = (bf16[16,224,128]{2,1,0:T(8,128)(2,1)S(1)}, bf16[4,2,64,128]{3,2,1,0:T(8,128)(2,1)S(1)}, bf16[4,64,128]{2,1,0:T(8,128)(2,1)S(1)}, bf16[2,2,64,128]{3,2,1,0:T(8,128)(2,1)S(1)}) custom-call(f32[512,128]{1,0:T(8,128)S(1)} %get-tuple-element.22.own_ref, f32[512,128]{1,0:T(8,128)S(1)} %collective-permute-done.4.other_ref, ...), custom_call_target="tpu_custom_call" | custom-call | tf_op jit(solution)/shard_map/pallas_call | solution.py:251
  37.4 25.6 %all_to_all.10.got_ref = bf16[16,224,128]{2,1,0:T(8,128)(2,1)S(1)} all-to-all(bf16[16,224,128]{2,1,0:T(8,128)(2,1)S(1)} %get-tuple-element.24), channel_id=1, replica_groups=mesh['zh'=2,'y'=4,'c'=2,'x'=4,'zl'=8] {'y','x'}, dimensions={0} | all-to-all | bytes 1835008 | tf_op jit(solution)/shard_map/all_to_all | solution.py:300
  63.0 0.9 shard_map.62
  63.9 8.7 %all-to-all-start.1 = ((f32[32,8,128]{2,1,0:T(8,128)}), f32[32,8,128]{2,1,0:T(8,128)S(1)}, u32[]{:S(2)}, u32[]{:S(2)}) async-start(f32[32,8,128]{2,1,0:T(8,128)} %shard_map.62), calls=%async_computation.1 | async-start | bytes 262144 | tf_op jit(solution)/shard_map/all_to_all | solution.py:304
  72.6 1.3 %collective-permute-start.5 = (bf16[2,2,64,128]{3,2,1,0:T(8,128)(2,1)S(1)}, bf16[2,2,64,128]{3,2,1,0:T(8,128)(2,1)S(1)}, u32[]{:S(2)}, u32[]{:S(2)}) collective-permute-start(bf16[2,2,64,128]{3,2,1,0:T(8,128)(2,1)S(1)} %get-tuple-element.26), channel_id=1, source_target_pairs={{64,32},{65,33},{66,34},{67,35},{68,36},{69,37},{70,38},{71,39},{7... | collective-permute-start | bytes 196616 | tf_op jit(solution)/shard_map/ppermute | solution.py:301
  73.9 0.7 collective-permute-start.6
  74.6 17.4 %collective-permute-done.5.before_ref = bf16[2,2,64,128]{3,2,1,0:T(8,128)(2,1)S(1)} collective-permute-done((bf16[2,2,64,128]{3,2,1,0:T(8,128)(2,1)S(1)}, bf16[2,2,64,128]{3,2,1,0:T(8,128)(2,1)S(1)}, u32[]{:S(2)}, u32[]{:S(2)}) %collective-permute-start.5) | collective-permute-done | bytes 65568 | tf_op jit(solution)/shard_map/ppermute | solution.py:301
  92.1 5.6 %collective-permute-start.8 = (bf16[4,64,128]{2,1,0:T(8,128)(2,1)S(1)}, bf16[4,64,128]{2,1,0:T(8,128)(2,1)S(1)}, u32[]{:S(2)}, u32[]{:S(2)}) collective-permute-start(bf16[4,64,128]{2,1,0:T(8,128)(2,1)S(1)} %get-tuple-element.30), channel_id=1, source_target_pairs={{0,1},{1,0},{2,3},{3,2},{4,5},{5,4},{6,7},{7,6},{8,9},{9,8},{10,11... | collective-permute-start | bytes 196616 | tf_op jit(solution)/shard_map/ppermute | solution.py:310
  97.7 1.3 %collective-permute-start.7 = (bf16[2,64,128]{2,1,0:T(8,128)(2,1)S(1)}, bf16[2,64,128]{2,1,0:T(8,128)(2,1)S(1)}, u32[]{:S(2)}, u32[]{:S(2)}) collective-permute-start(bf16[2,64,128]{2,1,0:T(8,128)(2,1)S(1)} %get-tuple-element.29), channel_id=1, source_target_pairs={{0,32},{1,33},{2,34},{3,35},{4,36},{5,37},{6,38},{7,39},{8,40},{9,... | collective-permute-start | bytes 98312 | tf_op jit(solution)/shard_map/ppermute | solution.py:311
  99.0 1.8 %collective-permute-done.7.corner_ref = bf16[2,64,128]{2,1,0:T(8,128)(2,1)S(1)} collective-permute-done((bf16[2,64,128]{2,1,0:T(8,128)(2,1)S(1)}, bf16[2,64,128]{2,1,0:T(8,128)(2,1)S(1)}, u32[]{:S(2)}, u32[]{:S(2)}) %collective-permute-start.7) | collective-permute-done | bytes 32800 | tf_op jit(solution)/shard_map/ppermute | solution.py:311
  100.8 1.3 %shard_map.64 = bf16[2,2,64,128]{3,2,1,0:T(8,128)(2,1)} custom-call(bf16[4,2,64,128]{3,2,1,0:T(8,128)(2,1)S(1)} %get-tuple-element.27.src_ref, bf16[4,64,128]{2,1,0:T(8,128)(2,1)S(1)} %collective-permute-done.6.edge_ref, bf16[2,64,128]{2,1,0:T(8,128)(2,1)S(1)} %collective-permute-done.7.corner_ref, bf16[4,64,128]{2,1,0:T(8,128)(2,1)S(1)} %collective-permute-done.8.near_ref, ...), custom_call_target="tpu_custom_call" | custom-call | tf_op jit(solution)/shard_map/pallas_call | solution.py:251
  102.1 0.6 shard_map.65
  (16 shorter events, 0.2 us)
Async XLA Ops:
  1.5 21.2 %collective-permute-start.1 = (bf16[2,2,64,128]{3,2,1,0:T(8,128)(2,1)S(1)}, bf16[2,2,64,128]{3,2,1,0:T(8,128)(2,1)S(1)}, u32[]{:S(2)}, u32[]{:S(2)}) collective-permute-start(bf16[2,2,64,128]{3,2,1,0:T(8,128)(2,1)S(1)} %broadcast_select_fusion), channel_id=1, source_target_pairs={{32,64},{96,128},{160,192},{224,256},{288,320},{352,384},{416,448}... | collective-permute-start | bytes 196616 | tf_op jit(solution)/shard_map/ppermute | solution.py:273
  17.2 5.5 %collective-permute-start = (bf16[2,2,64,128]{3,2,1,0:T(8,128)(2,1)S(1)}, bf16[2,2,64,128]{3,2,1,0:T(8,128)(2,1)S(1)}, u32[]{:S(2)}, u32[]{:S(2)}) collective-permute-start(bf16[2,2,64,128]{3,2,1,0:T(8,128)(2,1)S(1)} %broadcast_select_fusion), channel_id=1, source_target_pairs={{0,32},{32,0},{1,33},{33,1},{2,34},{34,2},{3,35},{35,3},{4,36},{36... | collective-permute-start | bytes 196616 | tf_op jit(solution)/shard_map/ppermute | solution.py:274
  21.1 1.6 %copy-start = (bf16[2,2,64,128]{3,2,1,0:T(8,128)(2,1)S(1)}, bf16[2,2,64,128]{3,2,1,0:T(8,128)(2,1)}, u32[]{:S(2)}) copy-start(bf16[2,2,64,128]{3,2,1,0:T(8,128)(2,1)} %cot_ref.3) | copy-start | bytes 196612
  21.1 1.6 %copy-start.1 = (bf16[2,2,64,128]{3,2,1,0:T(8,128)(2,1)S(1)}, bf16[2,2,64,128]{3,2,1,0:T(8,128)(2,1)}, u32[]{:S(2)}) copy-start(bf16[2,2,64,128]{3,2,1,0:T(8,128)(2,1)} %clip_ref.1) | copy-start | bytes 196612
  21.1 7.0 %copy-start.2 = (bf16[3,3,3,128,128]{4,3,2,1,0:T(8,128)(2,1)S(1)}, bf16[3,3,3,128,128]{4,3,2,1,0:T(8,128)(2,1)}, u32[]{:S(2)}) copy-start(bf16[3,3,3,128,128]{4,3,2,1,0:T(8,128)(2,1)} %param.5) | copy-start | bytes 2654212
  22.8 8.2 %collective-permute-start.2 = (bf16[6,64,128]{2,1,0:T(8,128)(2,1)S(1)}, bf16[6,64,128]{2,1,0:T(8,128)(2,1)S(1)}, u32[]{:S(2)}, u32[]{:S(2)}) collective-permute-start(bf16[6,64,128]{2,1,0:T(8,128)(2,1)S(1)} %get-tuple-element.19), channel_id=1, source_target_pairs={{1,2},{3,4},{5,6},{7,8},{9,10},{11,12},{13,14},{15,16},{17,18},{19... | collective-permute-start | bytes 294920 | tf_op jit(solution)/shard_map/ppermute | solution.py:283
  23.5 7.5 %collective-permute-start.3 = (bf16[6,64,128]{2,1,0:T(8,128)(2,1)S(1)}, bf16[6,64,128]{2,1,0:T(8,128)(2,1)S(1)}, u32[]{:S(2)}, u32[]{:S(2)}) collective-permute-start(bf16[6,64,128]{2,1,0:T(8,128)(2,1)S(1)} %get-tuple-element.20), channel_id=1, source_target_pairs={{0,1},{1,0},{2,3},{3,2},{4,5},{5,4},{6,7},{7,6},{8,9},{9,8},{10,11... | collective-permute-start | bytes 294920 | tf_op jit(solution)/shard_map/ppermute | solution.py:284
  32.1 4.1 %collective-permute-start.4 = (f32[512,128]{1,0:T(8,128)S(1)}, f32[512,128]{1,0:T(8,128)S(1)}, u32[]{:S(2)}, u32[]{:S(2)}) collective-permute-start(f32[512,128]{1,0:T(8,128)S(1)} %get-tuple-element.22.own_ref), channel_id=1, source_target_pairs={{0,32},{32,0},{1,33},{33,1},{2,34},{34,2},{3,35},{35,3},{4,36},{36... | collective-permute-start | bytes 786440 | tf_op jit(solution)/shard_map/ppermute | solution.py:290
  63.9 38.2 %all-to-all-start.1 = ((f32[32,8,128]{2,1,0:T(8,128)}), f32[32,8,128]{2,1,0:T(8,128)S(1)}, u32[]{:S(2)}, u32[]{:S(2)}) async-start(f32[32,8,128]{2,1,0:T(8,128)} %shard_map.62), calls=%async_computation.1 | async-start | bytes 262144 | tf_op jit(solution)/shard_map/all_to_all | solution.py:304
  72.6 19.4 %collective-permute-start.5 = (bf16[2,2,64,128]{3,2,1,0:T(8,128)(2,1)S(1)}, bf16[2,2,64,128]{3,2,1,0:T(8,128)(2,1)S(1)}, u32[]{:S(2)}, u32[]{:S(2)}) collective-permute-start(bf16[2,2,64,128]{3,2,1,0:T(8,128)(2,1)S(1)} %get-tuple-element.26), channel_id=1, source_target_pairs={{64,32},{65,33},{66,34},{67,35},{68,36},{69,37},{70,38},{71,39},{7... | collective-permute-start | bytes 196616 | tf_op jit(solution)/shard_map/ppermute | solution.py:301
  73.9 25.0 %collective-permute-start.6 = (bf16[4,64,128]{2,1,0:T(8,128)(2,1)S(1)}, bf16[4,64,128]{2,1,0:T(8,128)(2,1)S(1)}, u32[]{:S(2)}, u32[]{:S(2)}) collective-permute-start(bf16[4,64,128]{2,1,0:T(8,128)(2,1)S(1)} %get-tuple-element.28), channel_id=1, source_target_pairs={{1,2},{3,4},{5,6},{7,8},{9,10},{11,12},{13,14},{15,16},{17,18},{19... | collective-permute-start | bytes 196616 | tf_op jit(solution)/shard_map/ppermute | solution.py:302
  92.1 8.7 %collective-permute-start.8 = (bf16[4,64,128]{2,1,0:T(8,128)(2,1)S(1)}, bf16[4,64,128]{2,1,0:T(8,128)(2,1)S(1)}, u32[]{:S(2)}, u32[]{:S(2)}) collective-permute-start(bf16[4,64,128]{2,1,0:T(8,128)(2,1)S(1)} %get-tuple-element.30), channel_id=1, source_target_pairs={{0,1},{1,0},{2,3},{3,2},{4,5},{5,4},{6,7},{7,6},{8,9},{9,8},{10,11... | collective-permute-start | bytes 196616 | tf_op jit(solution)/shard_map/ppermute | solution.py:310
  97.7 3.1 %collective-permute-start.7 = (bf16[2,64,128]{2,1,0:T(8,128)(2,1)S(1)}, bf16[2,64,128]{2,1,0:T(8,128)(2,1)S(1)}, u32[]{:S(2)}, u32[]{:S(2)}) collective-permute-start(bf16[2,64,128]{2,1,0:T(8,128)(2,1)S(1)} %get-tuple-element.29), channel_id=1, source_target_pairs={{0,32},{1,33},{2,34},{3,35},{4,36},{5,37},{6,38},{7,39},{8,40},{9,... | collective-permute-start | bytes 98312 | tf_op jit(solution)/shard_map/ppermute | solution.py:311

commit v4 on v3

--- a/solution.py
+++ b/solution.py
@@ -218,8 +218,9 @@
     sum_ref[...] = total
     lane = lax.broadcasted_iota(jnp.int32, (8, 128), 1)
     for zh in range(2):
-        for c in range(2):
-            for zl in range(8):
+        for zl in range(8):
+            pieces = []
+            for c in range(2):
                 value = (zh * 2 + c) * 54 * 128 + zl * 864
                 row, shift = value // 128, value % 128
                 piece = sum_ref[row : row + 8, :]
@@ -230,23 +231,30 @@
                         pltpu.roll(piece, 128 - shift, 1),
                         pltpu.roll(after, 128 - shift, 1),
                     )
-                send_ref[zh * 16 + c * 8 + zl] = piece
-
-
-def line_sum_kernel(scale, got_ref, out_ref):
+                pieces.append(piece)
+            send_ref[zh * 8 + zl] = jnp.concatenate(pieces, axis=0).astype(jnp.bfloat16)
+
+
+def line_sum_kernel(got_ref, own_ref, send_ref):
+    core = lax.axis_index("c")
+    total = got_ref[0].astype(jnp.float32)
+    for k in range(1, 16):
+        total = total + got_ref[k].astype(jnp.float32)
+    own_ref[...] = jnp.where(core == 0, total[0:8], total[8:16])
+    send_ref[...] = jnp.where(core == 0, total[8:16], total[0:8])
+
+
+def place_kernel(scale, own_ref, other_ref, out_ref):
+    core = lax.axis_index("c")
+    own, other = own_ref[...] * scale, other_ref[...] * scale
+    shares = (jnp.where(core == 0, own, other), jnp.where(core == 0, other, own))
     for k in range(2):
-        total = None
-        for zh in range(2):
-            for zl in range(8):
-                term = got_ref[zh * 16 + k * 8 + zl]
-                total = term if total is None else total + term
-        total = total * scale
         for r in range(7):
             width = min(128, 864 - 128 * r)
-            out_ref[k : k + 1, 128 * r : 128 * r + width] = total[r : r + 1, :width]
-
-
-def call(kernel, out_shape, *args, scratch=()):
+            out_ref[k : k + 1, 128 * r : 128 * r + width] = shares[k][r : r + 1, :width]
+
+
+def call(kernel, out_shape, *args, scratch=(), flops=0):
     many = isinstance(out_shape, (list, tuple))
     return pl.pallas_call(
         kernel,
@@ -255,6 +263,7 @@
         out_specs=[VMEM] * len(out_shape) if many else VMEM,
         scratch_shapes=scratch,
         compiler_params=PARAMS,
+        cost_estimate=pl.CostEstimate(flops=flops, bytes_accessed=0, transcendentals=0) if flops else None,
     )(*args)
 
 
@@ -300,8 +309,10 @@
     got = lax.all_to_all(send, ("y", "x"), 0, 0, tiled=True)
     before = lax.ppermute(before, TM + ROWS, BEFORE)
     far = lax.ppermute(edge, ROWS, FAR_ROWS)
-    send = call(plane_sum_kernel, shaped((32, 8, 128), f32), got, scratch=[pltpu.VMEM((224, 128), f32)])
-    got = lax.all_to_all(send, ("zh", "c", "zl"), 0, 0, tiled=True)
+    got, before = lax.optimization_barrier((got, before))
+    send = call(plane_sum_kernel, shaped((16, 16, 128), bf16), got, scratch=[pltpu.VMEM((224, 128), f32)])
+    got = lax.all_to_all(send, ("zh", "zl"), 0, 0, tiled=True)
+    _, before, far = lax.optimization_barrier((send, before, far))
     source, inner, corner = call(
         assemble_grad_kernel,
         (shaped((4, 2, 64, 128), bf16), shaped((4, 64, 128), bf16), shaped((2, 64, 128), bf16)),
@@ -316,10 +327,15 @@
         scratch=[
             pltpu.VMEM((4, 64, 128), bf16), pltpu.VMEM((4, 4, 64, 384), bf16), pltpu.VMEM((256, 128), f32)
         ],
+        flops=1_600_000_000,
     )
     got, input_grad = lax.optimization_barrier((got, input_grad))
     scale = 1.0 / math.sqrt(131072)
-    weight_grads = call(lambda *refs: line_sum_kernel(scale, *refs), shaped((2, 864), f32), got)
+    own_share, send_share = call(line_sum_kernel, (shaped((8, 128), f32),) * 2, got)
+    other_share = lax.ppermute(send_share, "c", SWAP)
+    weight_grads = call(
+        lambda *refs: place_kernel(scale, *refs), shaped((2, 864), f32), own_share, other_share
+    )
     return input_grad, weight_grads
 
 

time: 103 us -> 93.8 us (0.911)
  the two profiles are of different devices: /device:TPU:25 before, /device:TPU:1 now
where the time goes in v4:
time: 93.8 us; the launch traced here: 93.2 us
  starting transfers between devices  56.7 us (60%)
  waiting for transfers between devices  21.6 us (23%)
  Pallas kernels  6.89 us (7%)
  local copies, waits for them, and re-layouts  4.85 us (5%)
  other arithmetic  2.41 us (3%)
    all_to_all x1, starting transfers between devices, per_device(): got = lax.all_to_all(send, ('y', 'x'), 0, 0, tiled=True)  21.7 us
    ppermute x1, waiting for transfers between devices, per_device(): before = lax.ppermute(before, TM + ROWS, BEFORE)  8.07 us
    pallas_call x8, Pallas kernels, call(): pl.pallas_call(kernel, out_shape=out_shape, in_specs=[VMEM] * len(args),...  6.89 us
    ppermute x2, starting transfers between devices, per_device(): near = lax.ppermute(inner, ROWS, NEAR_ROWS)  6.76 us
    all_to_all x1, starting transfers between devices, per_device(): got = lax.all_to_all(send, ('zh', 'zl'), 0, 0, tiled=True)  6.59 us
    ppermute x1, starting transfers between devices, per_device(): other_share = lax.ppermute(send_share, 'c', SWAP)  5.85 us
    ppermute x1, starting transfers between devices, per_device(): other_frames = lax.ppermute(given, 'c', SWAP)  4.86 us
    all_to_all x1, waiting for transfers between devices, per_device(): got = lax.all_to_all(send, ('y', 'x'), 0, 0, tiled=True)  4.81 us
  transfers between devices with their start and end apart: 12, of which 7 were waited for; matrix products, arithmetic and copies ran while one was open for 7% of the time, Pallas kernels for 2%

profile of v4, /device:TPU:1, one launch (start us, length us, event | category | flops | bytes accessed | tf_op | source)
XLA Modules:
  0.0 93.2 jit_solution(10213591686396551187)
XLA Ops:
  0.6 0.9 broadcast_select_fusion
  1.5 4.6 %collective-permute-start.1 = (bf16[2,2,64,128]{3,2,1,0:T(8,128)(2,1)S(1)}, bf16[2,2,64,128]{3,2,1,0:T(8,128)(2,1)S(1)}, u32[]{:S(2)}, u32[]{:S(2)}) collective-permute-start(bf16[2,2,64,128]{3,2,1,0:T(8,128)(2,1)S(1)} %broadcast_select_fusion), channel_id=1, source_target_pairs={{32,64},{96,128},{160,192},{224,256},{288,320},{352,384},{416,448}... | collective-permute-start | bytes 196616 | tf_op jit(solution)/shard_map/ppermute | solution.py:282
  6.1 4.9 %collective-permute-start = (bf16[2,2,64,128]{3,2,1,0:T(8,128)(2,1)S(1)}, bf16[2,2,64,128]{3,2,1,0:T(8,128)(2,1)S(1)}, u32[]{:S(2)}, u32[]{:S(2)}) collective-permute-start(bf16[2,2,64,128]{3,2,1,0:T(8,128)(2,1)S(1)} %broadcast_select_fusion), channel_id=1, source_target_pairs={{0,32},{32,0},{1,33},{33,1},{2,34},{34,2},{3,35},{35,3},{4,36},{36... | collective-permute-start | bytes 196616 | tf_op jit(solution)/shard_map/ppermute | solution.py:283
  11.0 2.0 %copy.6 = bf16[3,3,3,128,128]{3,4,2,1,0:T(8,128)(2,1)S(1)} copy(bf16[3,3,3,128,128]{4,3,2,1,0:T(8,128)(2,1)} %param.5) | data formatting | bytes 1769472 | tf_op args[1]
  13.0 1.5 %bitcast_select_fusion = bf16[3,3,3,128,128]{3,4,2,1,0:T(8,128)(2,1)S(1)} fusion(bf16[3,3,3,128,128]{3,4,2,1,0:T(8,128)(2,1)S(1)} %copy.6, bf16[3,3,3,128,128]{4,3,2,1,0:T(8,128)(2,1)} %param.6, pred[]{:T(512)S(6)} %eq.4), kind=kLoop, calls=%fused_computation | loop fusion | flops 442368 | bytes 2654209 | tf_op jit(solution)/shard_map/jit(_where)/select_n | solution.py:284
  15.3 3.5 %collective-permute-start.3 = (bf16[6,64,128]{2,1,0:T(8,128)(2,1)S(1)}, bf16[6,64,128]{2,1,0:T(8,128)(2,1)S(1)}, u32[]{:S(2)}, u32[]{:S(2)}) collective-permute-start(bf16[6,64,128]{2,1,0:T(8,128)(2,1)S(1)} %get-tuple-element.26), channel_id=1, source_target_pairs={{0,1},{1,0},{2,3},{3,2},{4,5},{5,4},{6,7},{7,6},{8,9},{9,8},{10,11... | collective-permute-start | bytes 294920 | tf_op jit(solution)/shard_map/ppermute | solution.py:293
  18.9 1.4 %copy.8 = bf16[3,3,3,128,128]{4,3,2,1,0:T(8,128)(2,1)S(1)} copy(bf16[3,3,3,128,128]{3,4,2,1,0:T(8,128)(2,1)S(1)} %reverse_bitcast_fusion) | data formatting | bytes 1769472 | tf_op jit(solution)/shard_map/transpose | solution.py:275
  20.3 1.4 %copy.7 = bf16[3,3,3,128,128]{4,3,2,1,0:T(8,128)(2,1)S(1)} copy(bf16[3,3,3,128,128]{3,4,2,1,0:T(8,128)(2,1)S(1)} %bitcast_select_fusion) | data formatting | bytes 1769472 | tf_op jit(solution)/shard_map/jit(_where)/select_n | solution.py:284
  21.7 1.0 %collective-permute-done.3.near_ref = bf16[6,64,128]{2,1,0:T(8,128)(2,1)S(1)} collective-permute-done((bf16[6,64,128]{2,1,0:T(8,128)(2,1)S(1)}, bf16[6,64,128]{2,1,0:T(8,128)(2,1)S(1)}, u32[]{:S(2)}, u32[]{:S(2)}) %collective-permute-start.3) | collective-permute-done | bytes 98336 | tf_op jit(solution)/shard_map/ppermute | solution.py:293
  22.7 1.5 %shard_map.60 = (f32[512,128]{1,0:T(8,128)S(1)}, bf16[6,4,64,384]{3,2,1,0:T(8,128)(2,1)S(1)}) custom-call(bf16[6,2,64,128]{3,2,1,0:T(8,128)(2,1)S(1)} %get-tuple-element.24.src_ref, bf16[6,64,128]{2,1,0:T(8,128)(2,1)S(1)} %collective-permute-done.2.far_ref, bf16[6,64,128]{2,1,0:T(8,128)(2,1)S(1)} %collective-permute-done.3.near_ref, ...), custom_call_target="tpu_custom_call" | custom-call | tf_op jit(solution)/shard_map/pallas_call | solution.py:259
  24.2 2.4 %collective-permute-start.4 = (f32[512,128]{1,0:T(8,128)S(1)}, f32[512,128]{1,0:T(8,128)S(1)}, u32[]{:S(2)}, u32[]{:S(2)}) collective-permute-start(f32[512,128]{1,0:T(8,128)S(1)} %get-tuple-element.28.own_ref), channel_id=1, source_target_pairs={{0,32},{32,0},{1,33},{33,1},{2,34},{34,2},{3,35},{35,3},{4,36},{36... | collective-permute-start | bytes 786440 | tf_op jit(solution)/shard_map/ppermute | solution.py:299
  26.6 1.1 %collective-permute-done.4.other_ref = f32[512,128]{1,0:T(8,128)S(1)} collective-permute-done((f32[512,128]{1,0:T(8,128)S(1)}, f32[512,128]{1,0:T(8,128)S(1)}, u32[]{:S(2)}, u32[]{:S(2)}) %collective-permute-start.4) | collective-permute-done | bytes 262176 | tf_op jit(solution)/shard_map/ppermute | solution.py:299
  27.7 2.5 %shard_map.61 = (bf16[16,224,128]{2,1,0:T(8,128)(2,1)}, bf16[4,2,64,128]{3,2,1,0:T(8,128)(2,1)S(1)}, bf16[4,64,128]{2,1,0:T(8,128)(2,1)S(1)}, bf16[2,2,64,128]{3,2,1,0:T(8,128)(2,1)S(1)}) custom-call(f32[512,128]{1,0:T(8,128)S(1)} %get-tuple-element.28.own_ref, f32[512,128]{1,0:T(8,128)S(1)} %collective-permute-done.4.other_ref, ...), custom_call_target="tpu_custom_call" | custom-call | tf_op jit(solution)/shard_map/pallas_call | solution.py:259
  30.3 21.7 %all-to-all-start = ((bf16[16,224,128]{2,1,0:T(8,128)(2,1)}), bf16[16,224,128]{2,1,0:T(8,128)(2,1)S(1)}, u32[]{:S(2)}, u32[]{:S(2)}) async-start(bf16[16,224,128]{2,1,0:T(8,128)(2,1)} %get-tuple-element.30), calls=%async_computation | async-start | bytes 1835008 | tf_op jit(solution)/shard_map/all_to_all | solution.py:309
  52.0 1.3 %collective-permute-start.5 = (bf16[2,2,64,128]{3,2,1,0:T(8,128)(2,1)S(1)}, bf16[2,2,64,128]{3,2,1,0:T(8,128)(2,1)S(1)}, u32[]{:S(2)}, u32[]{:S(2)}) collective-permute-start(bf16[2,2,64,128]{3,2,1,0:T(8,128)(2,1)S(1)} %get-tuple-element.31), channel_id=1, source_target_pairs={{64,32},{65,33},{66,34},{67,35},{68,36},{69,37},{70,38},{71,39},{7... | collective-permute-start | bytes 196616 | tf_op jit(solution)/shard_map/ppermute | solution.py:310
  53.9 8.1 %collective-permute-done.5.before_ref = bf16[2,2,64,128]{3,2,1,0:T(8,128)(2,1)S(1)} collective-permute-done((bf16[2,2,64,128]{3,2,1,0:T(8,128)(2,1)S(1)}, bf16[2,2,64,128]{3,2,1,0:T(8,128)(2,1)S(1)}, u32[]{:S(2)}, u32[]{:S(2)}) %collective-permute-start.5) | collective-permute-done | bytes 65568 | tf_op jit(solution)/shard_map/ppermute | solution.py:310
  62.0 4.8 %all-to-all-done.got_ref = bf16[16,224,128]{2,1,0:T(8,128)(2,1)S(1)} async-done(((bf16[16,224,128]{2,1,0:T(8,128)(2,1)}), bf16[16,224,128]{2,1,0:T(8,128)(2,1)S(1)}, u32[]{:S(2)}, u32[]{:S(2)}) %all-to-all-start) | async-done | bytes 917536 | tf_op jit(solution)/shard_map/all_to_all | solution.py:309
  67.7 6.6 %all-to-all-start.1 = ((bf16[16,16,128]{2,1,0:T(8,128)(2,1)}), bf16[16,16,128]{2,1,0:T(8,128)(2,1)S(1)}, u32[]{:S(2)}, u32[]{:S(2)}) async-start(bf16[16,16,128]{2,1,0:T(8,128)(2,1)} %shard_map.62), calls=%async_computation.1 | async-start | bytes 131072 | tf_op jit(solution)/shard_map/all_to_all | solution.py:314
  74.3 3.3 %collective-permute-start.8 = (bf16[4,64,128]{2,1,0:T(8,128)(2,1)S(1)}, bf16[4,64,128]{2,1,0:T(8,128)(2,1)S(1)}, u32[]{:S(2)}, u32[]{:S(2)}) collective-permute-start(bf16[4,64,128]{2,1,0:T(8,128)(2,1)S(1)} %get-tuple-element.40), channel_id=1, source_target_pairs={{0,1},{1,0},{2,3},{3,2},{4,5},{5,4},{6,7},{7,6},{8,9},{9,8},{10,11... | collective-permute-start | bytes 196616 | tf_op jit(solution)/shard_map/ppermute | solution.py:321
  77.6 1.3 %collective-permute-start.7 = (bf16[2,64,128]{2,1,0:T(8,128)(2,1)S(1)}, bf16[2,64,128]{2,1,0:T(8,128)(2,1)S(1)}, u32[]{:S(2)}, u32[]{:S(2)}) collective-permute-start(bf16[2,64,128]{2,1,0:T(8,128)(2,1)S(1)} %get-tuple-element.39), channel_id=1, source_target_pairs={{0,32},{1,33},{2,34},{3,35},{4,36},{5,37},{6,38},{7,39},{8,40},{9,... | collective-permute-start | bytes 98312 | tf_op jit(solution)/shard_map/ppermute | solution.py:322
  78.9 4.0 %collective-permute-done.7.corner_ref = bf16[2,64,128]{2,1,0:T(8,128)(2,1)S(1)} collective-permute-done((bf16[2,64,128]{2,1,0:T(8,128)(2,1)S(1)}, bf16[2,64,128]{2,1,0:T(8,128)(2,1)S(1)}, u32[]{:S(2)}, u32[]{:S(2)}) %collective-permute-start.7) | collective-permute-done | bytes 32800 | tf_op jit(solution)/shard_map/ppermute | solution.py:322
  82.9 1.3 %shard_map.64 = bf16[2,2,64,128]{3,2,1,0:T(8,128)(2,1)} custom-call(bf16[4,2,64,128]{3,2,1,0:T(8,128)(2,1)S(1)} %get-tuple-element.37.src_ref, bf16[4,64,128]{2,1,0:T(8,128)(2,1)S(1)} %collective-permute-done.6.edge_ref, bf16[2,64,128]{2,1,0:T(8,128)(2,1)S(1)} %collective-permute-done.7.corner_ref, bf16[4,64,128]{2,1,0:T(8,128)(2,1)S(1)} %collective-permute-done.8.near_ref, ...), custom_call_target="tpu_custom_call" | custom-call | flops 1600000000 | tf_op jit(solution)/shard_map/pallas_call | solution.py:259
  84.2 1.8 %all-to-all-done.1.got_ref = bf16[16,16,128]{2,1,0:T(8,128)(2,1)S(1)} async-done(((bf16[16,16,128]{2,1,0:T(8,128)(2,1)}), bf16[16,16,128]{2,1,0:T(8,128)(2,1)S(1)}, u32[]{:S(2)}, u32[]{:S(2)}) %all-to-all-start.1) | async-done | bytes 65568 | tf_op jit(solution)/shard_map/all_to_all | solution.py:314
  86.0 5.9 %collective-permute-start.9 = (f32[8,128]{1,0:T(8,128)S(1)}, f32[8,128]{1,0:T(8,128)S(1)}, u32[]{:S(2)}, u32[]{:S(2)}) collective-permute-start(f32[8,128]{1,0:T(8,128)S(1)} %get-tuple-element.45), channel_id=1, source_target_pairs={{0,32},{32,0},{1,33},{33,1},{2,34},{34,2},{3,35},{35,3},{4,36},{36... | collective-permute-start | bytes 12296 | tf_op jit(solution)/shard_map/ppermute | solution.py:335
  (20 shorter events, 3.8 us)
Async XLA Ops:
  1.5 13.1 %collective-permute-start.1 = (bf16[2,2,64,128]{3,2,1,0:T(8,128)(2,1)S(1)}, bf16[2,2,64,128]{3,2,1,0:T(8,128)(2,1)S(1)}, u32[]{:S(2)}, u32[]{:S(2)}) collective-permute-start(bf16[2,2,64,128]{3,2,1,0:T(8,128)(2,1)S(1)} %broadcast_select_fusion), channel_id=1, source_target_pairs={{32,64},{96,128},{160,192},{224,256},{288,320},{352,384},{416,448}... | collective-permute-start | bytes 196616 | tf_op jit(solution)/shard_map/ppermute | solution.py:282
  6.1 8.5 %collective-permute-start = (bf16[2,2,64,128]{3,2,1,0:T(8,128)(2,1)S(1)}, bf16[2,2,64,128]{3,2,1,0:T(8,128)(2,1)S(1)}, u32[]{:S(2)}, u32[]{:S(2)}) collective-permute-start(bf16[2,2,64,128]{3,2,1,0:T(8,128)(2,1)S(1)} %broadcast_select_fusion), channel_id=1, source_target_pairs={{0,32},{32,0},{1,33},{33,1},{2,34},{34,2},{3,35},{35,3},{4,36},{36... | collective-permute-start | bytes 196616 | tf_op jit(solution)/shard_map/ppermute | solution.py:283
  13.0 1.6 %copy-start = (bf16[2,2,64,128]{3,2,1,0:T(8,128)(2,1)S(1)}, bf16[2,2,64,128]{3,2,1,0:T(8,128)(2,1)}, u32[]{:S(2)}) copy-start(bf16[2,2,64,128]{3,2,1,0:T(8,128)(2,1)} %clip_ref.1) | copy-start | bytes 196612
  13.0 1.6 %copy-start.1 = (bf16[2,2,64,128]{3,2,1,0:T(8,128)(2,1)S(1)}, bf16[2,2,64,128]{3,2,1,0:T(8,128)(2,1)}, u32[]{:S(2)}) copy-start(bf16[2,2,64,128]{3,2,1,0:T(8,128)(2,1)} %cot_ref.3) | copy-start | bytes 196612
  13.0 5.8 %copy-start.2 = (bf16[3,3,3,128,128]{4,3,2,1,0:T(8,128)(2,1)S(1)}, bf16[3,3,3,128,128]{4,3,2,1,0:T(8,128)(2,1)}, u32[]{:S(2)}) copy-start(bf16[3,3,3,128,128]{4,3,2,1,0:T(8,128)(2,1)} %param.5) | copy-start | bytes 2654212
  14.7 7.0 %collective-permute-start.2 = (bf16[6,64,128]{2,1,0:T(8,128)(2,1)S(1)}, bf16[6,64,128]{2,1,0:T(8,128)(2,1)S(1)}, u32[]{:S(2)}, u32[]{:S(2)}) collective-permute-start(bf16[6,64,128]{2,1,0:T(8,128)(2,1)S(1)} %get-tuple-element.25), channel_id=1, source_target_pairs={{1,2},{3,4},{5,6},{7,8},{9,10},{11,12},{13,14},{15,16},{17,18},{19... | collective-permute-start | bytes 294920 | tf_op jit(solution)/shard_map/ppermute | solution.py:292
  15.3 7.4 %collective-permute-start.3 = (bf16[6,64,128]{2,1,0:T(8,128)(2,1)S(1)}, bf16[6,64,128]{2,1,0:T(8,128)(2,1)S(1)}, u32[]{:S(2)}, u32[]{:S(2)}) collective-permute-start(bf16[6,64,128]{2,1,0:T(8,128)(2,1)S(1)} %get-tuple-element.26), channel_id=1, source_target_pairs={{0,1},{1,0},{2,3},{3,2},{4,5},{5,4},{6,7},{7,6},{8,9},{9,8},{10,11... | collective-permute-start | bytes 294920 | tf_op jit(solution)/shard_map/ppermute | solution.py:293
  24.2 3.5 %collective-permute-start.4 = (f32[512,128]{1,0:T(8,128)S(1)}, f32[512,128]{1,0:T(8,128)S(1)}, u32[]{:S(2)}, u32[]{:S(2)}) collective-permute-start(f32[512,128]{1,0:T(8,128)S(1)} %get-tuple-element.28.own_ref), channel_id=1, source_target_pairs={{0,32},{32,0},{1,33},{33,1},{2,34},{34,2},{3,35},{35,3},{4,36},{36... | collective-permute-start | bytes 786440 | tf_op jit(solution)/shard_map/ppermute | solution.py:299
  30.3 36.6 %all-to-all-start = ((bf16[16,224,128]{2,1,0:T(8,128)(2,1)}), bf16[16,224,128]{2,1,0:T(8,128)(2,1)S(1)}, u32[]{:S(2)}, u32[]{:S(2)}) async-start(bf16[16,224,128]{2,1,0:T(8,128)(2,1)} %get-tuple-element.30), calls=%async_computation | async-start | bytes 1835008 | tf_op jit(solution)/shard_map/all_to_all | solution.py:309
  52.0 10.0 %collective-permute-start.5 = (bf16[2,2,64,128]{3,2,1,0:T(8,128)(2,1)S(1)}, bf16[2,2,64,128]{3,2,1,0:T(8,128)(2,1)S(1)}, u32[]{:S(2)}, u32[]{:S(2)}) collective-permute-start(bf16[2,2,64,128]{3,2,1,0:T(8,128)(2,1)S(1)} %get-tuple-element.31), channel_id=1, source_target_pairs={{64,32},{65,33},{66,34},{67,35},{68,36},{69,37},{70,38},{71,39},{7... | collective-permute-start | bytes 196616 | tf_op jit(solution)/shard_map/ppermute | solution.py:310
  53.3 21.0 %collective-permute-start.6 = (bf16[4,64,128]{2,1,0:T(8,128)(2,1)S(1)}, bf16[4,64,128]{2,1,0:T(8,128)(2,1)S(1)}, u32[]{:S(2)}, u32[]{:S(2)}) collective-permute-start(bf16[4,64,128]{2,1,0:T(8,128)(2,1)S(1)} %get-tuple-element.35), channel_id=1, source_target_pairs={{1,2},{3,4},{5,6},{7,8},{9,10},{11,12},{13,14},{15,16},{17,18},{19... | collective-permute-start | bytes 196616 | tf_op jit(solution)/shard_map/ppermute | solution.py:311
  67.7 18.3 %all-to-all-start.1 = ((bf16[16,16,128]{2,1,0:T(8,128)(2,1)}), bf16[16,16,128]{2,1,0:T(8,128)(2,1)S(1)}, u32[]{:S(2)}, u32[]{:S(2)}) async-start(bf16[16,16,128]{2,1,0:T(8,128)(2,1)} %shard_map.62), calls=%async_computation.1 | async-start | bytes 131072 | tf_op jit(solution)/shard_map/all_to_all | solution.py:314
  74.3 8.5 %collective-permute-start.8 = (bf16[4,64,128]{2,1,0:T(8,128)(2,1)S(1)}, bf16[4,64,128]{2,1,0:T(8,128)(2,1)S(1)}, u32[]{:S(2)}, u32[]{:S(2)}) collective-permute-start(bf16[4,64,128]{2,1,0:T(8,128)(2,1)S(1)} %get-tuple-element.40), channel_id=1, source_target_pairs={{0,1},{1,0},{2,3},{3,2},{4,5},{5,4},{6,7},{7,6},{8,9},{9,8},{10,11... | collective-permute-start | bytes 196616 | tf_op jit(solution)/shard_map/ppermute | solution.py:321
  77.6 5.3 %collective-permute-start.7 = (bf16[2,64,128]{2,1,0:T(8,128)(2,1)S(1)}, bf16[2,64,128]{2,1,0:T(8,128)(2,1)S(1)}, u32[]{:S(2)}, u32[]{:S(2)}) collective-permute-start(bf16[2,64,128]{2,1,0:T(8,128)(2,1)S(1)} %get-tuple-element.39), channel_id=1, source_target_pairs={{0,32},{1,33},{2,34},{3,35},{4,36},{5,37},{6,38},{7,39},{8,40},{9,... | collective-permute-start | bytes 98312 | tf_op jit(solution)/shard_map/ppermute | solution.py:322
  86.0 6.7 %collective-permute-start.9 = (f32[8,128]{1,0:T(8,128)S(1)}, f32[8,128]{1,0:T(8,128)S(1)}, u32[]{:S(2)}, u32[]{:S(2)}) collective-permute-start(f32[8,128]{1,0:T(8,128)S(1)} %get-tuple-element.45), channel_id=1, source_target_pairs={{0,32},{32,0},{1,33},{33,1},{2,34},{34,2},{3,35},{35,3},{4,36},{36... | collective-permute-start | bytes 12296 | tf_op jit(solution)/shard_map/ppermute | solution.py:335

commit v5 on v4

--- a/solution.py
+++ b/solution.py
@@ -11,24 +11,47 @@
 TM = ("zh", "y", "c")
 ROWS = ("x", "zl")
 VMEM = pl.BlockSpec(memory_space=pltpu.VMEM)
-PARAMS = pltpu.CompilerParams(vmem_limit_bytes=48 * 1024 * 1024)
 
 
 SWAP = [(0, 1), (1, 0)]
 NEAR_ROWS = [(r, r ^ 1) for r in range(32)]
 FAR_ROWS = [(r, r + 1) for r in range(1, 31, 2)] + [(r + 1, r) for r in range(1, 31, 2)]
-BEYOND = [(2 * k + 1, 2 * k + 2) for k in range(7)] + [(2 * k + 2, 2 * k + 1) for k in range(7)]
-BEFORE = [((2 * k + 2) * 32 + r, (2 * k + 1) * 32 + r) for k in range(7) for r in range(32)] + [
-    ((2 * k + 3) * 32 + r, 2 * k * 32 + q) for k in range(7) for r, q in FAR_ROWS
+ENDS = [(r, q) for r, q in FAR_ROWS if r // 8 != q // 8]
+MIDDLES = [(r, q) for r, q in FAR_ROWS if r // 8 == q // 8]
+ENDS_OF = [r for r, _ in ENDS]
+
+
+PLANES = [list(range(15, -1, -1)), list(range(16, 32))]
+
+
+def device(chip, core, slab):
+    return (2 * chip + core) * 32 + slab
+
+
+BEYOND = [pair for k in (0, 1, 2, 4, 5, 6) for pair in ((2 * k + 1, 2 * k + 2), (2 * k + 2, 2 * k + 1))]
+BEYOND_FAR = [(7, 8), (8, 7)]
+CORNER_FREE = [(device(3, 0, r), device(4, 1, q)) for r, q in ENDS] + [
+    (device(4, 1, r), device(3, 0, q)) for r, q in ENDS
 ]
+CORNER_ROWS = [(device(k, c, r), device(k, c, q)) for k, c in ((3, 1), (4, 0)) for r, q in MIDDLES] + [
+    (device(k, c, r), device(k, 1 - c, r)) for k, c in ((3, 0), (4, 1)) for r in ENDS_OF
+]
+BEFORE = [(device(k + 1, 0, r), device(k, 1, r)) for k in range(7) for r in range(32)] + [
+    (device(4, 1, r), device(3, 0, q)) for r, q in ENDS
+]
+CORNER_GRAD = (
+    [(device(k, 1, r), device(k, 1, q)) for k in range(7) for r, q in MIDDLES]
+    + [(device(k + 1, 1, r), device(k, 1, r)) for k in (0, 1, 2, 4, 5, 6) for r in ENDS_OF]
+    + [(device(3, 0, r), device(3, 1, r)) for r in ENDS_OF]
+)
 
 
 def place():
     core = lax.axis_index("c")
     chip = lax.axis_index("zh") * 4 + lax.axis_index("y")
-    slab = lax.axis_index("x") * 8 + lax.axis_index("zl")
-    odd = slab & 1
-    return core, chip, slab, odd
+    odd = lax.axis_index("zl") & 1
+    end = (lax.axis_index("zl") == 0) | (lax.axis_index("zl") == 7)
+    return core, chip, end, odd
 
 
 def contract_first(lhs, rhs):
@@ -59,96 +82,119 @@
     return part.reshape(count * 2 * part.shape[2], part.shape[3])
 
 
-def conv_all(triples_ref, kernel_ref, frames):
+def conv(triples_ref, kernel_ref, frames):
     total = None
     for a in range(3):
         for b in range(3):
+            start = (a * 3 + b) * 384
             term = jnp.dot(
                 stripe(triples_ref, a, frames, b),
-                kernel_ref[a * 3 + b],
+                kernel_ref[start : start + 384, :],
                 preferred_element_type=jnp.float32,
             )
             total = term if total is None else total + term
     return total
 
 
-def fold_all(triples_ref, kernel_ref):
+def back_terms(triples_ref, kernel_ref, frames, taps):
     total = None
-    for f, a in ((0, 2), (0, 1), (1, 2)):
+    for f, a in taps:
         for b in range(3):
-            term = jnp.dot(
-                stripe(triples_ref, f, 1, b),
-                kernel_ref[a * 3 + b],
-                preferred_element_type=jnp.float32,
-            )
+            part = stripe(triples_ref, f, frames, b)
+            starts = [((2 - a) * 9 + (2 - b) * 3 + (2 - d)) * 128 for d in range(3)]
+            turned = jnp.concatenate([kernel_ref[start : start + 128, :] for start in starts], axis=1)
+            term = lax.dot_general(part, turned, (((1,), (1,)), ((), ())), preferred_element_type=jnp.float32)
             total = term if total is None else total + term
     return total
 
 
-def assemble_kernel(clip_ref, cot_ref, other_ref, beyond_ref, src_ref, edge_ref, inner_ref):
+TAPS = ((0, 0), (1, 1), (2, 2))
+FOLD = ((0, 2), (0, 1), (1, 2))
+
+
+def edge_kernel(mine_ref, both_ref, beyond_ref, edge_ref, corner_ref):
     core, chip, _, odd = place()
+    other_ref = both_ref.at[pl.ds(2 - 2 * core, 2)]
+    corner_ref[...] = other_ref[:, odd]
+    edge_ref[pl.ds(4 * core, 2)] = beyond_ref[:, odd]
+    edge_ref[2:4] = mine_ref[:, odd]
+    edge_ref[pl.ds(4 - 4 * core, 2)] = other_ref[:, odd]
+
+    @pl.when((core == 0) & (chip == 0))
+    def _():
+        edge_ref[0] = mine_ref[0, odd]
+        edge_ref[1] = mine_ref[0, odd]
+
+
+def assemble_kernel(mine_ref, both_ref, beyond_ref, beyond_far_ref, free_ref, src_ref, inner_ref, corner_ref):
+    core, chip, end, odd = place()
+    src_ref[pl.ds(4 * core, 2)] = beyond_ref[...] + beyond_far_ref[...]
+    src_ref[2:4] = mine_ref[...]
+    src_ref[pl.ds(4 - 4 * core, 2)] = both_ref[pl.ds(2 - 2 * core, 2)]
+
+    @pl.when((core == 0) & (chip == 0))
+    def _():
+        src_ref[0] = mine_ref[0]
+        src_ref[1] = mine_ref[0]
+
+    inner_ref[...] = src_ref[:, 1 - odd]
+    corner_ref[...] = jnp.where(end, free_ref[...], beyond_far_ref[:, odd])
+
+
+def first_conv_kernel(
+    src_ref, far_ref, near_ref, corner_ref, kernel_ref, out_ref, triples_ref, outer_ref
+):
+    core, chip, _, _ = place()
+    outer_ref[...] = far_ref[...]
+    outer_ref[pl.ds(4 * core, 2)] += corner_ref[...]
+    fill_triples(src_ref, outer_ref, near_ref, triples_ref, 6)
 
     @pl.when(core == 0)
     def _():
-        src_ref[0:2] = beyond_ref[...]
-        src_ref[2:4] = clip_ref[...]
-        src_ref[4:6] = other_ref[...]
-
-        @pl.when(chip == 0)
-        def _():
-            src_ref[0] = clip_ref[0]
-            src_ref[1] = clip_ref[0]
+        out_ref[...] = conv(triples_ref, kernel_ref, 4)
 
     @pl.when(core == 1)
     def _():
-        src_ref[0:2] = other_ref[...]
-        src_ref[2:4] = cot_ref[...]
-        src_ref[4:6] = beyond_ref[...]
-
-    edge_ref[...] = src_ref[:, odd]
-    inner_ref[...] = src_ref[:, 1 - odd]
-
-
-def assemble_grad_kernel(act_ref, before_ref, src_ref, inner_ref, corner_ref):
-    core, _, _, odd = place()
-    corner_ref[...] = before_ref[:, 0]
+        out_ref[...] = back_terms(triples_ref, kernel_ref, 4, TAPS)
+
+    @pl.when((core == 1) & (chip == 0))
+    def _():
+        out_ref[0:128, :] += back_terms(triples_ref, kernel_ref, 1, FOLD)
+
+
+def assemble_grad_kernel(act_ref, before_ref, far_ref, src_ref, inner_ref, corner_ref):
+    core, _, end, odd = place()
 
     @pl.when(core == 0)
     def _():
         src_ref[...] = act_ref[...]
+        corner_ref[...] = before_ref[:, 0]
 
     @pl.when(core == 1)
     def _():
         src_ref[0:2] = act_ref[2:4]
         src_ref[2:4] = before_ref[...]
+        corner_ref[...] = jnp.where(end, far_ref[2:4], before_ref[:, odd])
 
     inner_ref[...] = src_ref[:, 1 - odd]
 
 
-def first_conv_kernel(src_ref, far_ref, near_ref, kernel_ref, out_ref, triples_ref):
-    fill_triples(src_ref, far_ref, near_ref, triples_ref, 6)
-    out_ref[...] = conv_all(triples_ref, kernel_ref, 4)
-
-    @pl.when((lax.axis_index("c") == 1) & (lax.axis_index("zh") == 0) & (lax.axis_index("y") == 0))
-    def _():
-        out_ref[0:128, :] += fold_all(triples_ref, kernel_ref)
-
-
 def input_conv_kernel(
-    src_ref, edge_ref, corner_ref, near_ref, kernel_ref, cot_ref, out_ref, far_ref, triples_ref, sum_ref
+    src_ref, far_ref, corner_ref, near_ref, kernel_ref, cot_ref, out_ref, outer_ref, triples_ref, sum_ref
 ):
-    far_ref[...] = edge_ref[...]
-
-    @pl.when(lax.axis_index("c") == 1)
-    def _():
-        far_ref[2:4] = corner_ref[...]
-
-    fill_triples(src_ref, far_ref, near_ref, triples_ref, 4)
-    sum_ref[...] = conv_all(triples_ref, kernel_ref, 2)
-
-    @pl.when((lax.axis_index("c") == 0) & (lax.axis_index("zh") == 0) & (lax.axis_index("y") == 0))
-    def _():
-        sum_ref[0:128, :] += fold_all(triples_ref, kernel_ref)
+    core, chip, _, _ = place()
+    outer_ref[...] = far_ref[...]
+
+    @pl.when(core == 1)
+    def _():
+        outer_ref[2:4] = corner_ref[...]
+
+    fill_triples(src_ref, outer_ref, near_ref, triples_ref, 4)
+    sum_ref[...] = back_terms(triples_ref, kernel_ref, 2, TAPS)
+
+    @pl.when((core == 0) & (chip == 0))
+    def _():
+        sum_ref[0:128, :] += back_terms(triples_ref, kernel_ref, 1, FOLD)
 
     cot = cot_ref[...].reshape(256, 128).astype(jnp.float32)
     out_ref[...] = (cot + sum_ref[...]).astype(jnp.bfloat16).reshape(out_ref.shape)
@@ -164,7 +210,7 @@
     hidden = (pre_act * sig).astype(jnp.bfloat16)
     act_ref[...] = act_grad.reshape(act_ref.shape)
     edge_ref[0:2] = act_ref[pl.ds(2 * core, 2), odd]
-    edge_ref[2:4] = act_ref[2:4, odd]
+    edge_ref[2:4] = act_ref[pl.ds(2 - 2 * core, 2), odd]
 
     @pl.when(core == 0)
     def _():
@@ -208,7 +254,9 @@
                     start = 54 * (((zh * 4 + y) * 2 + c) * 4 + x)
                     blocks.append(terms_ref[start : start + 54, :])
             blocks.append(jnp.zeros((8, 128), jnp.float32))
-            send_ref[y * 4 + x] = jnp.concatenate(blocks, axis=0).astype(jnp.bfloat16)
+            rank = y * 4 + x
+            rank = jnp.where(lax.axis_index("zh") == 0, 15 - rank, rank)
+            send_ref[rank] = jnp.concatenate(blocks, axis=0).astype(jnp.bfloat16)
 
 
 def plane_sum_kernel(got_ref, send_ref, sum_ref):
@@ -262,39 +310,48 @@
         in_specs=[VMEM] * len(args),
         out_specs=[VMEM] * len(out_shape) if many else VMEM,
         scratch_shapes=scratch,
-        compiler_params=PARAMS,
+        compiler_params=pltpu.CompilerParams(vmem_limit_bytes=32 * 1024 * 1024),
         cost_estimate=pl.CostEstimate(flops=flops, bytes_accessed=0, transcendentals=0) if flops else None,
     )(*args)
 
 
 def shaped(shape, dtype):
     return jax.ShapeDtypeStruct(shape, dtype)
-
-
-def flipped(kernel):
-    return jnp.flip(kernel, (0, 1, 2)).transpose(0, 1, 2, 4, 3)
 
 
 def per_device(video_clip, first_kernel, second_kernel, cotangent):
     bf16, f32 = jnp.bfloat16, jnp.float32
     core = lax.axis_index("c")
+    everywhere = TM + ROWS
+    first_kernel, second_kernel = first_kernel.reshape(3456, 128), second_kernel.reshape(3456, 128)
     given = jnp.where(core == 0, cotangent, video_clip)
+    mine = jnp.where(core == 0, video_clip, cotangent)
+    given, mine = lax.optimization_barrier((given, mine))
+    both = lax.all_gather(given, "c", tiled=True)
+    both, given = lax.optimization_barrier((both, given))
+    beyond_far = lax.ppermute(given, TM, BEYOND_FAR)
     beyond = lax.ppermute(given, TM, BEYOND)
-    other_frames = lax.ppermute(given, "c", SWAP)
-    kernel = jnp.where(core == 0, first_kernel, flipped(second_kernel)).reshape(9, 384, 128)
-    first_back = flipped(first_kernel).reshape(9, 384, 128)
-    kernel, first_back = lax.optimization_barrier((kernel, first_back))
-    source, edge, inner = call(
+    edge, corner = call(
+        edge_kernel,
+        (shaped((6, 64, 128), bf16), shaped((2, 64, 128), bf16)),
+        mine, both, beyond,
+    )
+    far = lax.ppermute(edge, ROWS, FAR_ROWS)
+    free = lax.ppermute(corner, everywhere, CORNER_FREE)
+    source, inner, corner = call(
         assemble_kernel,
-        (shaped((6, 2, 64, 128), bf16), shaped((6, 64, 128), bf16), shaped((6, 64, 128), bf16)),
-        video_clip, cotangent, other_frames, beyond,
-    )
-    far = lax.ppermute(edge, ROWS, FAR_ROWS)
+        (shaped((6, 2, 64, 128), bf16), shaped((6, 64, 128), bf16), shaped((2, 64, 128), bf16)),
+        mine, both, beyond, beyond_far, free,
+    )
+    inner, corner, second = lax.optimization_barrier((inner, corner, second_kernel))
+    kernel = jnp.where(core == 0, first_kernel, second)
     near = lax.ppermute(inner, ROWS, NEAR_ROWS)
+    corner = lax.ppermute(corner, everywhere, CORNER_ROWS)
     own, triples = call(
         first_conv_kernel,
         (shaped((512, 128), f32), shaped((6, 4, 64, 384), bf16)),
-        source, far, near, kernel,
+        source, far, near, corner, kernel,
+        scratch=[pltpu.VMEM((6, 64, 128), bf16)],
     )
     other = lax.ppermute(own, "c", SWAP)
     send, act_grad, edge, before = call(
@@ -306,26 +363,25 @@
         own, other, triples,
         scratch=[pltpu.VMEM((3456, 128), f32)],
     )
-    got = lax.all_to_all(send, ("y", "x"), 0, 0, tiled=True)
-    before = lax.ppermute(before, TM + ROWS, BEFORE)
+    got = lax.all_to_all(send, ("zh", "y", "x"), 0, 0, axis_index_groups=PLANES, tiled=True)
+    before = lax.ppermute(before, everywhere, BEFORE)
     far = lax.ppermute(edge, ROWS, FAR_ROWS)
-    got, before = lax.optimization_barrier((got, before))
     send = call(plane_sum_kernel, shaped((16, 16, 128), bf16), got, scratch=[pltpu.VMEM((224, 128), f32)])
     got = lax.all_to_all(send, ("zh", "zl"), 0, 0, tiled=True)
     _, before, far = lax.optimization_barrier((send, before, far))
     source, inner, corner = call(
         assemble_grad_kernel,
         (shaped((4, 2, 64, 128), bf16), shaped((4, 64, 128), bf16), shaped((2, 64, 128), bf16)),
-        act_grad, before,
+        act_grad, before, far,
     )
     near = lax.ppermute(inner, ROWS, NEAR_ROWS)
-    corner = lax.ppermute(corner, "c", [(0, 1)])
+    corner = lax.ppermute(corner, everywhere, CORNER_GRAD)
     input_grad = call(
         input_conv_kernel,
         shaped((2, 2, 64, 128), bf16),
-        source, far, corner, near, first_back, cotangent,
+        source, far, corner, near, first_kernel, cotangent,
         scratch=[
-            pltpu.VMEM((4, 64, 128), bf16), pltpu.VMEM((4, 4, 64, 384), bf16), pltpu.VMEM((256, 128), f32)
+            pltpu.VMEM((4, 64, 128), bf16), pltpu.VMEM((4, 4, 64, 384), bf16), pltpu.VMEM((256, 128), f32),
         ],
         flops=1_600_000_000,
     )

time: 93.8 us -> 92 us (0.981)
  blocking collectives: 0 us -> 8.43 us
  starting transfers between devices: 56.7 us -> 48.8 us
  local copies, waits for them, and re-layouts: 4.85 us -> 0.01 us
  waiting for transfers between devices: 21.6 us -> 23.8 us
    ppermute x3 -> x5, waiting for transfers between devices: 12 us -> 0.01 us  [the longest x1 0.01 us: per_device(): beyond_far = lax.ppermute(given, TM, BEYOND_FAR)]
    all_gather x0 -> x1, blocking collectives: none -> 8.43 us  [per_device(): both = lax.all_gather(given, 'c', tiled=True)]
    all_to_all x1, waiting for transfers between devices: 4.81 us -> 9.83 us  [per_device(): lax.all_to_all(send, ('zh', 'y', 'x'), 0, 0, axis_index_groups=PLANES, ti...]
    ppermute x3 -> x5, starting transfers between devices: 7.44 us -> 3.93 us  [the longest x1 1.28 us: per_device(): before = lax.ppermute(before, everywhere, BEFORE)]
    all_to_all x1, waiting for transfers between devices: 1.78 us -> 4.98 us  [per_device(): got = lax.all_to_all(send, ('zh', 'zl'), 0, 0, tiled=True)]
    ppermute x1, waiting for transfers between devices: 0.01 us -> 2.98 us  [per_device(): beyond = lax.ppermute(given, TM, BEYOND)]
    ppermute x1, starting transfers between devices: 4.59 us -> 1.91 us  [per_device(): beyond = lax.ppermute(given, TM, BEYOND)]
    ppermute x2, waiting for transfers between devices: 0.98 us -> 3.64 us  [per_device(): near = lax.ppermute(inner, ROWS, NEAR_ROWS)]
  transfers between devices with their start and end apart: 12 -> 14, of which waited for: 7 -> 7; matrix products, arithmetic and copies ran while one was open for 7% -> 1% of each run, Pallas kernels for 2% -> 2%
where the time goes in v5:
time: 92 us; the launch traced here: 91.4 us
  starting transfers between devices  48.8 us (53%)
  waiting for transfers between devices  23.8 us (26%)
  blocking collectives  8.43 us (9%)
  Pallas kernels  7.3 us (8%)
  other arithmetic  2.23 us (2%)
    all_to_all x1, starting transfers between devices, per_device(): lax.all_to_all(send, ('zh', 'y', 'x'), 0, 0, axis_index_groups=PLANES, ti...  20.9 us
    all_to_all x1, waiting for transfers between devices, per_device(): lax.all_to_all(send, ('zh', 'y', 'x'), 0, 0, axis_index_groups=PLANES, ti...  9.83 us
    all_gather x1, blocking collectives, per_device(): both = lax.all_gather(given, 'c', tiled=True)  8.43 us
    all_to_all x1, starting transfers between devices, per_device(): got = lax.all_to_all(send, ('zh', 'zl'), 0, 0, tiled=True)  7.62 us
    pallas_call x9, Pallas kernels, call(): pl.pallas_call(kernel, out_shape=out_shape, in_specs=[VMEM] * len(args),...  7.3 us
    ppermute x1, starting transfers between devices, per_device(): other_share = lax.ppermute(send_share, 'c', SWAP)  5.94 us
    ppermute x2, starting transfers between devices, per_device(): near = lax.ppermute(inner, ROWS, NEAR_ROWS)  5.19 us
    all_to_all x1, waiting for transfers between devices, per_device(): got = lax.all_to_all(send, ('zh', 'zl'), 0, 0, tiled=True)  4.98 us
  transfers between devices with their start and end apart: 14, of which 7 were waited for; matrix products, arithmetic and copies ran while one was open for 1% of the time, Pallas kernels for 2%

profile of v5, /device:TPU:1, one launch (start us, length us, event | category | flops | bytes accessed | tf_op | source)
XLA Modules:
  0.0 91.4 jit_solution(7323822213873008489)
XLA Ops:
  0.6 1.0 %broadcast_select_fusion.1 = (bf16[2,2,64,128]{3,2,1,0:T(8,128)(2,1)S(1)}, bf16[2,2,64,128]{3,2,1,0:T(8,128)(2,1)S(1)}) fusion(bf16[2,2,64,128]{3,2,1,0:T(8,128)(2,1)} %param.4, bf16[2,2,64,128]{3,2,1,0:T(8,128)(2,1)} %cot_ref.1, pred[]{:T(512)S(6)} %eq.2), kind=kLoop, calls=%fused_computation.1 | loop fusion | flops 65536 | bytes 262145 | tf_op jit(solution)/shard_map/jit(_where)/select_n | solution.py:328
  1.6 8.4 %all_gather.3.both_ref = bf16[4,2,64,128]{3,2,1,0:T(8,128)(2,1)S(1)} all-gather(bf16[2,2,64,128]{3,2,1,0:T(8,128)(2,1)S(1)} %get-tuple-element.32), channel_id=1, replica_groups=mesh['zh'=2,'y'=4,'c'=2,'x'=4,'zl'=8] {'c'}, dimensions={0}, use_global_device_ids=true | all-gather | bytes 196608 | tf_op jit(solution)/shard_map/all_gather | solution.py:330
  10.0 1.9 %collective-permute-start = (bf16[2,2,64,128]{3,2,1,0:T(8,128)(2,1)S(1)}, bf16[2,2,64,128]{3,2,1,0:T(8,128)(2,1)S(1)}, u32[]{:S(2)}, u32[]{:S(2)}) collective-permute-start(bf16[2,2,64,128]{3,2,1,0:T(8,128)(2,1)S(1)} %get-tuple-element.32), channel_id=1, source_target_pairs={{32,64},{64,32},{96,128},{128,96},{160,192},{192,160},{288,320},{3... | collective-permute-start | bytes 196616 | tf_op jit(solution)/shard_map/ppermute | solution.py:333
  12.6 3.0 %collective-permute-done.beyond_ref = bf16[2,2,64,128]{3,2,1,0:T(8,128)(2,1)S(1)} collective-permute-done((bf16[2,2,64,128]{3,2,1,0:T(8,128)(2,1)S(1)}, bf16[2,2,64,128]{3,2,1,0:T(8,128)(2,1)S(1)}, u32[]{:S(2)}, u32[]{:S(2)}) %collective-permute-start) | collective-permute-done | bytes 65568 | tf_op jit(solution)/shard_map/ppermute | solution.py:333
  16.3 0.7 collective-permute-start.3
  17.7 1.9 %collective-permute-start.4 = (bf16[6,64,128]{2,1,0:T(8,128)(2,1)S(1)}, bf16[6,64,128]{2,1,0:T(8,128)(2,1)S(1)}, u32[]{:S(2)}, u32[]{:S(2)}) collective-permute-start(bf16[6,64,128]{2,1,0:T(8,128)(2,1)S(1)} %get-tuple-element.38), channel_id=1, source_target_pairs={{0,1},{1,0},{2,3},{3,2},{4,5},{5,4},{6,7},{7,6},{8,9},{9,8},{10,11... | collective-permute-start | bytes 294920 | tf_op jit(solution)/shard_map/ppermute | solution.py:348
  19.7 1.3 %broadcast_select_fusion.kernel_ref = bf16[3456,128]{1,0:T(8,128)(2,1)S(1)} fusion(bf16[3456,128]{1,0:T(8,128)(2,1)} %bitcast.4, pred[]{:T(512)S(6)} %eq.2, bf16[3,3,3,128,128]{4,3,2,1,0:T(8,128)(2,1)S(1)} %copy-done), kind=kLoop, calls=%fused_computation | loop fusion | flops 442368 | bytes 2654209 | tf_op jit(solution)/shard_map/jit(_where)/select_n | solution.py:347
  21.0 2.4 %collective-permute-done.4.near_ref = bf16[6,64,128]{2,1,0:T(8,128)(2,1)S(1)} collective-permute-done((bf16[6,64,128]{2,1,0:T(8,128)(2,1)S(1)}, bf16[6,64,128]{2,1,0:T(8,128)(2,1)S(1)}, u32[]{:S(2)}, u32[]{:S(2)}) %collective-permute-start.4) | collective-permute-done | bytes 98336 | tf_op jit(solution)/shard_map/ppermute | solution.py:348
  23.3 1.8 %shard_map.61 = (f32[512,128]{1,0:T(8,128)S(1)}, bf16[6,4,64,384]{3,2,1,0:T(8,128)(2,1)S(1)}) custom-call(bf16[6,2,64,128]{3,2,1,0:T(8,128)(2,1)S(1)} %get-tuple-element.34.src_ref, bf16[6,64,128]{2,1,0:T(8,128)(2,1)S(1)} %collective-permute-done.3.far_ref, bf16[6,64,128]{2,1,0:T(8,128)(2,1)S(1)} %collective-permute-done.4.near_ref, ...), custom_call_target="tpu_custom_call" | custom-call | tf_op jit(solution)/shard_map/pallas_call | solution.py:307
  25.2 1.9 %collective-permute-start.6 = (f32[512,128]{1,0:T(8,128)S(1)}, f32[512,128]{1,0:T(8,128)S(1)}, u32[]{:S(2)}, u32[]{:S(2)}) collective-permute-start(f32[512,128]{1,0:T(8,128)S(1)} %get-tuple-element.41.own_ref), channel_id=1, source_target_pairs={{0,32},{32,0},{1,33},{33,1},{2,34},{34,2},{3,35},{35,3},{4,36},{36... | collective-permute-start | bytes 786440 | tf_op jit(solution)/shard_map/ppermute | solution.py:356
  27.1 1.5 %collective-permute-done.6.other_ref = f32[512,128]{1,0:T(8,128)S(1)} collective-permute-done((f32[512,128]{1,0:T(8,128)S(1)}, f32[512,128]{1,0:T(8,128)S(1)}, u32[]{:S(2)}, u32[]{:S(2)}) %collective-permute-start.6) | collective-permute-done | bytes 262176 | tf_op jit(solution)/shard_map/ppermute | solution.py:356
  28.6 2.6 %shard_map.62 = (bf16[16,224,128]{2,1,0:T(8,128)(2,1)}, bf16[4,2,64,128]{3,2,1,0:T(8,128)(2,1)S(1)}, bf16[4,64,128]{2,1,0:T(8,128)(2,1)S(1)}, bf16[2,2,64,128]{3,2,1,0:T(8,128)(2,1)S(1)}) custom-call(f32[512,128]{1,0:T(8,128)S(1)} %get-tuple-element.41.own_ref, f32[512,128]{1,0:T(8,128)S(1)} %collective-permute-done.6.other_ref, ...), custom_call_target="tpu_custom_call" | custom-call | tf_op jit(solution)/shard_map/pallas_call | solution.py:307
  31.2 20.9 %all-to-all-start = ((bf16[16,224,128]{2,1,0:T(8,128)(2,1)}), bf16[16,224,128]{2,1,0:T(8,128)(2,1)S(1)}, u32[]{:S(2)}, u32[]{:S(2)}) async-start(bf16[16,224,128]{2,1,0:T(8,128)(2,1)} %get-tuple-element.43), calls=%async_computation | async-start | bytes 1835008 | tf_op jit(solution)/shard_map/all_to_all | solution.py:366
  52.1 1.3 %collective-permute-start.7 = (bf16[2,2,64,128]{3,2,1,0:T(8,128)(2,1)S(1)}, bf16[2,2,64,128]{3,2,1,0:T(8,128)(2,1)S(1)}, u32[]{:S(2)}, u32[]{:S(2)}) collective-permute-start(bf16[2,2,64,128]{3,2,1,0:T(8,128)(2,1)S(1)} %get-tuple-element.45), channel_id=1, source_target_pairs={{64,32},{65,33},{66,34},{67,35},{68,36},{69,37},{70,38},{71,39},{7... | collective-permute-start | bytes 196616 | tf_op jit(solution)/shard_map/ppermute | solution.py:367
  53.4 0.7 collective-permute-start.8
  54.1 9.8 %all-to-all-done.got_ref = bf16[16,224,128]{2,1,0:T(8,128)(2,1)S(1)} async-done(((bf16[16,224,128]{2,1,0:T(8,128)(2,1)}), bf16[16,224,128]{2,1,0:T(8,128)(2,1)S(1)}, u32[]{:S(2)}, u32[]{:S(2)}) %all-to-all-start) | async-done | bytes 917536 | tf_op jit(solution)/shard_map/all_to_all | solution.py:366
  63.9 0.9 shard_map.63
  64.8 7.6 %all-to-all-start.1 = ((bf16[16,16,128]{2,1,0:T(8,128)(2,1)}), bf16[16,16,128]{2,1,0:T(8,128)(2,1)S(1)}, u32[]{:S(2)}, u32[]{:S(2)}) async-start(bf16[16,16,128]{2,1,0:T(8,128)(2,1)} %shard_map.63), calls=%async_computation.1 | async-start | bytes 131072 | tf_op jit(solution)/shard_map/all_to_all | solution.py:370
  72.5 3.3 %collective-permute-start.10 = (bf16[4,64,128]{2,1,0:T(8,128)(2,1)S(1)}, bf16[4,64,128]{2,1,0:T(8,128)(2,1)S(1)}, u32[]{:S(2)}, u32[]{:S(2)}) collective-permute-start(bf16[4,64,128]{2,1,0:T(8,128)(2,1)S(1)} %get-tuple-element.51), channel_id=1, source_target_pairs={{0,1},{1,0},{2,3},{3,2},{4,5},{5,4},{6,7},{7,6},{8,9},{9,8},{10,11... | collective-permute-start | bytes 196616 | tf_op jit(solution)/shard_map/ppermute | solution.py:377
  76.4 1.3 %collective-permute-done.10.near_ref = bf16[4,64,128]{2,1,0:T(8,128)(2,1)S(1)} collective-permute-done((bf16[4,64,128]{2,1,0:T(8,128)(2,1)S(1)}, bf16[4,64,128]{2,1,0:T(8,128)(2,1)S(1)}, u32[]{:S(2)}, u32[]{:S(2)}) %collective-permute-start.10) | collective-permute-done | bytes 65568 | tf_op jit(solution)/shard_map/ppermute | solution.py:377
  77.7 1.3 %shard_map.65 = bf16[2,2,64,128]{3,2,1,0:T(8,128)(2,1)} custom-call(bf16[4,2,64,128]{3,2,1,0:T(8,128)(2,1)S(1)} %get-tuple-element.49.src_ref, bf16[4,64,128]{2,1,0:T(8,128)(2,1)S(1)} %collective-permute-done.8.far_ref, bf16[2,64,128]{2,1,0:T(8,128)(2,1)S(1)} %collective-permute-done.9.corner_ref, bf16[4,64,128]{2,1,0:T(8,128)(2,1)S(1)} %collective-permute-done.10.near_ref, ...), custom_call_target="tpu_custom_call" | custom-call | flops 1600000000 | tf_op jit(solution)/shard_map/pallas_call | solution.py:307
  79.0 5.0 %all-to-all-done.1.got_ref = bf16[16,16,128]{2,1,0:T(8,128)(2,1)S(1)} async-done(((bf16[16,16,128]{2,1,0:T(8,128)(2,1)}), bf16[16,16,128]{2,1,0:T(8,128)(2,1)S(1)}, u32[]{:S(2)}, u32[]{:S(2)}) %all-to-all-start.1) | async-done | bytes 65568 | tf_op jit(solution)/shard_map/all_to_all | solution.py:370
  84.0 5.9 %collective-permute-start.11 = (f32[8,128]{1,0:T(8,128)S(1)}, f32[8,128]{1,0:T(8,128)S(1)}, u32[]{:S(2)}, u32[]{:S(2)}) collective-permute-start(f32[8,128]{1,0:T(8,128)S(1)} %get-tuple-element.55), channel_id=1, source_target_pairs={{0,32},{32,0},{1,33},{33,1},{2,34},{34,2},{3,35},{35,3},{4,36},{36... | collective-permute-start | bytes 12296 | tf_op jit(solution)/shard_map/ppermute | solution.py:391
  90.0 0.8 collective-permute-done.11.refs_1_
  (20 shorter events, 3.4 us)
Async XLA Ops:
  0.6 19.0 %copy-start = (bf16[3,3,3,128,128]{4,3,2,1,0:T(8,128)(2,1)S(1)}, bf16[3,3,3,128,128]{4,3,2,1,0:T(8,128)(2,1)}, u32[]{:S(2)}) copy-start(bf16[3,3,3,128,128]{4,3,2,1,0:T(8,128)(2,1)} %param.5) | copy-start | bytes 2654212
  10.0 5.6 %collective-permute-start = (bf16[2,2,64,128]{3,2,1,0:T(8,128)(2,1)S(1)}, bf16[2,2,64,128]{3,2,1,0:T(8,128)(2,1)S(1)}, u32[]{:S(2)}, u32[]{:S(2)}) collective-permute-start(bf16[2,2,64,128]{3,2,1,0:T(8,128)(2,1)S(1)} %get-tuple-element.32), channel_id=1, source_target_pairs={{32,64},{64,32},{96,128},{128,96},{160,192},{192,160},{288,320},{3... | collective-permute-start | bytes 196616 | tf_op jit(solution)/shard_map/ppermute | solution.py:333
  12.0 5.0 %collective-permute-start.1 = (bf16[2,2,64,128]{3,2,1,0:T(8,128)(2,1)S(1)}, bf16[2,2,64,128]{3,2,1,0:T(8,128)(2,1)S(1)}, u32[]{:S(2)}, u32[]{:S(2)}) collective-permute-start(bf16[2,2,64,128]{3,2,1,0:T(8,128)(2,1)S(1)} %get-tuple-element.32), channel_id=1, source_target_pairs={{224,256},{256,224},{225,257},{257,225},{226,258},{258,226},{227,2... | collective-permute-start | bytes 196616 | tf_op jit(solution)/shard_map/ppermute | solution.py:332
  15.6 1.4 %collective-permute-start.2 = (bf16[2,64,128]{2,1,0:T(8,128)(2,1)S(1)}, bf16[2,64,128]{2,1,0:T(8,128)(2,1)S(1)}, u32[]{:S(2)}, u32[]{:S(2)}) collective-permute-start(bf16[2,64,128]{2,1,0:T(8,128)(2,1)S(1)} %get-tuple-element.33), channel_id=1, source_target_pairs={{199,296},{207,304},{215,312},{200,295},{208,303},{216,311},{295,2... | collective-permute-start | bytes 98312 | tf_op jit(solution)/shard_map/ppermute | solution.py:340
  16.3 4.6 %collective-permute-start.3 = (bf16[6,64,128]{2,1,0:T(8,128)(2,1)S(1)}, bf16[6,64,128]{2,1,0:T(8,128)(2,1)S(1)}, u32[]{:S(2)}, u32[]{:S(2)}) collective-permute-start(bf16[6,64,128]{2,1,0:T(8,128)(2,1)S(1)} %get-tuple-element.35), channel_id=1, source_target_pairs={{1,2},{3,4},{5,6},{7,8},{9,10},{11,12},{13,14},{15,16},{17,18},{19... | collective-permute-start | bytes 294920 | tf_op jit(solution)/shard_map/ppermute | solution.py:339
  17.1 3.9 %collective-permute-start.5 = (bf16[2,64,128]{2,1,0:T(8,128)(2,1)S(1)}, bf16[2,64,128]{2,1,0:T(8,128)(2,1)S(1)}, u32[]{:S(2)}, u32[]{:S(2)}) collective-permute-start(bf16[2,64,128]{2,1,0:T(8,128)(2,1)S(1)} %get-tuple-element.39), channel_id=1, source_target_pairs={{225,226},{227,228},{229,230},{233,234},{235,236},{237,238},{241,2... | collective-permute-start | bytes 98312 | tf_op jit(solution)/shard_map/ppermute | solution.py:349
  17.7 5.6 %collective-permute-start.4 = (bf16[6,64,128]{2,1,0:T(8,128)(2,1)S(1)}, bf16[6,64,128]{2,1,0:T(8,128)(2,1)S(1)}, u32[]{:S(2)}, u32[]{:S(2)}) collective-permute-start(bf16[6,64,128]{2,1,0:T(8,128)(2,1)S(1)} %get-tuple-element.38), channel_id=1, source_target_pairs={{0,1},{1,0},{2,3},{3,2},{4,5},{5,4},{6,7},{7,6},{8,9},{9,8},{10,11... | collective-permute-start | bytes 294920 | tf_op jit(solution)/shard_map/ppermute | solution.py:348
  25.2 3.4 %collective-permute-start.6 = (f32[512,128]{1,0:T(8,128)S(1)}, f32[512,128]{1,0:T(8,128)S(1)}, u32[]{:S(2)}, u32[]{:S(2)}) collective-permute-start(f32[512,128]{1,0:T(8,128)S(1)} %get-tuple-element.41.own_ref), channel_id=1, source_target_pairs={{0,32},{32,0},{1,33},{33,1},{2,34},{34,2},{3,35},{35,3},{4,36},{36... | collective-permute-start | bytes 786440 | tf_op jit(solution)/shard_map/ppermute | solution.py:356
  31.2 46.5 %copy-start.1 = (bf16[2,2,64,128]{3,2,1,0:T(8,128)(2,1)S(1)}, bf16[2,2,64,128]{3,2,1,0:T(8,128)(2,1)}, u32[]{:S(2)}) copy-start(bf16[2,2,64,128]{3,2,1,0:T(8,128)(2,1)} %cot_ref.1) | copy-start | bytes 196612
  31.2 32.7 %all-to-all-start = ((bf16[16,224,128]{2,1,0:T(8,128)(2,1)}), bf16[16,224,128]{2,1,0:T(8,128)(2,1)S(1)}, u32[]{:S(2)}, u32[]{:S(2)}) async-start(bf16[16,224,128]{2,1,0:T(8,128)(2,1)} %get-tuple-element.43), calls=%async_computation | async-start | bytes 1835008 | tf_op jit(solution)/shard_map/all_to_all | solution.py:366
  52.1 20.3 %collective-permute-start.7 = (bf16[2,2,64,128]{3,2,1,0:T(8,128)(2,1)S(1)}, bf16[2,2,64,128]{3,2,1,0:T(8,128)(2,1)S(1)}, u32[]{:S(2)}, u32[]{:S(2)}) collective-permute-start(bf16[2,2,64,128]{3,2,1,0:T(8,128)(2,1)S(1)} %get-tuple-element.45), channel_id=1, source_target_pairs={{64,32},{65,33},{66,34},{67,35},{68,36},{69,37},{70,38},{71,39},{7... | collective-permute-start | bytes 196616 | tf_op jit(solution)/shard_map/ppermute | solution.py:367
  53.4 19.0 %collective-permute-start.8 = (bf16[4,64,128]{2,1,0:T(8,128)(2,1)S(1)}, bf16[4,64,128]{2,1,0:T(8,128)(2,1)S(1)}, u32[]{:S(2)}, u32[]{:S(2)}) collective-permute-start(bf16[4,64,128]{2,1,0:T(8,128)(2,1)S(1)} %get-tuple-element.46), channel_id=1, source_target_pairs={{1,2},{3,4},{5,6},{7,8},{9,10},{11,12},{13,14},{15,16},{17,18},{19... | collective-permute-start | bytes 196616 | tf_op jit(solution)/shard_map/ppermute | solution.py:368
  64.8 19.2 %all-to-all-start.1 = ((bf16[16,16,128]{2,1,0:T(8,128)(2,1)}), bf16[16,16,128]{2,1,0:T(8,128)(2,1)S(1)}, u32[]{:S(2)}, u32[]{:S(2)}) async-start(bf16[16,16,128]{2,1,0:T(8,128)(2,1)} %shard_map.63), calls=%async_computation.1 | async-start | bytes 131072 | tf_op jit(solution)/shard_map/all_to_all | solution.py:370
  72.5 5.2 %collective-permute-start.10 = (bf16[4,64,128]{2,1,0:T(8,128)(2,1)S(1)}, bf16[4,64,128]{2,1,0:T(8,128)(2,1)S(1)}, u32[]{:S(2)}, u32[]{:S(2)}) collective-permute-start(bf16[4,64,128]{2,1,0:T(8,128)(2,1)S(1)} %get-tuple-element.51), channel_id=1, source_target_pairs={{0,1},{1,0},{2,3},{3,2},{4,5},{5,4},{6,7},{7,6},{8,9},{9,8},{10,11... | collective-permute-start | bytes 196616 | tf_op jit(solution)/shard_map/ppermute | solution.py:377
  75.8 0.7 collective-permute-start.9
  84.0 6.8 %collective-permute-start.11 = (f32[8,128]{1,0:T(8,128)S(1)}, f32[8,128]{1,0:T(8,128)S(1)}, u32[]{:S(2)}, u32[]{:S(2)}) collective-permute-start(f32[8,128]{1,0:T(8,128)S(1)} %get-tuple-element.55), channel_id=1, source_target_pairs={{0,32},{32,0},{1,33},{33,1},{2,34},{34,2},{3,35},{35,3},{4,36},{36... | collective-permute-start | bytes 12296 | tf_op jit(solution)/shard_map/ppermute | solution.py:391

commit v6 on v5

--- a/solution.py
+++ b/solution.py
@@ -13,7 +13,6 @@
 VMEM = pl.BlockSpec(memory_space=pltpu.VMEM)
 
 
-SWAP = [(0, 1), (1, 0)]
 NEAR_ROWS = [(r, r ^ 1) for r in range(32)]
 FAR_ROWS = [(r, r + 1) for r in range(1, 31, 2)] + [(r + 1, r) for r in range(1, 31, 2)]
 ENDS = [(r, q) for r, q in FAR_ROWS if r // 8 != q // 8]
@@ -21,7 +20,10 @@
 ENDS_OF = [r for r, _ in ENDS]
 
 
-PLANES = [list(range(15, -1, -1)), list(range(16, 32))]
+PLANES = [list(range(12, 16)) + list(range(12)), list(range(16, 32))]
+
+
+LINES = [[(12 - z) % 16 for z in range(16)]]
 
 
 def device(chip, core, slab):
@@ -200,11 +202,10 @@
     out_ref[...] = (cot + sum_ref[...]).astype(jnp.bfloat16).reshape(out_ref.shape)
 
 
-def grads_kernel(own_ref, other_ref, triples_ref, send_ref, act_ref, edge_ref, before_ref, terms_ref):
+def grads_kernel(both_ref, triples_ref, send_ref, act_ref, edge_ref, before_ref, terms_ref):
     core, _, _, odd = place()
-    own, other = own_ref[...], other_ref[...]
-    pre_act = jnp.where(core == 0, own, other).astype(jnp.bfloat16).astype(jnp.float32)
-    back_grad = jnp.where(core == 0, other, own)
+    pre_act = both_ref[0:512, :].astype(jnp.bfloat16).astype(jnp.float32)
+    back_grad = both_ref[512:1024, :]
     sig = 1.0 / (1.0 + jnp.exp(-pre_act))
     act_grad = (back_grad * (sig * (1.0 + pre_act * (1.0 - sig)))).astype(jnp.bfloat16)
     hidden = (pre_act * sig).astype(jnp.bfloat16)
@@ -255,7 +256,7 @@
                     blocks.append(terms_ref[start : start + 54, :])
             blocks.append(jnp.zeros((8, 128), jnp.float32))
             rank = y * 4 + x
-            rank = jnp.where(lax.axis_index("zh") == 0, 15 - rank, rank)
+            rank = jnp.where(lax.axis_index("zh") == 0, (rank + 4) % 16, rank)
             send_ref[rank] = jnp.concatenate(blocks, axis=0).astype(jnp.bfloat16)
 
 
@@ -280,26 +281,23 @@
                         pltpu.roll(after, 128 - shift, 1),
                     )
                 pieces.append(piece)
-            send_ref[zh * 8 + zl] = jnp.concatenate(pieces, axis=0).astype(jnp.bfloat16)
-
-
-def line_sum_kernel(got_ref, own_ref, send_ref):
-    core = lax.axis_index("c")
+            send_ref[LINES[0].index(zh * 8 + zl)] = jnp.concatenate(pieces, axis=0).astype(jnp.bfloat16)
+
+
+def line_sum_kernel(got_ref, sum_ref):
     total = got_ref[0].astype(jnp.float32)
     for k in range(1, 16):
         total = total + got_ref[k].astype(jnp.float32)
-    own_ref[...] = jnp.where(core == 0, total[0:8], total[8:16])
-    send_ref[...] = jnp.where(core == 0, total[8:16], total[0:8])
-
-
-def place_kernel(scale, own_ref, other_ref, out_ref):
-    core = lax.axis_index("c")
-    own, other = own_ref[...] * scale, other_ref[...] * scale
-    shares = (jnp.where(core == 0, own, other), jnp.where(core == 0, other, own))
+    sum_ref[...] = total
+
+
+def place_kernel(scale, shares_ref, out_ref):
     for k in range(2):
+        start = pl.multiple_of(16 * k + 8 * lax.axis_index("c"), 8)
+        share = shares_ref[pl.ds(start, 8), :] * scale
         for r in range(7):
             width = min(128, 864 - 128 * r)
-            out_ref[k : k + 1, 128 * r : 128 * r + width] = shares[k][r : r + 1, :width]
+            out_ref[k : k + 1, 128 * r : 128 * r + width] = share[r : r + 1, :width]
 
 
 def call(kernel, out_shape, *args, scratch=(), flops=0):
@@ -353,21 +351,21 @@
         source, far, near, corner, kernel,
         scratch=[pltpu.VMEM((6, 64, 128), bf16)],
     )
-    other = lax.ppermute(own, "c", SWAP)
+    both = lax.all_gather(own, "c", tiled=True)
     send, act_grad, edge, before = call(
         grads_kernel,
         (
             shaped((16, 224, 128), bf16), shaped((4, 2, 64, 128), bf16),
             shaped((4, 64, 128), bf16), shaped((2, 2, 64, 128), bf16),
         ),
-        own, other, triples,
+        both, triples,
         scratch=[pltpu.VMEM((3456, 128), f32)],
     )
     got = lax.all_to_all(send, ("zh", "y", "x"), 0, 0, axis_index_groups=PLANES, tiled=True)
     before = lax.ppermute(before, everywhere, BEFORE)
     far = lax.ppermute(edge, ROWS, FAR_ROWS)
     send = call(plane_sum_kernel, shaped((16, 16, 128), bf16), got, scratch=[pltpu.VMEM((224, 128), f32)])
-    got = lax.all_to_all(send, ("zh", "zl"), 0, 0, tiled=True)
+    got = lax.all_to_all(send, ("zh", "zl"), 0, 0, axis_index_groups=LINES, tiled=True)
     _, before, far = lax.optimization_barrier((send, before, far))
     source, inner, corner = call(
         assemble_grad_kernel,
@@ -387,11 +385,9 @@
     )
     got, input_grad = lax.optimization_barrier((got, input_grad))
     scale = 1.0 / math.sqrt(131072)
-    own_share, send_share = call(line_sum_kernel, (shaped((8, 128), f32),) * 2, got)
-    other_share = lax.ppermute(send_share, "c", SWAP)
-    weight_grads = call(
-        lambda *refs: place_kernel(scale, *refs), shaped((2, 864), f32), own_share, other_share
-    )
+    shares = call(line_sum_kernel, shaped((16, 128), f32), got)
+    shares = lax.all_gather(shares, "c", tiled=True)
+    weight_grads = call(lambda *refs: place_kernel(scale, *refs), shaped((2, 864), f32), shares)
     return input_grad, weight_grads
 
 

time: 92 us -> 85.9 us (0.934)
  starting transfers between devices: 48.8 us -> 41 us
  blocking collectives: 8.43 us -> 15.8 us
  waiting for transfers between devices: 23.8 us -> 18.2 us
    ppermute x2 -> x0, starting transfers between devices: 7.86 us -> none  [the longest x1 5.94 us: per_device(): other_share = lax.ppermute(send_share, 'c', SWAP)]
    all_gather x0 -> x2, blocking collectives: none -> 7.37 us  [the longest x1 5.19 us: per_device(): shares = lax.all_gather(shares, 'c', tiled=True)]
    all_to_all x1, waiting for transfers between devices: 4.98 us -> 0.9 us  [per_device(): lax.all_to_all(send, ('zh', 'zl'), 0, 0, axis_index_groups=LINES, tiled=T...]
    ppermute x2 -> x0, waiting for transfers between devices: 2.3 us -> none  [the longest x1 1.5 us: per_device(): other = lax.ppermute(own, 'c', SWAP)]
    all_to_all x1, starting transfers between devices: 7.62 us -> 9.21 us  [per_device(): lax.all_to_all(send, ('zh', 'zl'), 0, 0, axis_index_groups=LINES, tiled=T...]
    all_to_all x1, starting transfers between devices: 20.9 us -> 19.6 us  [per_device(): lax.all_to_all(send, ('zh', 'y', 'x'), 0, 0, axis_index_groups=PLANES, ti...]
  transfers between devices with their start and end apart: 14 -> 12, of which waited for: 7 -> 5; matrix products, arithmetic and copies ran while one was open for 1% -> 1% of each run, Pallas kernels for 2% -> 3%
where the time goes in v6:
time: 85.9 us; the launch traced here: 85.3 us
  starting transfers between devices  41 us (48%)
  waiting for transfers between devices  18.2 us (21%)
  blocking collectives  15.8 us (18%)
  Pallas kernels  7.22 us (8%)
  other arithmetic  2.23 us (3%)
    all_to_all x1, starting transfers between devices, per_device(): lax.all_to_all(send, ('zh', 'y', 'x'), 0, 0, axis_index_groups=PLANES, ti...  19.6 us
    all_to_all x1, waiting for transfers between devices, per_device(): lax.all_to_all(send, ('zh', 'y', 'x'), 0, 0, axis_index_groups=PLANES, ti...  10.3 us
    all_to_all x1, starting transfers between devices, per_device(): lax.all_to_all(send, ('zh', 'zl'), 0, 0, axis_index_groups=LINES, tiled=T...  9.21 us
    all_gather x1, blocking collectives, per_device(): both = lax.all_gather(given, 'c', tiled=True)  8.43 us
    pallas_call x9, Pallas kernels, call(): pl.pallas_call(kernel, out_shape=out_shape, in_specs=[VMEM] * len(args),...  7.22 us
    all_gather x1, blocking collectives, per_device(): shares = lax.all_gather(shares, 'c', tiled=True)  5.19 us
    ppermute x2, starting transfers between devices, per_device(): near = lax.ppermute(inner, ROWS, NEAR_ROWS)  5 us
    ppermute x2, waiting for transfers between devices, per_device(): near = lax.ppermute(inner, ROWS, NEAR_ROWS)  4.01 us
  transfers between devices with their start and end apart: 12, of which 5 were waited for; matrix products, arithmetic and copies ran while one was open for 1% of the time, Pallas kernels for 3%

profile of v6, /device:TPU:1, one launch (start us, length us, event | category | flops | bytes accessed | tf_op | source)
XLA Modules:
  0.0 85.3 jit_solution(10840577754566770554)
XLA Ops:
  0.6 1.0 %broadcast_select_fusion.1 = (bf16[2,2,64,128]{3,2,1,0:T(8,128)(2,1)S(1)}, bf16[2,2,64,128]{3,2,1,0:T(8,128)(2,1)S(1)}) fusion(bf16[2,2,64,128]{3,2,1,0:T(8,128)(2,1)} %param.4, bf16[2,2,64,128]{3,2,1,0:T(8,128)(2,1)} %cot_ref.1, pred[]{:T(512)S(6)} %eq.2), kind=kLoop, calls=%fused_computation.1 | loop fusion | flops 65536 | bytes 262145 | tf_op jit(solution)/shard_map/jit(_where)/select_n | solution.py:326
  1.6 8.4 %all_gather.9.both_ref = bf16[4,2,64,128]{3,2,1,0:T(8,128)(2,1)S(1)} all-gather(bf16[2,2,64,128]{3,2,1,0:T(8,128)(2,1)S(1)} %get-tuple-element.30), channel_id=1, replica_groups=mesh['zh'=2,'y'=4,'c'=2,'x'=4,'zl'=8] {'c'}, dimensions={0}, use_global_device_ids=true | all-gather | bytes 196608 | tf_op jit(solution)/shard_map/all_gather | solution.py:328
  10.0 1.9 %collective-permute-start = (bf16[2,2,64,128]{3,2,1,0:T(8,128)(2,1)S(1)}, bf16[2,2,64,128]{3,2,1,0:T(8,128)(2,1)S(1)}, u32[]{:S(2)}, u32[]{:S(2)}) collective-permute-start(bf16[2,2,64,128]{3,2,1,0:T(8,128)(2,1)S(1)} %get-tuple-element.30), channel_id=1, source_target_pairs={{32,64},{64,32},{96,128},{128,96},{160,192},{192,160},{288,320},{3... | collective-permute-start | bytes 196616 | tf_op jit(solution)/shard_map/ppermute | solution.py:331
  12.0 0.7 collective-permute-start.1
  12.6 3.0 %collective-permute-done.beyond_ref = bf16[2,2,64,128]{3,2,1,0:T(8,128)(2,1)S(1)} collective-permute-done((bf16[2,2,64,128]{3,2,1,0:T(8,128)(2,1)S(1)}, bf16[2,2,64,128]{3,2,1,0:T(8,128)(2,1)S(1)}, u32[]{:S(2)}, u32[]{:S(2)}) %collective-permute-start) | collective-permute-done | bytes 65568 | tf_op jit(solution)/shard_map/ppermute | solution.py:331
  15.6 0.7 collective-permute-start.2
  16.3 0.7 collective-permute-start.3
  17.7 1.9 %collective-permute-start.4 = (bf16[6,64,128]{2,1,0:T(8,128)(2,1)S(1)}, bf16[6,64,128]{2,1,0:T(8,128)(2,1)S(1)}, u32[]{:S(2)}, u32[]{:S(2)}) collective-permute-start(bf16[6,64,128]{2,1,0:T(8,128)(2,1)S(1)} %get-tuple-element.36), channel_id=1, source_target_pairs={{0,1},{1,0},{2,3},{3,2},{4,5},{5,4},{6,7},{7,6},{8,9},{9,8},{10,11... | collective-permute-start | bytes 294920 | tf_op jit(solution)/shard_map/ppermute | solution.py:346
  19.7 1.3 %broadcast_select_fusion.kernel_ref = bf16[3456,128]{1,0:T(8,128)(2,1)S(1)} fusion(bf16[3456,128]{1,0:T(8,128)(2,1)} %bitcast.4, pred[]{:T(512)S(6)} %eq.2, bf16[3,3,3,128,128]{4,3,2,1,0:T(8,128)(2,1)S(1)} %copy-done), kind=kLoop, calls=%fused_computation | loop fusion | flops 442368 | bytes 2654209 | tf_op jit(solution)/shard_map/jit(_where)/select_n | solution.py:345
  21.0 2.4 %collective-permute-done.4.near_ref = bf16[6,64,128]{2,1,0:T(8,128)(2,1)S(1)} collective-permute-done((bf16[6,64,128]{2,1,0:T(8,128)(2,1)S(1)}, bf16[6,64,128]{2,1,0:T(8,128)(2,1)S(1)}, u32[]{:S(2)}, u32[]{:S(2)}) %collective-permute-start.4) | collective-permute-done | bytes 98336 | tf_op jit(solution)/shard_map/ppermute | solution.py:346
  23.3 1.8 %shard_map.61 = (f32[512,128]{1,0:T(8,128)S(1)}, bf16[6,4,64,384]{3,2,1,0:T(8,128)(2,1)S(1)}) custom-call(bf16[6,2,64,128]{3,2,1,0:T(8,128)(2,1)S(1)} %get-tuple-element.32.src_ref, bf16[6,64,128]{2,1,0:T(8,128)(2,1)S(1)} %collective-permute-done.3.far_ref, bf16[6,64,128]{2,1,0:T(8,128)(2,1)S(1)} %collective-permute-done.4.near_ref, ...), custom_call_target="tpu_custom_call" | custom-call | tf_op jit(solution)/shard_map/pallas_call | solution.py:305
  25.2 2.2 %all_gather.10.both_ref = f32[1024,128]{1,0:T(8,128)S(1)} all-gather(f32[512,128]{1,0:T(8,128)S(1)} %get-tuple-element.39), channel_id=1, replica_groups=mesh['zh'=2,'y'=4,'c'=2,'x'=4,'zl'=8] {'c'}, dimensions={0}, use_global_device_ids=true | all-gather | bytes 786432 | tf_op jit(solution)/shard_map/all_gather | solution.py:354
  27.4 2.5 %shard_map.62 = (bf16[16,224,128]{2,1,0:T(8,128)(2,1)}, bf16[4,2,64,128]{3,2,1,0:T(8,128)(2,1)S(1)}, bf16[4,64,128]{2,1,0:T(8,128)(2,1)S(1)}, bf16[2,2,64,128]{3,2,1,0:T(8,128)(2,1)S(1)}) custom-call(f32[1024,128]{1,0:T(8,128)S(1)} %all_gather.10.both_ref, bf16[6,4,64,384]{3,2,1,0:T(8,128)(2,1)S(1)} %get-tuple-element.40.triples_ref), custom_call_target="tpu_custom_call" | custom-call | tf_op jit(solution)/shard_map/pallas_call | solution.py:305
  29.9 19.6 %all-to-all-start = ((bf16[16,224,128]{2,1,0:T(8,128)(2,1)}), bf16[16,224,128]{2,1,0:T(8,128)(2,1)S(1)}, u32[]{:S(2)}, u32[]{:S(2)}) async-start(bf16[16,224,128]{2,1,0:T(8,128)(2,1)} %get-tuple-element.41), calls=%async_computation | async-start | bytes 1835008 | tf_op jit(solution)/shard_map/all_to_all | solution.py:364
  49.4 1.3 %collective-permute-start.6 = (bf16[2,2,64,128]{3,2,1,0:T(8,128)(2,1)S(1)}, bf16[2,2,64,128]{3,2,1,0:T(8,128)(2,1)S(1)}, u32[]{:S(2)}, u32[]{:S(2)}) collective-permute-start(bf16[2,2,64,128]{3,2,1,0:T(8,128)(2,1)S(1)} %get-tuple-element.43), channel_id=1, source_target_pairs={{64,32},{65,33},{66,34},{67,35},{68,36},{69,37},{70,38},{71,39},{7... | collective-permute-start | bytes 196616 | tf_op jit(solution)/shard_map/ppermute | solution.py:365
  50.7 0.7 collective-permute-start.7
  51.4 10.3 %all-to-all-done.got_ref = bf16[16,224,128]{2,1,0:T(8,128)(2,1)S(1)} async-done(((bf16[16,224,128]{2,1,0:T(8,128)(2,1)}), bf16[16,224,128]{2,1,0:T(8,128)(2,1)S(1)}, u32[]{:S(2)}, u32[]{:S(2)}) %all-to-all-start) | async-done | bytes 917536 | tf_op jit(solution)/shard_map/all_to_all | solution.py:364
  61.7 0.9 %shard_map.63 = bf16[16,16,128]{2,1,0:T(8,128)(2,1)} custom-call(bf16[16,224,128]{2,1,0:T(8,128)(2,1)S(1)} %all-to-all-done.got_ref), custom_call_target="tpu_custom_call" | custom-call | tf_op jit(solution)/shard_map/pallas_call | solution.py:305
  62.6 9.2 %all-to-all-start.1 = ((bf16[16,16,128]{2,1,0:T(8,128)(2,1)}), bf16[16,16,128]{2,1,0:T(8,128)(2,1)S(1)}, u32[]{:S(2)}, u32[]{:S(2)}) async-start(bf16[16,16,128]{2,1,0:T(8,128)(2,1)} %shard_map.63), calls=%async_computation.1 | async-start | bytes 131072 | tf_op jit(solution)/shard_map/all_to_all | solution.py:368
  71.9 3.1 %collective-permute-start.9 = (bf16[4,64,128]{2,1,0:T(8,128)(2,1)S(1)}, bf16[4,64,128]{2,1,0:T(8,128)(2,1)S(1)}, u32[]{:S(2)}, u32[]{:S(2)}) collective-permute-start(bf16[4,64,128]{2,1,0:T(8,128)(2,1)S(1)} %get-tuple-element.49), channel_id=1, source_target_pairs={{0,1},{1,0},{2,3},{3,2},{4,5},{5,4},{6,7},{7,6},{8,9},{9,8},{10,11... | collective-permute-start | bytes 196616 | tf_op jit(solution)/shard_map/ppermute | solution.py:375
  75.6 1.6 %collective-permute-done.9.near_ref = bf16[4,64,128]{2,1,0:T(8,128)(2,1)S(1)} collective-permute-done((bf16[4,64,128]{2,1,0:T(8,128)(2,1)S(1)}, bf16[4,64,128]{2,1,0:T(8,128)(2,1)S(1)}, u32[]{:S(2)}, u32[]{:S(2)}) %collective-permute-start.9) | collective-permute-done | bytes 65568 | tf_op jit(solution)/shard_map/ppermute | solution.py:375
  77.3 1.3 %shard_map.65 = bf16[2,2,64,128]{3,2,1,0:T(8,128)(2,1)} custom-call(bf16[4,2,64,128]{3,2,1,0:T(8,128)(2,1)S(1)} %get-tuple-element.47.src_ref, bf16[4,64,128]{2,1,0:T(8,128)(2,1)S(1)} %collective-permute-done.7.far_ref, bf16[2,64,128]{2,1,0:T(8,128)(2,1)S(1)} %collective-permute-done.8.corner_ref, bf16[4,64,128]{2,1,0:T(8,128)(2,1)S(1)} %collective-permute-done.9.near_ref, ...), custom_call_target="tpu_custom_call" | custom-call | flops 1600000000 | tf_op jit(solution)/shard_map/pallas_call | solution.py:305
  78.6 0.9 %all-to-all-done.1.got_ref = bf16[16,16,128]{2,1,0:T(8,128)(2,1)S(1)} async-done(((bf16[16,16,128]{2,1,0:T(8,128)(2,1)}), bf16[16,16,128]{2,1,0:T(8,128)(2,1)S(1)}, u32[]{:S(2)}, u32[]{:S(2)}) %all-to-all-start.1) | async-done | bytes 65568 | tf_op jit(solution)/shard_map/all_to_all | solution.py:368
  79.5 5.2 %all_gather.11.refs_0_ = f32[32,128]{1,0:T(8,128)S(1)} all-gather(f32[16,128]{1,0:T(8,128)S(1)} %shard_map.66), channel_id=1, replica_groups=mesh['zh'=2,'y'=4,'c'=2,'x'=4,'zl'=8] {'c'}, dimensions={0}, use_global_device_ids=true | all-gather | bytes 24576 | tf_op jit(solution)/shard_map/all_gather | solution.py:389
  (18 shorter events, 2.1 us)
Async XLA Ops:
  0.6 19.0 %copy-start = (bf16[3,3,3,128,128]{4,3,2,1,0:T(8,128)(2,1)S(1)}, bf16[3,3,3,128,128]{4,3,2,1,0:T(8,128)(2,1)}, u32[]{:S(2)}) copy-start(bf16[3,3,3,128,128]{4,3,2,1,0:T(8,128)(2,1)} %param.5) | copy-start | bytes 2654212
  10.0 5.6 %collective-permute-start = (bf16[2,2,64,128]{3,2,1,0:T(8,128)(2,1)S(1)}, bf16[2,2,64,128]{3,2,1,0:T(8,128)(2,1)S(1)}, u32[]{:S(2)}, u32[]{:S(2)}) collective-permute-start(bf16[2,2,64,128]{3,2,1,0:T(8,128)(2,1)S(1)} %get-tuple-element.30), channel_id=1, source_target_pairs={{32,64},{64,32},{96,128},{128,96},{160,192},{192,160},{288,320},{3... | collective-permute-start | bytes 196616 | tf_op jit(solution)/shard_map/ppermute | solution.py:331
  12.0 5.0 %collective-permute-start.1 = (bf16[2,2,64,128]{3,2,1,0:T(8,128)(2,1)S(1)}, bf16[2,2,64,128]{3,2,1,0:T(8,128)(2,1)S(1)}, u32[]{:S(2)}, u32[]{:S(2)}) collective-permute-start(bf16[2,2,64,128]{3,2,1,0:T(8,128)(2,1)S(1)} %get-tuple-element.30), channel_id=1, source_target_pairs={{224,256},{256,224},{225,257},{257,225},{226,258},{258,226},{227,2... | collective-permute-start | bytes 196616 | tf_op jit(solution)/shard_map/ppermute | solution.py:330
  15.6 1.4 %collective-permute-start.2 = (bf16[2,64,128]{2,1,0:T(8,128)(2,1)S(1)}, bf16[2,64,128]{2,1,0:T(8,128)(2,1)S(1)}, u32[]{:S(2)}, u32[]{:S(2)}) collective-permute-start(bf16[2,64,128]{2,1,0:T(8,128)(2,1)S(1)} %get-tuple-element.31), channel_id=1, source_target_pairs={{199,296},{207,304},{215,312},{200,295},{208,303},{216,311},{295,2... | collective-permute-start | bytes 98312 | tf_op jit(solution)/shard_map/ppermute | solution.py:338
  16.3 4.6 %collective-permute-start.3 = (bf16[6,64,128]{2,1,0:T(8,128)(2,1)S(1)}, bf16[6,64,128]{2,1,0:T(8,128)(2,1)S(1)}, u32[]{:S(2)}, u32[]{:S(2)}) collective-permute-start(bf16[6,64,128]{2,1,0:T(8,128)(2,1)S(1)} %get-tuple-element.33), channel_id=1, source_target_pairs={{1,2},{3,4},{5,6},{7,8},{9,10},{11,12},{13,14},{15,16},{17,18},{19... | collective-permute-start | bytes 294920 | tf_op jit(solution)/shard_map/ppermute | solution.py:337
  17.1 3.9 %collective-permute-start.5 = (bf16[2,64,128]{2,1,0:T(8,128)(2,1)S(1)}, bf16[2,64,128]{2,1,0:T(8,128)(2,1)S(1)}, u32[]{:S(2)}, u32[]{:S(2)}) collective-permute-start(bf16[2,64,128]{2,1,0:T(8,128)(2,1)S(1)} %get-tuple-element.37), channel_id=1, source_target_pairs={{225,226},{227,228},{229,230},{233,234},{235,236},{237,238},{241,2... | collective-permute-start | bytes 98312 | tf_op jit(solution)/shard_map/ppermute | solution.py:347
  17.7 5.6 %collective-permute-start.4 = (bf16[6,64,128]{2,1,0:T(8,128)(2,1)S(1)}, bf16[6,64,128]{2,1,0:T(8,128)(2,1)S(1)}, u32[]{:S(2)}, u32[]{:S(2)}) collective-permute-start(bf16[6,64,128]{2,1,0:T(8,128)(2,1)S(1)} %get-tuple-element.36), channel_id=1, source_target_pairs={{0,1},{1,0},{2,3},{3,2},{4,5},{5,4},{6,7},{7,6},{8,9},{9,8},{10,11... | collective-permute-start | bytes 294920 | tf_op jit(solution)/shard_map/ppermute | solution.py:346
  29.9 47.4 %copy-start.1 = (bf16[2,2,64,128]{3,2,1,0:T(8,128)(2,1)S(1)}, bf16[2,2,64,128]{3,2,1,0:T(8,128)(2,1)}, u32[]{:S(2)}) copy-start(bf16[2,2,64,128]{3,2,1,0:T(8,128)(2,1)} %cot_ref.1) | copy-start | bytes 196612
  29.9 31.9 %all-to-all-start = ((bf16[16,224,128]{2,1,0:T(8,128)(2,1)}), bf16[16,224,128]{2,1,0:T(8,128)(2,1)S(1)}, u32[]{:S(2)}, u32[]{:S(2)}) async-start(bf16[16,224,128]{2,1,0:T(8,128)(2,1)} %get-tuple-element.41), calls=%async_computation | async-start | bytes 1835008 | tf_op jit(solution)/shard_map/all_to_all | solution.py:364
  49.4 22.4 %collective-permute-start.6 = (bf16[2,2,64,128]{3,2,1,0:T(8,128)(2,1)S(1)}, bf16[2,2,64,128]{3,2,1,0:T(8,128)(2,1)S(1)}, u32[]{:S(2)}, u32[]{:S(2)}) collective-permute-start(bf16[2,2,64,128]{3,2,1,0:T(8,128)(2,1)S(1)} %get-tuple-element.43), channel_id=1, source_target_pairs={{64,32},{65,33},{66,34},{67,35},{68,36},{69,37},{70,38},{71,39},{7... | collective-permute-start | bytes 196616 | tf_op jit(solution)/shard_map/ppermute | solution.py:365
  50.7 21.1 %collective-permute-start.7 = (bf16[4,64,128]{2,1,0:T(8,128)(2,1)S(1)}, bf16[4,64,128]{2,1,0:T(8,128)(2,1)S(1)}, u32[]{:S(2)}, u32[]{:S(2)}) collective-permute-start(bf16[4,64,128]{2,1,0:T(8,128)(2,1)S(1)} %get-tuple-element.44), channel_id=1, source_target_pairs={{1,2},{3,4},{5,6},{7,8},{9,10},{11,12},{13,14},{15,16},{17,18},{19... | collective-permute-start | bytes 196616 | tf_op jit(solution)/shard_map/ppermute | solution.py:366
  62.6 16.9 %all-to-all-start.1 = ((bf16[16,16,128]{2,1,0:T(8,128)(2,1)}), bf16[16,16,128]{2,1,0:T(8,128)(2,1)S(1)}, u32[]{:S(2)}, u32[]{:S(2)}) async-start(bf16[16,16,128]{2,1,0:T(8,128)(2,1)} %shard_map.63), calls=%async_computation.1 | async-start | bytes 131072 | tf_op jit(solution)/shard_map/all_to_all | solution.py:368
  71.9 5.4 %collective-permute-start.9 = (bf16[4,64,128]{2,1,0:T(8,128)(2,1)S(1)}, bf16[4,64,128]{2,1,0:T(8,128)(2,1)S(1)}, u32[]{:S(2)}, u32[]{:S(2)}) collective-permute-start(bf16[4,64,128]{2,1,0:T(8,128)(2,1)S(1)} %get-tuple-element.49), channel_id=1, source_target_pairs={{0,1},{1,0},{2,3},{3,2},{4,5},{5,4},{6,7},{7,6},{8,9},{9,8},{10,11... | collective-permute-start | bytes 196616 | tf_op jit(solution)/shard_map/ppermute | solution.py:375
  75.0 0.7 collective-permute-start.8

commit v7 on v6

--- a/solution.py
+++ b/solution.py
@@ -20,7 +20,7 @@
 ENDS_OF = [r for r, _ in ENDS]
 
 
-PLANES = [list(range(12, 16)) + list(range(12)), list(range(16, 32))]
+PLANES = [[12, 13, 14, 15, 8, 9, 10, 11, 4, 5, 6, 7, 0, 1, 2, 3], [16 + i for i in [0, 1, 2, 3, 12, 13, 14, 15, 8, 9, 10, 11, 4, 5, 6, 7]]]
 
 
 LINES = [[(12 - z) % 16 for z in range(16)]]
@@ -60,23 +60,26 @@
     return lax.dot_general(lhs, rhs, (((0,), (0,)), ((), ())), preferred_element_type=jnp.float32)
 
 
-def fill_triples(src_ref, far_ref, near_ref, triples_ref, frames):
+def side_by_side(cells):
+    columns, chans = cells.shape
+    col = lax.broadcasted_iota(jnp.int32, (columns, chans), 0)
+    wide = cells.astype(jnp.float32)
+    before = jnp.where(col == 0, 0.0, pltpu.roll(wide, 1, 0)).astype(cells.dtype)
+    after = jnp.where(col == columns - 1, 0.0, pltpu.roll(wide, columns - 1, 0)).astype(cells.dtype)
+    return jnp.concatenate([before, cells, after], axis=1)
+
+
+def fill_inner(src_ref, triples_ref, frames):
+    for f in range(frames):
+        for r in range(2):
+            triples_ref[f, r + 1] = side_by_side(src_ref[f, r])
+
+
+def fill_outer(far_ref, near_ref, triples_ref, frames):
     odd = place()[3]
-    columns = src_ref.shape[2]
-    chans = src_ref.shape[3]
-    col = lax.broadcasted_iota(jnp.int32, (columns, chans), 0)
     for f in range(frames):
-        for r in range(4):
-            if r in (0, 3):
-                cells = jnp.where(odd == (r == 3), far_ref[f], near_ref[f])
-            else:
-                cells = src_ref[f, r - 1]
-            wide = cells.astype(jnp.float32)
-            before = jnp.where(col == 0, 0.0, pltpu.roll(wide, 1, 0))
-            after = jnp.where(col == columns - 1, 0.0, pltpu.roll(wide, columns - 1, 0))
-            triples_ref[f, r, :, 0:chans] = before.astype(cells.dtype)
-            triples_ref[f, r, :, chans : 2 * chans] = cells
-            triples_ref[f, r, :, 2 * chans : 3 * chans] = after.astype(cells.dtype)
+        triples_ref[f, 0] = side_by_side(jnp.where(odd == 0, far_ref[f], near_ref[f]))
+        triples_ref[f, 3] = side_by_side(jnp.where(odd == 1, far_ref[f], near_ref[f]))
 
 
 def stripe(triples_ref, f, count, b):
@@ -84,34 +87,50 @@
     return part.reshape(count * 2 * part.shape[2], part.shape[3])
 
 
-def conv(triples_ref, kernel_ref, frames):
-    total = None
+def turned(kernel_ref, a, b):
+    starts = [((2 - a) * 9 + (2 - b) * 3 + (2 - d)) * 128 for d in range(3)]
+    return jnp.concatenate([kernel_ref[start : start + 128, :] for start in starts], axis=1)
+
+
+def stage_taps(kernel_ref, taps_ref, back):
     for a in range(3):
         for b in range(3):
-            start = (a * 3 + b) * 384
-            term = jnp.dot(
-                stripe(triples_ref, a, frames, b),
-                kernel_ref[start : start + 384, :],
-                preferred_element_type=jnp.float32,
-            )
+            if back:
+                taps_ref[a * 3 + b] = turned(kernel_ref, a, b).T
+            else:
+                taps_ref[a * 3 + b] = kernel_ref[(a * 3 + b) * 384 : (a * 3 + b + 1) * 384, :]
+
+
+INNER = (((1, 1), (2, 2)), ((0, 1), (1, 2)))
+OUTER = (((0, 0),), ((2, 3),))
+TAPS = ((0, 0), (1, 1), (2, 2))
+FOLD = ((0, 2), (0, 1), (1, 2))
+
+
+def row_terms(triples_ref, taps_ref, frames, pairs, times):
+    total = None
+    for f, a in times:
+        for b, row in pairs:
+            part = triples_ref[f : f + frames, row].reshape(frames * 64, 384)
+            term = jnp.dot(part, taps_ref[a * 3 + b], preferred_element_type=jnp.float32)
             total = term if total is None else total + term
     return total
 
 
-def back_terms(triples_ref, kernel_ref, frames, taps):
-    total = None
-    for f, a in taps:
-        for b in range(3):
-            part = stripe(triples_ref, f, frames, b)
-            starts = [((2 - a) * 9 + (2 - b) * 3 + (2 - d)) * 128 for d in range(3)]
-            turned = jnp.concatenate([kernel_ref[start : start + 128, :] for start in starts], axis=1)
-            term = lax.dot_general(part, turned, (((1,), (1,)), ((), ())), preferred_element_type=jnp.float32)
-            total = term if total is None else total + term
-    return total
-
-
-TAPS = ((0, 0), (1, 1), (2, 2))
-FOLD = ((0, 2), (0, 1), (1, 2))
+def add_rows(triples_ref, taps_ref, sum_ref, frames, rows, fresh, fold):
+    for row in range(2):
+        term = row_terms(triples_ref, taps_ref, frames, rows[row], TAPS)
+        sum_ref[row] = term if fresh else sum_ref[row] + term
+
+    @pl.when(fold)
+    def _():
+        for row in range(2):
+            sum_ref[row, 0:64, :] += row_terms(triples_ref, taps_ref, 1, rows[row], FOLD)
+
+
+def interleaved(sum_ref, frames):
+    rows = [sum_ref[r, f * 64 : (f + 1) * 64, :] for f in range(frames) for r in range(2)]
+    return jnp.concatenate(rows, axis=0)
 
 
 def edge_kernel(mine_ref, both_ref, beyond_ref, edge_ref, corner_ref):
@@ -143,25 +162,31 @@
     corner_ref[...] = jnp.where(end, free_ref[...], beyond_far_ref[:, odd])
 
 
-def first_conv_kernel(
-    src_ref, far_ref, near_ref, corner_ref, kernel_ref, out_ref, triples_ref, outer_ref
+def first_inner_kernel(src_ref, kernel_ref, sum_ref, triples_ref, taps_ref):
+    core, chip, _, _ = place()
+    fill_inner(src_ref, triples_ref, 6)
+
+    @pl.when(core == 0)
+    def _():
+        stage_taps(kernel_ref, taps_ref, False)
+
+    @pl.when(core == 1)
+    def _():
+        stage_taps(kernel_ref, taps_ref, True)
+
+    add_rows(triples_ref, taps_ref, sum_ref, 4, INNER, True, (core == 1) & (chip == 0))
+
+
+def first_outer_kernel(
+    inner_ref, triples_in_ref, taps_ref, far_ref, near_ref, corner_ref, out_ref, triples_ref, outer_ref, sum_ref
 ):
     core, chip, _, _ = place()
     outer_ref[...] = far_ref[...]
     outer_ref[pl.ds(4 * core, 2)] += corner_ref[...]
-    fill_triples(src_ref, outer_ref, near_ref, triples_ref, 6)
-
-    @pl.when(core == 0)
-    def _():
-        out_ref[...] = conv(triples_ref, kernel_ref, 4)
-
-    @pl.when(core == 1)
-    def _():
-        out_ref[...] = back_terms(triples_ref, kernel_ref, 4, TAPS)
-
-    @pl.when((core == 1) & (chip == 0))
-    def _():
-        out_ref[0:128, :] += back_terms(triples_ref, kernel_ref, 1, FOLD)
+    fill_outer(outer_ref, near_ref, triples_ref, 6)
+    sum_ref[...] = inner_ref[...]
+    add_rows(triples_ref, taps_ref, sum_ref, 4, OUTER, False, (core == 1) & (chip == 0))
+    out_ref[...] = interleaved(sum_ref, 4)
 
 
 def assemble_grad_kernel(act_ref, before_ref, far_ref, src_ref, inner_ref, corner_ref):
@@ -181,8 +206,16 @@
     inner_ref[...] = src_ref[:, 1 - odd]
 
 
-def input_conv_kernel(
-    src_ref, far_ref, corner_ref, near_ref, kernel_ref, cot_ref, out_ref, outer_ref, triples_ref, sum_ref
+def input_inner_kernel(src_ref, kernel_ref, sum_ref, triples_ref, taps_ref):
+    core, chip, _, _ = place()
+    fill_inner(src_ref, triples_ref, 4)
+    stage_taps(kernel_ref, taps_ref, True)
+    add_rows(triples_ref, taps_ref, sum_ref, 2, INNER, True, (core == 0) & (chip == 0))
+
+
+def input_outer_kernel(
+    inner_ref, taps_ref, far_ref, corner_ref, near_ref, cot_ref, triples_in_ref, out_ref, triples_ref, outer_ref,
+    sum_ref
 ):
     core, chip, _, _ = place()
     outer_ref[...] = far_ref[...]
@@ -191,15 +224,11 @@
     def _():
         outer_ref[2:4] = corner_ref[...]
 
-    fill_triples(src_ref, outer_ref, near_ref, triples_ref, 4)
-    sum_ref[...] = back_terms(triples_ref, kernel_ref, 2, TAPS)
-
-    @pl.when((core == 0) & (chip == 0))
-    def _():
-        sum_ref[0:128, :] += back_terms(triples_ref, kernel_ref, 1, FOLD)
-
+    fill_outer(outer_ref, near_ref, triples_ref, 4)
+    sum_ref[...] = inner_ref[...]
+    add_rows(triples_ref, taps_ref, sum_ref, 2, OUTER, False, (core == 0) & (chip == 0))
     cot = cot_ref[...].reshape(256, 128).astype(jnp.float32)
-    out_ref[...] = (cot + sum_ref[...]).astype(jnp.bfloat16).reshape(out_ref.shape)
+    out_ref[...] = (cot + interleaved(sum_ref, 2)).astype(jnp.bfloat16).reshape(out_ref.shape)
 
 
 def grads_kernel(both_ref, triples_ref, send_ref, act_ref, edge_ref, before_ref, terms_ref):
@@ -254,9 +283,8 @@
                 for c in range(2):
                     start = 54 * (((zh * 4 + y) * 2 + c) * 4 + x)
                     blocks.append(terms_ref[start : start + 54, :])
-            blocks.append(jnp.zeros((8, 128), jnp.float32))
-            rank = y * 4 + x
-            rank = jnp.where(lax.axis_index("zh") == 0, (rank + 4) % 16, rank)
+            place0, place1 = PLANES[0].index(y * 4 + x), PLANES[1].index(16 + y * 4 + x)
+            rank = jnp.where(lax.axis_index("zh") == 0, place0, place1)
             send_ref[rank] = jnp.concatenate(blocks, axis=0).astype(jnp.bfloat16)
 
 
@@ -264,7 +292,8 @@
     total = got_ref[0].astype(jnp.float32)
     for k in range(1, 16):
         total = total + got_ref[k].astype(jnp.float32)
-    sum_ref[...] = total
+    sum_ref[0:216] = total
+    sum_ref[216:224] = jnp.zeros((8, 128), jnp.float32)
     lane = lax.broadcasted_iota(jnp.int32, (8, 128), 1)
     for zh in range(2):
         for zl in range(8):
@@ -300,7 +329,7 @@
             out_ref[k : k + 1, 128 * r : 128 * r + width] = share[r : r + 1, :width]
 
 
-def call(kernel, out_shape, *args, scratch=(), flops=0):
+def call(kernel, out_shape, *args, scratch=(), flops=0, aliases=None):
     many = isinstance(out_shape, (list, tuple))
     return pl.pallas_call(
         kernel,
@@ -308,6 +337,7 @@
         in_specs=[VMEM] * len(args),
         out_specs=[VMEM] * len(out_shape) if many else VMEM,
         scratch_shapes=scratch,
+        input_output_aliases=aliases or {},
         compiler_params=pltpu.CompilerParams(vmem_limit_bytes=32 * 1024 * 1024),
         cost_estimate=pl.CostEstimate(flops=flops, bytes_accessed=0, transcendentals=0) if flops else None,
     )(*args)
@@ -345,17 +375,24 @@
     kernel = jnp.where(core == 0, first_kernel, second)
     near = lax.ppermute(inner, ROWS, NEAR_ROWS)
     corner = lax.ppermute(corner, everywhere, CORNER_ROWS)
+    inner, triples, taps = call(
+        first_inner_kernel,
+        (shaped((2, 256, 128), f32), shaped((6, 4, 64, 384), bf16), shaped((9, 384, 128), bf16)),
+        source, kernel,
+        flops=300_000_000,
+    )
     own, triples = call(
-        first_conv_kernel,
+        first_outer_kernel,
         (shaped((512, 128), f32), shaped((6, 4, 64, 384), bf16)),
-        source, far, near, corner, kernel,
-        scratch=[pltpu.VMEM((6, 64, 128), bf16)],
+        inner, triples, taps, far, near, corner,
+        scratch=[pltpu.VMEM((6, 64, 128), bf16), pltpu.VMEM((2, 256, 128), f32)],
+        aliases={1: 1},
     )
     both = lax.all_gather(own, "c", tiled=True)
     send, act_grad, edge, before = call(
         grads_kernel,
         (
-            shaped((16, 224, 128), bf16), shaped((4, 2, 64, 128), bf16),
+            shaped((16, 216, 128), bf16), shaped((4, 2, 64, 128), bf16),
             shaped((4, 64, 128), bf16), shaped((2, 2, 64, 128), bf16),
         ),
         both, triples,
@@ -374,13 +411,18 @@
     )
     near = lax.ppermute(inner, ROWS, NEAR_ROWS)
     corner = lax.ppermute(corner, everywhere, CORNER_GRAD)
-    input_grad = call(
-        input_conv_kernel,
-        shaped((2, 2, 64, 128), bf16),
-        source, far, corner, near, first_kernel, cotangent,
-        scratch=[
-            pltpu.VMEM((4, 64, 128), bf16), pltpu.VMEM((4, 4, 64, 384), bf16), pltpu.VMEM((256, 128), f32),
-        ],
+    inner, triples, taps = call(
+        input_inner_kernel,
+        (shaped((2, 128, 128), f32), shaped((4, 4, 64, 384), bf16), shaped((9, 384, 128), bf16)),
+        source, first_kernel,
+        flops=150_000_000,
+    )
+    input_grad, _ = call(
+        input_outer_kernel,
+        (shaped((2, 2, 64, 128), bf16), shaped((4, 4, 64, 384), bf16)),
+        inner, taps, far, corner, near, cotangent, triples,
+        scratch=[pltpu.VMEM((4, 64, 128), bf16), pltpu.VMEM((2, 128, 128), f32)],
+        aliases={6: 1},
         flops=1_600_000_000,
     )
     got, input_grad = lax.optimization_barrier((got, input_grad))

time: 85.9 us -> 84.1 us (0.979)
  waiting for transfers between devices: 18.2 us -> 16.2 us
    ppermute x2, waiting for transfers between devices: 4.01 us -> 1.89 us  [per_device(): near = lax.ppermute(inner, ROWS, NEAR_ROWS)]
    pallas_call x9 -> x11, Pallas kernels: 7.22 us -> 7.89 us  [call(): pl.pallas_call(kernel, out_shape=out_shape, in_specs=[VMEM] * len(args),...]
  transfers between devices with their start and end apart: 12 -> 12, of which waited for: 5 -> 5; matrix products, arithmetic and copies ran while one was open for 1% -> 2% of each run, Pallas kernels for 3% -> 5%
where the time goes in v7:
time: 84.1 us; the launch traced here: 83.6 us
  starting transfers between devices  40.6 us (48%)
  waiting for transfers between devices  16.2 us (19%)
  blocking collectives  15.8 us (19%)
  Pallas kernels  7.89 us (9%)
  other arithmetic  2.23 us (3%)
  between operations  0.85 us (1%)
    all_to_all x1, starting transfers between devices, per_device(): lax.all_to_all(send, ('zh', 'y', 'x'), 0, 0, axis_index_groups=PLANES, ti...  19.7 us
    all_to_all x1, waiting for transfers between devices, per_device(): lax.all_to_all(send, ('zh', 'y', 'x'), 0, 0, axis_index_groups=PLANES, ti...  10.1 us
    all_to_all x1, starting transfers between devices, per_device(): lax.all_to_all(send, ('zh', 'zl'), 0, 0, axis_index_groups=LINES, tiled=T...  8.59 us
    all_gather x1, blocking collectives, per_device(): both = lax.all_gather(given, 'c', tiled=True)  8.43 us
    pallas_call x11, Pallas kernels, call(): pl.pallas_call(kernel, out_shape=out_shape, in_specs=[VMEM] * len(args),...  7.89 us
    all_gather x1, blocking collectives, per_device(): shares = lax.all_gather(shares, 'c', tiled=True)  5.15 us
    ppermute x2, starting transfers between devices, per_device(): near = lax.ppermute(inner, ROWS, NEAR_ROWS)  5.01 us
    ppermute x1, waiting for transfers between devices, per_device(): beyond = lax.ppermute(given, TM, BEYOND)  2.98 us
  transfers between devices with their start and end apart: 12, of which 5 were waited for; matrix products, arithmetic and copies ran while one was open for 2% of the time, Pallas kernels for 5%

profile of v7, /device:TPU:1, one launch (start us, length us, event | category | flops | bytes accessed | tf_op | source)
XLA Modules:
  0.0 83.6 jit_solution(5022727449208420580)
XLA Ops:
  0.6 1.0 %broadcast_select_fusion.1 = (bf16[2,2,64,128]{3,2,1,0:T(8,128)(2,1)S(1)}, bf16[2,2,64,128]{3,2,1,0:T(8,128)(2,1)S(1)}) fusion(bf16[2,2,64,128]{3,2,1,0:T(8,128)(2,1)} %param.4, bf16[2,2,64,128]{3,2,1,0:T(8,128)(2,1)} %cot_ref.1, pred[]{:T(512)S(6)} %eq.2), kind=kLoop, calls=%fused_computation.1 | loop fusion | flops 65536 | bytes 262145 | tf_op jit(solution)/shard_map/jit(_where)/select_n | solution.py:356
  1.6 8.4 %all_gather.9.both_ref = bf16[4,2,64,128]{3,2,1,0:T(8,128)(2,1)S(1)} all-gather(bf16[2,2,64,128]{3,2,1,0:T(8,128)(2,1)S(1)} %get-tuple-element.37), channel_id=1, replica_groups=mesh['zh'=2,'y'=4,'c'=2,'x'=4,'zl'=8] {'c'}, dimensions={0}, use_global_device_ids=true | all-gather | bytes 196608 | tf_op jit(solution)/shard_map/all_gather | solution.py:358
  10.0 1.9 %collective-permute-start = (bf16[2,2,64,128]{3,2,1,0:T(8,128)(2,1)S(1)}, bf16[2,2,64,128]{3,2,1,0:T(8,128)(2,1)S(1)}, u32[]{:S(2)}, u32[]{:S(2)}) collective-permute-start(bf16[2,2,64,128]{3,2,1,0:T(8,128)(2,1)S(1)} %get-tuple-element.37), channel_id=1, source_target_pairs={{32,64},{64,32},{96,128},{128,96},{160,192},{192,160},{288,320},{3... | collective-permute-start | bytes 196616 | tf_op jit(solution)/shard_map/ppermute | solution.py:361
  12.0 0.7 collective-permute-start.1
  12.6 3.0 %collective-permute-done.beyond_ref = bf16[2,2,64,128]{3,2,1,0:T(8,128)(2,1)S(1)} collective-permute-done((bf16[2,2,64,128]{3,2,1,0:T(8,128)(2,1)S(1)}, bf16[2,2,64,128]{3,2,1,0:T(8,128)(2,1)S(1)}, u32[]{:S(2)}, u32[]{:S(2)}) %collective-permute-start) | collective-permute-done | bytes 65568 | tf_op jit(solution)/shard_map/ppermute | solution.py:361
  16.3 0.7 collective-permute-start.3
  17.7 1.9 %collective-permute-start.4 = (bf16[6,64,128]{2,1,0:T(8,128)(2,1)S(1)}, bf16[6,64,128]{2,1,0:T(8,128)(2,1)S(1)}, u32[]{:S(2)}, u32[]{:S(2)}) collective-permute-start(bf16[6,64,128]{2,1,0:T(8,128)(2,1)S(1)} %get-tuple-element.47), channel_id=1, source_target_pairs={{0,1},{1,0},{2,3},{3,2},{4,5},{5,4},{6,7},{7,6},{8,9},{9,8},{10,11... | collective-permute-start | bytes 294920 | tf_op jit(solution)/shard_map/ppermute | solution.py:376
  19.7 1.3 %broadcast_select_fusion.kernel_ref = bf16[3456,128]{1,0:T(8,128)(2,1)S(1)} fusion(bf16[3456,128]{1,0:T(8,128)(2,1)} %bitcast.4, pred[]{:T(512)S(6)} %eq.2, bf16[3,3,3,128,128]{4,3,2,1,0:T(8,128)(2,1)S(1)} %copy-done), kind=kLoop, calls=%fused_computation | loop fusion | flops 442368 | bytes 2654209 | tf_op jit(solution)/shard_map/jit(_where)/select_n | solution.py:375
  20.9 1.5 %shard_map.61 = (f32[2,256,128]{2,1,0:T(8,128)S(1)}, bf16[6,4,64,384]{3,2,1,0:T(8,128)(2,1)S(1)}, bf16[9,384,128]{2,1,0:T(8,128)(2,1)S(1)}) custom-call(bf16[6,2,64,128]{3,2,1,0:T(8,128)(2,1)S(1)} %get-tuple-element.39.src_ref, bf16[3456,128]{1,0:T(8,128)(2,1)S(1)} %broadcast_select_fusion.kernel_ref), custom_call_target="tpu_custom_call" | custom-call | flops 300000000 | tf_op jit(solution)/shard_map/pallas_call | solution.py:334
  22.5 0.9 %collective-permute-done.4.near_ref = bf16[6,64,128]{2,1,0:T(8,128)(2,1)S(1)} collective-permute-done((bf16[6,64,128]{2,1,0:T(8,128)(2,1)S(1)}, bf16[6,64,128]{2,1,0:T(8,128)(2,1)S(1)}, u32[]{:S(2)}, u32[]{:S(2)}) %collective-permute-start.4) | collective-permute-done | bytes 98336 | tf_op jit(solution)/shard_map/ppermute | solution.py:376
  23.3 0.7 shard_map.62
  24.1 2.2 %all_gather.10.both_ref = f32[1024,128]{1,0:T(8,128)S(1)} all-gather(f32[512,128]{1,0:T(8,128)S(1)} %get-tuple-element.49), channel_id=1, replica_groups=mesh['zh'=2,'y'=4,'c'=2,'x'=4,'zl'=8] {'c'}, dimensions={0}, use_global_device_ids=true | all-gather | bytes 786432 | tf_op jit(solution)/shard_map/all_gather | solution.py:391
  26.3 2.5 %shard_map.63 = (bf16[16,216,128]{2,1,0:T(8,128)(2,1)}, bf16[4,2,64,128]{3,2,1,0:T(8,128)(2,1)S(1)}, bf16[4,64,128]{2,1,0:T(8,128)(2,1)S(1)}, bf16[2,2,64,128]{3,2,1,0:T(8,128)(2,1)S(1)}) custom-call(f32[1024,128]{1,0:T(8,128)S(1)} %all_gather.10.both_ref, bf16[6,4,64,384]{3,2,1,0:T(8,128)(2,1)S(1)} %get-tuple-element.50.triples_ref), custom_call_target="tpu_custom_call" | custom-call | tf_op jit(solution)/shard_map/pallas_call | solution.py:334
  28.8 19.7 %all-to-all-start = ((bf16[16,216,128]{2,1,0:T(8,128)(2,1)}), bf16[16,216,128]{2,1,0:T(8,128)(2,1)S(1)}, u32[]{:S(2)}, u32[]{:S(2)}) async-start(bf16[16,216,128]{2,1,0:T(8,128)(2,1)} %get-tuple-element.51), calls=%async_computation | async-start | bytes 1769472 | tf_op jit(solution)/shard_map/all_to_all | solution.py:401
  48.5 1.3 %collective-permute-start.6 = (bf16[2,2,64,128]{3,2,1,0:T(8,128)(2,1)S(1)}, bf16[2,2,64,128]{3,2,1,0:T(8,128)(2,1)S(1)}, u32[]{:S(2)}, u32[]{:S(2)}) collective-permute-start(bf16[2,2,64,128]{3,2,1,0:T(8,128)(2,1)S(1)} %get-tuple-element.53), channel_id=1, source_target_pairs={{64,32},{65,33},{66,34},{67,35},{68,36},{69,37},{70,38},{71,39},{7... | collective-permute-start | bytes 196616 | tf_op jit(solution)/shard_map/ppermute | solution.py:402
  49.8 0.8 collective-permute-start.7
  50.6 10.1 %all-to-all-done.got_ref = bf16[16,216,128]{2,1,0:T(8,128)(2,1)S(1)} async-done(((bf16[16,216,128]{2,1,0:T(8,128)(2,1)}), bf16[16,216,128]{2,1,0:T(8,128)(2,1)S(1)}, u32[]{:S(2)}, u32[]{:S(2)}) %all-to-all-start) | async-done | bytes 884768 | tf_op jit(solution)/shard_map/all_to_all | solution.py:401
  60.7 0.9 %shard_map.64 = bf16[16,16,128]{2,1,0:T(8,128)(2,1)} custom-call(bf16[16,216,128]{2,1,0:T(8,128)(2,1)S(1)} %all-to-all-done.got_ref), custom_call_target="tpu_custom_call" | custom-call | tf_op jit(solution)/shard_map/pallas_call | solution.py:334
  61.6 8.6 %all-to-all-start.1 = ((bf16[16,16,128]{2,1,0:T(8,128)(2,1)}), bf16[16,16,128]{2,1,0:T(8,128)(2,1)S(1)}, u32[]{:S(2)}, u32[]{:S(2)}) async-start(bf16[16,16,128]{2,1,0:T(8,128)(2,1)} %shard_map.64), calls=%async_computation.1 | async-start | bytes 131072 | tf_op jit(solution)/shard_map/all_to_all | solution.py:405
  70.2 3.1 %collective-permute-start.9 = (bf16[4,64,128]{2,1,0:T(8,128)(2,1)S(1)}, bf16[4,64,128]{2,1,0:T(8,128)(2,1)S(1)}, u32[]{:S(2)}, u32[]{:S(2)}) collective-permute-start(bf16[4,64,128]{2,1,0:T(8,128)(2,1)S(1)} %get-tuple-element.61), channel_id=1, source_target_pairs={{0,1},{1,0},{2,3},{3,2},{4,5},{5,4},{6,7},{7,6},{8,9},{9,8},{10,11... | collective-permute-start | bytes 196616 | tf_op jit(solution)/shard_map/ppermute | solution.py:412
  74.6 1.0 %collective-permute-done.9.near_ref = bf16[4,64,128]{2,1,0:T(8,128)(2,1)S(1)} collective-permute-done((bf16[4,64,128]{2,1,0:T(8,128)(2,1)S(1)}, bf16[4,64,128]{2,1,0:T(8,128)(2,1)S(1)}, u32[]{:S(2)}, u32[]{:S(2)}) %collective-permute-start.9) | collective-permute-done | bytes 65568 | tf_op jit(solution)/shard_map/ppermute | solution.py:412
  75.6 1.0 %shard_map.67 = (bf16[2,2,64,128]{3,2,1,0:T(8,128)(2,1)}, bf16[4,4,64,384]{3,2,1,0:T(8,128)(2,1)S(1)}) custom-call(f32[2,128,128]{2,1,0:T(8,128)S(1)} %get-tuple-element.58.inner_ref, bf16[9,384,128]{2,1,0:T(8,128)(2,1)S(1)} %get-tuple-element.59.taps_ref, bf16[4,64,128]{2,1,0:T(8,128)(2,1)S(1)} %collective-permute-done.7.far_ref, ...), custom_call_target="tpu_custom_call", output_to_operand_aliasing={{1}: (6, {})} | custom-call | flops 1600000000 | tf_op jit(solution)/shard_map/pallas_call | solution.py:334
  76.6 1.2 %all-to-all-done.1.got_ref = bf16[16,16,128]{2,1,0:T(8,128)(2,1)S(1)} async-done(((bf16[16,16,128]{2,1,0:T(8,128)(2,1)}), bf16[16,16,128]{2,1,0:T(8,128)(2,1)S(1)}, u32[]{:S(2)}, u32[]{:S(2)}) %all-to-all-start.1) | async-done | bytes 65568 | tf_op jit(solution)/shard_map/all_to_all | solution.py:405
  77.8 5.2 %all_gather.11.refs_0_ = f32[32,128]{1,0:T(8,128)S(1)} all-gather(f32[16,128]{1,0:T(8,128)S(1)} %shard_map.68), channel_id=1, replica_groups=mesh['zh'=2,'y'=4,'c'=2,'x'=4,'zl'=8] {'c'}, dimensions={0}, use_global_device_ids=true | all-gather | bytes 24576 | tf_op jit(solution)/shard_map/all_gather | solution.py:431
  (20 shorter events, 3.3 us)
Async XLA Ops:
  0.6 19.0 %copy-start = (bf16[3,3,3,128,128]{4,3,2,1,0:T(8,128)(2,1)S(1)}, bf16[3,3,3,128,128]{4,3,2,1,0:T(8,128)(2,1)}, u32[]{:S(2)}) copy-start(bf16[3,3,3,128,128]{4,3,2,1,0:T(8,128)(2,1)} %param.5) | copy-start | bytes 2654212
  10.0 5.6 %collective-permute-start = (bf16[2,2,64,128]{3,2,1,0:T(8,128)(2,1)S(1)}, bf16[2,2,64,128]{3,2,1,0:T(8,128)(2,1)S(1)}, u32[]{:S(2)}, u32[]{:S(2)}) collective-permute-start(bf16[2,2,64,128]{3,2,1,0:T(8,128)(2,1)S(1)} %get-tuple-element.37), channel_id=1, source_target_pairs={{32,64},{64,32},{96,128},{128,96},{160,192},{192,160},{288,320},{3... | collective-permute-start | bytes 196616 | tf_op jit(solution)/shard_map/ppermute | solution.py:361
  12.0 5.0 %collective-permute-start.1 = (bf16[2,2,64,128]{3,2,1,0:T(8,128)(2,1)S(1)}, bf16[2,2,64,128]{3,2,1,0:T(8,128)(2,1)S(1)}, u32[]{:S(2)}, u32[]{:S(2)}) collective-permute-start(bf16[2,2,64,128]{3,2,1,0:T(8,128)(2,1)S(1)} %get-tuple-element.37), channel_id=1, source_target_pairs={{224,256},{256,224},{225,257},{257,225},{226,258},{258,226},{227,2... | collective-permute-start | bytes 196616 | tf_op jit(solution)/shard_map/ppermute | solution.py:360
  15.6 1.4 %collective-permute-start.2 = (bf16[2,64,128]{2,1,0:T(8,128)(2,1)S(1)}, bf16[2,64,128]{2,1,0:T(8,128)(2,1)S(1)}, u32[]{:S(2)}, u32[]{:S(2)}) collective-permute-start(bf16[2,64,128]{2,1,0:T(8,128)(2,1)S(1)} %get-tuple-element.38), channel_id=1, source_target_pairs={{199,296},{207,304},{215,312},{200,295},{208,303},{216,311},{295,2... | collective-permute-start | bytes 98312 | tf_op jit(solution)/shard_map/ppermute | solution.py:368
  16.3 6.2 %collective-permute-start.3 = (bf16[6,64,128]{2,1,0:T(8,128)(2,1)S(1)}, bf16[6,64,128]{2,1,0:T(8,128)(2,1)S(1)}, u32[]{:S(2)}, u32[]{:S(2)}) collective-permute-start(bf16[6,64,128]{2,1,0:T(8,128)(2,1)S(1)} %get-tuple-element.46), channel_id=1, source_target_pairs={{1,2},{3,4},{5,6},{7,8},{9,10},{11,12},{13,14},{15,16},{17,18},{19... | collective-permute-start | bytes 294920 | tf_op jit(solution)/shard_map/ppermute | solution.py:367
  17.1 5.4 %collective-permute-start.5 = (bf16[2,64,128]{2,1,0:T(8,128)(2,1)S(1)}, bf16[2,64,128]{2,1,0:T(8,128)(2,1)S(1)}, u32[]{:S(2)}, u32[]{:S(2)}) collective-permute-start(bf16[2,64,128]{2,1,0:T(8,128)(2,1)S(1)} %get-tuple-element.48), channel_id=1, source_target_pairs={{225,226},{227,228},{229,230},{233,234},{235,236},{237,238},{241,2... | collective-permute-start | bytes 98312 | tf_op jit(solution)/shard_map/ppermute | solution.py:377
  17.7 5.6 %collective-permute-start.4 = (bf16[6,64,128]{2,1,0:T(8,128)(2,1)S(1)}, bf16[6,64,128]{2,1,0:T(8,128)(2,1)S(1)}, u32[]{:S(2)}, u32[]{:S(2)}) collective-permute-start(bf16[6,64,128]{2,1,0:T(8,128)(2,1)S(1)} %get-tuple-element.47), channel_id=1, source_target_pairs={{0,1},{1,0},{2,3},{3,2},{4,5},{5,4},{6,7},{7,6},{8,9},{9,8},{10,11... | collective-permute-start | bytes 294920 | tf_op jit(solution)/shard_map/ppermute | solution.py:376
  28.8 31.9 %all-to-all-start = ((bf16[16,216,128]{2,1,0:T(8,128)(2,1)}), bf16[16,216,128]{2,1,0:T(8,128)(2,1)S(1)}, u32[]{:S(2)}, u32[]{:S(2)}) async-start(bf16[16,216,128]{2,1,0:T(8,128)(2,1)} %get-tuple-element.51), calls=%async_computation | async-start | bytes 1769472 | tf_op jit(solution)/shard_map/all_to_all | solution.py:401
  48.5 21.7 %collective-permute-start.6 = (bf16[2,2,64,128]{3,2,1,0:T(8,128)(2,1)S(1)}, bf16[2,2,64,128]{3,2,1,0:T(8,128)(2,1)S(1)}, u32[]{:S(2)}, u32[]{:S(2)}) collective-permute-start(bf16[2,2,64,128]{3,2,1,0:T(8,128)(2,1)S(1)} %get-tuple-element.53), channel_id=1, source_target_pairs={{64,32},{65,33},{66,34},{67,35},{68,36},{69,37},{70,38},{71,39},{7... | collective-permute-start | bytes 196616 | tf_op jit(solution)/shard_map/ppermute | solution.py:402
  49.8 25.9 %copy-start.1 = (bf16[2,2,64,128]{3,2,1,0:T(8,128)(2,1)S(1)}, bf16[2,2,64,128]{3,2,1,0:T(8,128)(2,1)}, u32[]{:S(2)}) copy-start(bf16[2,2,64,128]{3,2,1,0:T(8,128)(2,1)} %cot_ref.1) | copy-start | bytes 196612
  49.8 20.4 %collective-permute-start.7 = (bf16[4,64,128]{2,1,0:T(8,128)(2,1)S(1)}, bf16[4,64,128]{2,1,0:T(8,128)(2,1)S(1)}, u32[]{:S(2)}, u32[]{:S(2)}) collective-permute-start(bf16[4,64,128]{2,1,0:T(8,128)(2,1)S(1)} %get-tuple-element.54), channel_id=1, source_target_pairs={{1,2},{3,4},{5,6},{7,8},{9,10},{11,12},{13,14},{15,16},{17,18},{19... | collective-permute-start | bytes 196616 | tf_op jit(solution)/shard_map/ppermute | solution.py:403
  61.6 16.2 %all-to-all-start.1 = ((bf16[16,16,128]{2,1,0:T(8,128)(2,1)}), bf16[16,16,128]{2,1,0:T(8,128)(2,1)S(1)}, u32[]{:S(2)}, u32[]{:S(2)}) async-start(bf16[16,16,128]{2,1,0:T(8,128)(2,1)} %shard_map.64), calls=%async_computation.1 | async-start | bytes 131072 | tf_op jit(solution)/shard_map/all_to_all | solution.py:405
  70.2 5.4 %collective-permute-start.9 = (bf16[4,64,128]{2,1,0:T(8,128)(2,1)S(1)}, bf16[4,64,128]{2,1,0:T(8,128)(2,1)S(1)}, u32[]{:S(2)}, u32[]{:S(2)}) collective-permute-start(bf16[4,64,128]{2,1,0:T(8,128)(2,1)S(1)} %get-tuple-element.61), channel_id=1, source_target_pairs={{0,1},{1,0},{2,3},{3,2},{4,5},{5,4},{6,7},{7,6},{8,9},{9,8},{10,11... | collective-permute-start | bytes 196616 | tf_op jit(solution)/shard_map/ppermute | solution.py:412
  73.3 1.3 %collective-permute-start.8 = (bf16[2,64,128]{2,1,0:T(8,128)(2,1)S(1)}, bf16[2,64,128]{2,1,0:T(8,128)(2,1)S(1)}, u32[]{:S(2)}, u32[]{:S(2)}) collective-permute-start(bf16[2,64,128]{2,1,0:T(8,128)(2,1)S(1)} %get-tuple-element.60), channel_id=1, source_target_pairs={{33,34},{35,36},{37,38},{41,42},{43,44},{45,46},{49,50},{51,52},{5... | collective-permute-start | bytes 98312 | tf_op jit(solution)/shard_map/ppermute | solution.py:413

commit v8 on v7

--- a/solution.py
+++ b/solution.py
@@ -23,7 +23,7 @@
 PLANES = [[12, 13, 14, 15, 8, 9, 10, 11, 4, 5, 6, 7, 0, 1, 2, 3], [16 + i for i in [0, 1, 2, 3, 12, 13, 14, 15, 8, 9, 10, 11, 4, 5, 6, 7]]]
 
 
-LINES = [[(12 - z) % 16 for z in range(16)]]
+LINES = [[11, 10, 9, 8, 7, 6, 5, 4, 3, 2, 1, 0, 15, 14, 13, 12]]
 
 
 def device(chip, core, slab):

time: 84.1 us -> 83.6 us (level)
    all_to_all x1, waiting for transfers between devices: 1.18 us -> 0.01 us  [per_device(): lax.all_to_all(send, ('zh', 'zl'), 0, 0, axis_index_groups=LINES, tiled=T...]
    ppermute x2, waiting for transfers between devices: 1.89 us -> 2.77 us  [per_device(): near = lax.ppermute(inner, ROWS, NEAR_ROWS)]
  transfers between devices with their start and end apart: 12 -> 12, of which waited for: 5 -> 4; matrix products, arithmetic and copies ran while one was open for 2% -> 2% of each run, Pallas kernels for 5% -> 5%
where the time goes in v8:
time: 83.6 us; the launch traced here: 83 us
  starting transfers between devices  40.8 us (49%)
  waiting for transfers between devices  15.9 us (19%)
  blocking collectives  15.4 us (18%)
  Pallas kernels  7.89 us (9%)
  other arithmetic  2.23 us (3%)
  between operations  0.85 us (1%)
    all_to_all x1, starting transfers between devices, per_device(): lax.all_to_all(send, ('zh', 'y', 'x'), 0, 0, axis_index_groups=PLANES, ti...  19.7 us
    all_to_all x1, waiting for transfers between devices, per_device(): lax.all_to_all(send, ('zh', 'y', 'x'), 0, 0, axis_index_groups=PLANES, ti...  10.1 us
    all_to_all x1, starting transfers between devices, per_device(): lax.all_to_all(send, ('zh', 'zl'), 0, 0, axis_index_groups=LINES, tiled=T...  8.78 us
    all_gather x1, blocking collectives, per_device(): both = lax.all_gather(given, 'c', tiled=True)  8.43 us
    pallas_call x11, Pallas kernels, call(): pl.pallas_call(kernel, out_shape=out_shape, in_specs=[VMEM] * len(args),...  7.89 us
    ppermute x2, starting transfers between devices, per_device(): near = lax.ppermute(inner, ROWS, NEAR_ROWS)  5.01 us
    all_gather x1, blocking collectives, per_device(): shares = lax.all_gather(shares, 'c', tiled=True)  4.76 us
    ppermute x1, waiting for transfers between devices, per_device(): beyond = lax.ppermute(given, TM, BEYOND)  2.98 us
  transfers between devices with their start and end apart: 12, of which 4 were waited for; matrix products, arithmetic and copies ran while one was open for 2% of the time, Pallas kernels for 5%

profile of v8, /device:TPU:1, one launch (start us, length us, event | category | flops | bytes accessed | tf_op | source)
XLA Modules:
  0.0 83.0 jit_solution(14401644763943248259)
XLA Ops:
  0.6 1.0 %broadcast_select_fusion.1 = (bf16[2,2,64,128]{3,2,1,0:T(8,128)(2,1)S(1)}, bf16[2,2,64,128]{3,2,1,0:T(8,128)(2,1)S(1)}) fusion(bf16[2,2,64,128]{3,2,1,0:T(8,128)(2,1)} %param.4, bf16[2,2,64,128]{3,2,1,0:T(8,128)(2,1)} %cot_ref.1, pred[]{:T(512)S(6)} %eq.2), kind=kLoop, calls=%fused_computation.1 | loop fusion | flops 65536 | bytes 262145 | tf_op jit(solution)/shard_map/jit(_where)/select_n | solution.py:356
  1.6 8.4 %all_gather.9.both_ref = bf16[4,2,64,128]{3,2,1,0:T(8,128)(2,1)S(1)} all-gather(bf16[2,2,64,128]{3,2,1,0:T(8,128)(2,1)S(1)} %get-tuple-element.37), channel_id=1, replica_groups=mesh['zh'=2,'y'=4,'c'=2,'x'=4,'zl'=8] {'c'}, dimensions={0}, use_global_device_ids=true | all-gather | bytes 196608 | tf_op jit(solution)/shard_map/all_gather | solution.py:358
  10.0 1.9 %collective-permute-start = (bf16[2,2,64,128]{3,2,1,0:T(8,128)(2,1)S(1)}, bf16[2,2,64,128]{3,2,1,0:T(8,128)(2,1)S(1)}, u32[]{:S(2)}, u32[]{:S(2)}) collective-permute-start(bf16[2,2,64,128]{3,2,1,0:T(8,128)(2,1)S(1)} %get-tuple-element.37), channel_id=1, source_target_pairs={{32,64},{64,32},{96,128},{128,96},{160,192},{192,160},{288,320},{3... | collective-permute-start | bytes 196616 | tf_op jit(solution)/shard_map/ppermute | solution.py:361
  12.0 0.7 collective-permute-start.1
  12.6 3.0 %collective-permute-done.beyond_ref = bf16[2,2,64,128]{3,2,1,0:T(8,128)(2,1)S(1)} collective-permute-done((bf16[2,2,64,128]{3,2,1,0:T(8,128)(2,1)S(1)}, bf16[2,2,64,128]{3,2,1,0:T(8,128)(2,1)S(1)}, u32[]{:S(2)}, u32[]{:S(2)}) %collective-permute-start) | collective-permute-done | bytes 65568 | tf_op jit(solution)/shard_map/ppermute | solution.py:361
  15.6 0.7 collective-permute-start.2
  16.3 0.7 collective-permute-start.3
  17.7 1.9 %collective-permute-start.4 = (bf16[6,64,128]{2,1,0:T(8,128)(2,1)S(1)}, bf16[6,64,128]{2,1,0:T(8,128)(2,1)S(1)}, u32[]{:S(2)}, u32[]{:S(2)}) collective-permute-start(bf16[6,64,128]{2,1,0:T(8,128)(2,1)S(1)} %get-tuple-element.47), channel_id=1, source_target_pairs={{0,1},{1,0},{2,3},{3,2},{4,5},{5,4},{6,7},{7,6},{8,9},{9,8},{10,11... | collective-permute-start | bytes 294920 | tf_op jit(solution)/shard_map/ppermute | solution.py:376
  19.7 1.3 %broadcast_select_fusion.kernel_ref = bf16[3456,128]{1,0:T(8,128)(2,1)S(1)} fusion(bf16[3456,128]{1,0:T(8,128)(2,1)} %bitcast.4, pred[]{:T(512)S(6)} %eq.2, bf16[3,3,3,128,128]{4,3,2,1,0:T(8,128)(2,1)S(1)} %copy-done), kind=kLoop, calls=%fused_computation | loop fusion | flops 442368 | bytes 2654209 | tf_op jit(solution)/shard_map/jit(_where)/select_n | solution.py:375
  20.9 1.5 %shard_map.61 = (f32[2,256,128]{2,1,0:T(8,128)S(1)}, bf16[6,4,64,384]{3,2,1,0:T(8,128)(2,1)S(1)}, bf16[9,384,128]{2,1,0:T(8,128)(2,1)S(1)}) custom-call(bf16[6,2,64,128]{3,2,1,0:T(8,128)(2,1)S(1)} %get-tuple-element.39.src_ref, bf16[3456,128]{1,0:T(8,128)(2,1)S(1)} %broadcast_select_fusion.kernel_ref), custom_call_target="tpu_custom_call" | custom-call | flops 300000000 | tf_op jit(solution)/shard_map/pallas_call | solution.py:334
  22.5 0.9 %collective-permute-done.4.near_ref = bf16[6,64,128]{2,1,0:T(8,128)(2,1)S(1)} collective-permute-done((bf16[6,64,128]{2,1,0:T(8,128)(2,1)S(1)}, bf16[6,64,128]{2,1,0:T(8,128)(2,1)S(1)}, u32[]{:S(2)}, u32[]{:S(2)}) %collective-permute-start.4) | collective-permute-done | bytes 98336 | tf_op jit(solution)/shard_map/ppermute | solution.py:376
  23.3 0.7 shard_map.62
  24.1 2.2 %all_gather.10.both_ref = f32[1024,128]{1,0:T(8,128)S(1)} all-gather(f32[512,128]{1,0:T(8,128)S(1)} %get-tuple-element.49), channel_id=1, replica_groups=mesh['zh'=2,'y'=4,'c'=2,'x'=4,'zl'=8] {'c'}, dimensions={0}, use_global_device_ids=true | all-gather | bytes 786432 | tf_op jit(solution)/shard_map/all_gather | solution.py:391
  26.3 2.5 %shard_map.63 = (bf16[16,216,128]{2,1,0:T(8,128)(2,1)}, bf16[4,2,64,128]{3,2,1,0:T(8,128)(2,1)S(1)}, bf16[4,64,128]{2,1,0:T(8,128)(2,1)S(1)}, bf16[2,2,64,128]{3,2,1,0:T(8,128)(2,1)S(1)}) custom-call(f32[1024,128]{1,0:T(8,128)S(1)} %all_gather.10.both_ref, bf16[6,4,64,384]{3,2,1,0:T(8,128)(2,1)S(1)} %get-tuple-element.50.triples_ref), custom_call_target="tpu_custom_call" | custom-call | tf_op jit(solution)/shard_map/pallas_call | solution.py:334
  28.8 19.7 %all-to-all-start = ((bf16[16,216,128]{2,1,0:T(8,128)(2,1)}), bf16[16,216,128]{2,1,0:T(8,128)(2,1)S(1)}, u32[]{:S(2)}, u32[]{:S(2)}) async-start(bf16[16,216,128]{2,1,0:T(8,128)(2,1)} %get-tuple-element.51), calls=%async_computation | async-start | bytes 1769472 | tf_op jit(solution)/shard_map/all_to_all | solution.py:401
  48.5 1.3 %collective-permute-start.6 = (bf16[2,2,64,128]{3,2,1,0:T(8,128)(2,1)S(1)}, bf16[2,2,64,128]{3,2,1,0:T(8,128)(2,1)S(1)}, u32[]{:S(2)}, u32[]{:S(2)}) collective-permute-start(bf16[2,2,64,128]{3,2,1,0:T(8,128)(2,1)S(1)} %get-tuple-element.53), channel_id=1, source_target_pairs={{64,32},{65,33},{66,34},{67,35},{68,36},{69,37},{70,38},{71,39},{7... | collective-permute-start | bytes 196616 | tf_op jit(solution)/shard_map/ppermute | solution.py:402
  49.8 0.8 collective-permute-start.7
  50.6 10.1 %all-to-all-done.got_ref = bf16[16,216,128]{2,1,0:T(8,128)(2,1)S(1)} async-done(((bf16[16,216,128]{2,1,0:T(8,128)(2,1)}), bf16[16,216,128]{2,1,0:T(8,128)(2,1)S(1)}, u32[]{:S(2)}, u32[]{:S(2)}) %all-to-all-start) | async-done | bytes 884768 | tf_op jit(solution)/shard_map/all_to_all | solution.py:401
  60.7 0.9 %shard_map.64 = bf16[16,16,128]{2,1,0:T(8,128)(2,1)} custom-call(bf16[16,216,128]{2,1,0:T(8,128)(2,1)S(1)} %all-to-all-done.got_ref), custom_call_target="tpu_custom_call" | custom-call | tf_op jit(solution)/shard_map/pallas_call | solution.py:334
  61.5 8.8 %all-to-all-start.1 = ((bf16[16,16,128]{2,1,0:T(8,128)(2,1)}), bf16[16,16,128]{2,1,0:T(8,128)(2,1)S(1)}, u32[]{:S(2)}, u32[]{:S(2)}) async-start(bf16[16,16,128]{2,1,0:T(8,128)(2,1)} %shard_map.64), calls=%async_computation.1 | async-start | bytes 131072 | tf_op jit(solution)/shard_map/all_to_all | solution.py:405
  70.4 3.1 %collective-permute-start.9 = (bf16[4,64,128]{2,1,0:T(8,128)(2,1)S(1)}, bf16[4,64,128]{2,1,0:T(8,128)(2,1)S(1)}, u32[]{:S(2)}, u32[]{:S(2)}) collective-permute-start(bf16[4,64,128]{2,1,0:T(8,128)(2,1)S(1)} %get-tuple-element.61), channel_id=1, source_target_pairs={{0,1},{1,0},{2,3},{3,2},{4,5},{5,4},{6,7},{7,6},{8,9},{9,8},{10,11... | collective-permute-start | bytes 196616 | tf_op jit(solution)/shard_map/ppermute | solution.py:412
  74.8 1.9 %collective-permute-done.9.near_ref = bf16[4,64,128]{2,1,0:T(8,128)(2,1)S(1)} collective-permute-done((bf16[4,64,128]{2,1,0:T(8,128)(2,1)S(1)}, bf16[4,64,128]{2,1,0:T(8,128)(2,1)S(1)}, u32[]{:S(2)}, u32[]{:S(2)}) %collective-permute-start.9) | collective-permute-done | bytes 65568 | tf_op jit(solution)/shard_map/ppermute | solution.py:412
  76.7 1.0 %shard_map.67 = (bf16[2,2,64,128]{3,2,1,0:T(8,128)(2,1)}, bf16[4,4,64,384]{3,2,1,0:T(8,128)(2,1)S(1)}) custom-call(f32[2,128,128]{2,1,0:T(8,128)S(1)} %get-tuple-element.58.inner_ref, bf16[9,384,128]{2,1,0:T(8,128)(2,1)S(1)} %get-tuple-element.59.taps_ref, bf16[4,64,128]{2,1,0:T(8,128)(2,1)S(1)} %collective-permute-done.7.far_ref, ...), custom_call_target="tpu_custom_call", output_to_operand_aliasing={{1}: (6, {})} | custom-call | flops 1600000000 | tf_op jit(solution)/shard_map/pallas_call | solution.py:334
  77.7 4.8 %all_gather.11.refs_0_ = f32[32,128]{1,0:T(8,128)S(1)} all-gather(f32[16,128]{1,0:T(8,128)S(1)} %shard_map.68), channel_id=1, replica_groups=mesh['zh'=2,'y'=4,'c'=2,'x'=4,'zl'=8] {'c'}, dimensions={0}, use_global_device_ids=true | all-gather | bytes 24576 | tf_op jit(solution)/shard_map/all_gather | solution.py:431
  (20 shorter events, 2.7 us)
Async XLA Ops:
  0.6 19.0 %copy-start = (bf16[3,3,3,128,128]{4,3,2,1,0:T(8,128)(2,1)S(1)}, bf16[3,3,3,128,128]{4,3,2,1,0:T(8,128)(2,1)}, u32[]{:S(2)}) copy-start(bf16[3,3,3,128,128]{4,3,2,1,0:T(8,128)(2,1)} %param.5) | copy-start | bytes 2654212
  10.0 5.6 %collective-permute-start = (bf16[2,2,64,128]{3,2,1,0:T(8,128)(2,1)S(1)}, bf16[2,2,64,128]{3,2,1,0:T(8,128)(2,1)S(1)}, u32[]{:S(2)}, u32[]{:S(2)}) collective-permute-start(bf16[2,2,64,128]{3,2,1,0:T(8,128)(2,1)S(1)} %get-tuple-element.37), channel_id=1, source_target_pairs={{32,64},{64,32},{96,128},{128,96},{160,192},{192,160},{288,320},{3... | collective-permute-start | bytes 196616 | tf_op jit(solution)/shard_map/ppermute | solution.py:361
  12.0 5.0 %collective-permute-start.1 = (bf16[2,2,64,128]{3,2,1,0:T(8,128)(2,1)S(1)}, bf16[2,2,64,128]{3,2,1,0:T(8,128)(2,1)S(1)}, u32[]{:S(2)}, u32[]{:S(2)}) collective-permute-start(bf16[2,2,64,128]{3,2,1,0:T(8,128)(2,1)S(1)} %get-tuple-element.37), channel_id=1, source_target_pairs={{224,256},{256,224},{225,257},{257,225},{226,258},{258,226},{227,2... | collective-permute-start | bytes 196616 | tf_op jit(solution)/shard_map/ppermute | solution.py:360
  15.6 1.4 %collective-permute-start.2 = (bf16[2,64,128]{2,1,0:T(8,128)(2,1)S(1)}, bf16[2,64,128]{2,1,0:T(8,128)(2,1)S(1)}, u32[]{:S(2)}, u32[]{:S(2)}) collective-permute-start(bf16[2,64,128]{2,1,0:T(8,128)(2,1)S(1)} %get-tuple-element.38), channel_id=1, source_target_pairs={{199,296},{207,304},{215,312},{200,295},{208,303},{216,311},{295,2... | collective-permute-start | bytes 98312 | tf_op jit(solution)/shard_map/ppermute | solution.py:368
  16.3 6.2 %collective-permute-start.3 = (bf16[6,64,128]{2,1,0:T(8,128)(2,1)S(1)}, bf16[6,64,128]{2,1,0:T(8,128)(2,1)S(1)}, u32[]{:S(2)}, u32[]{:S(2)}) collective-permute-start(bf16[6,64,128]{2,1,0:T(8,128)(2,1)S(1)} %get-tuple-element.46), channel_id=1, source_target_pairs={{1,2},{3,4},{5,6},{7,8},{9,10},{11,12},{13,14},{15,16},{17,18},{19... | collective-permute-start | bytes 294920 | tf_op jit(solution)/shard_map/ppermute | solution.py:367
  17.1 5.4 %collective-permute-start.5 = (bf16[2,64,128]{2,1,0:T(8,128)(2,1)S(1)}, bf16[2,64,128]{2,1,0:T(8,128)(2,1)S(1)}, u32[]{:S(2)}, u32[]{:S(2)}) collective-permute-start(bf16[2,64,128]{2,1,0:T(8,128)(2,1)S(1)} %get-tuple-element.48), channel_id=1, source_target_pairs={{225,226},{227,228},{229,230},{233,234},{235,236},{237,238},{241,2... | collective-permute-start | bytes 98312 | tf_op jit(solution)/shard_map/ppermute | solution.py:377
  17.7 5.6 %collective-permute-start.4 = (bf16[6,64,128]{2,1,0:T(8,128)(2,1)S(1)}, bf16[6,64,128]{2,1,0:T(8,128)(2,1)S(1)}, u32[]{:S(2)}, u32[]{:S(2)}) collective-permute-start(bf16[6,64,128]{2,1,0:T(8,128)(2,1)S(1)} %get-tuple-element.47), channel_id=1, source_target_pairs={{0,1},{1,0},{2,3},{3,2},{4,5},{5,4},{6,7},{7,6},{8,9},{9,8},{10,11... | collective-permute-start | bytes 294920 | tf_op jit(solution)/shard_map/ppermute | solution.py:376
  28.8 31.9 %all-to-all-start = ((bf16[16,216,128]{2,1,0:T(8,128)(2,1)}), bf16[16,216,128]{2,1,0:T(8,128)(2,1)S(1)}, u32[]{:S(2)}, u32[]{:S(2)}) async-start(bf16[16,216,128]{2,1,0:T(8,128)(2,1)} %get-tuple-element.51), calls=%async_computation | async-start | bytes 1769472 | tf_op jit(solution)/shard_map/all_to_all | solution.py:401
  48.5 21.9 %collective-permute-start.6 = (bf16[2,2,64,128]{3,2,1,0:T(8,128)(2,1)S(1)}, bf16[2,2,64,128]{3,2,1,0:T(8,128)(2,1)S(1)}, u32[]{:S(2)}, u32[]{:S(2)}) collective-permute-start(bf16[2,2,64,128]{3,2,1,0:T(8,128)(2,1)S(1)} %get-tuple-element.53), channel_id=1, source_target_pairs={{64,32},{65,33},{66,34},{67,35},{68,36},{69,37},{70,38},{71,39},{7... | collective-permute-start | bytes 196616 | tf_op jit(solution)/shard_map/ppermute | solution.py:402
  49.8 26.9 %copy-start.1 = (bf16[2,2,64,128]{3,2,1,0:T(8,128)(2,1)S(1)}, bf16[2,2,64,128]{3,2,1,0:T(8,128)(2,1)}, u32[]{:S(2)}) copy-start(bf16[2,2,64,128]{3,2,1,0:T(8,128)(2,1)} %cot_ref.1) | copy-start | bytes 196612
  49.8 20.6 %collective-permute-start.7 = (bf16[4,64,128]{2,1,0:T(8,128)(2,1)S(1)}, bf16[4,64,128]{2,1,0:T(8,128)(2,1)S(1)}, u32[]{:S(2)}, u32[]{:S(2)}) collective-permute-start(bf16[4,64,128]{2,1,0:T(8,128)(2,1)S(1)} %get-tuple-element.54), channel_id=1, source_target_pairs={{1,2},{3,4},{5,6},{7,8},{9,10},{11,12},{13,14},{15,16},{17,18},{19... | collective-permute-start | bytes 196616 | tf_op jit(solution)/shard_map/ppermute | solution.py:403
  61.5 16.1 %all-to-all-start.1 = ((bf16[16,16,128]{2,1,0:T(8,128)(2,1)}), bf16[16,16,128]{2,1,0:T(8,128)(2,1)S(1)}, u32[]{:S(2)}, u32[]{:S(2)}) async-start(bf16[16,16,128]{2,1,0:T(8,128)(2,1)} %shard_map.64), calls=%async_computation.1 | async-start | bytes 131072 | tf_op jit(solution)/shard_map/all_to_all | solution.py:405
  70.4 6.3 %collective-permute-start.9 = (bf16[4,64,128]{2,1,0:T(8,128)(2,1)S(1)}, bf16[4,64,128]{2,1,0:T(8,128)(2,1)S(1)}, u32[]{:S(2)}, u32[]{:S(2)}) collective-permute-start(bf16[4,64,128]{2,1,0:T(8,128)(2,1)S(1)} %get-tuple-element.61), channel_id=1, source_target_pairs={{0,1},{1,0},{2,3},{3,2},{4,5},{5,4},{6,7},{7,6},{8,9},{9,8},{10,11... | collective-permute-start | bytes 196616 | tf_op jit(solution)/shard_map/ppermute | solution.py:412
  73.5 1.3 %collective-permute-start.8 = (bf16[2,64,128]{2,1,0:T(8,128)(2,1)S(1)}, bf16[2,64,128]{2,1,0:T(8,128)(2,1)S(1)}, u32[]{:S(2)}, u32[]{:S(2)}) collective-permute-start(bf16[2,64,128]{2,1,0:T(8,128)(2,1)S(1)} %get-tuple-element.60), channel_id=1, source_target_pairs={{33,34},{35,36},{37,38},{41,42},{43,44},{45,46},{49,50},{51,52},{5... | collective-permute-start | bytes 98312 | tf_op jit(solution)/shard_map/ppermute | solution.py:413

commit v9 on v8

--- a/solution.py
+++ b/solution.py
@@ -20,10 +20,12 @@
 ENDS_OF = [r for r, _ in ENDS]
 
 
-PLANES = [[12, 13, 14, 15, 8, 9, 10, 11, 4, 5, 6, 7, 0, 1, 2, 3], [16 + i for i in [0, 1, 2, 3, 12, 13, 14, 15, 8, 9, 10, 11, 4, 5, 6, 7]]]
-
-
-LINES = [[11, 10, 9, 8, 7, 6, 5, 4, 3, 2, 1, 0, 15, 14, 13, 12]]
+PLANES = [
+    [half * 16 + (y + 2) % 4 * 4 + (x + 2) % 4 for y in range(4) for x in range(4)] for half in range(2)
+]
+
+
+LINES = [[(12 + z) % 16 for z in range(16)]]
 
 
 def device(chip, core, slab):

time: 83.6 us -> 82.4 us (0.986)
  blocking collectives: 15.4 us -> 13.9 us
  starting transfers between devices: 40.8 us -> 42 us
  waiting for transfers between devices: 15.9 us -> 14.8 us
    all_to_all x1, waiting for transfers between devices: 10.1 us -> 8.59 us  [per_device(): lax.all_to_all(send, ('zh', 'y', 'x'), 0, 0, axis_index_groups=PLANES, ti...]
    all_gather x1, blocking collectives: 4.76 us -> 3.31 us  [per_device(): shares = lax.all_gather(shares, 'c', tiled=True)]
    all_to_all x1, starting transfers between devices: 19.7 us -> 20.9 us  [per_device(): lax.all_to_all(send, ('zh', 'y', 'x'), 0, 0, axis_index_groups=PLANES, ti...]
    all_to_all x1, waiting for transfers between devices: 0.01 us -> 1.12 us  [per_device(): lax.all_to_all(send, ('zh', 'zl'), 0, 0, axis_index_groups=LINES, tiled=T...]
  transfers between devices with their start and end apart: 12 -> 12, of which waited for: 4 -> 5; matrix products, arithmetic and copies ran while one was open for 2% -> 2% of each run, Pallas kernels for 5% -> 5%
where the time goes in v9:
time: 82.4 us; the launch traced here: 81.8 us
  starting transfers between devices  42 us (51%)
  waiting for transfers between devices  14.8 us (18%)
  blocking collectives  13.9 us (17%)
  Pallas kernels  7.89 us (10%)
  other arithmetic  2.23 us (3%)
  between operations  0.85 us (1%)
    all_to_all x1, starting transfers between devices, per_device(): lax.all_to_all(send, ('zh', 'y', 'x'), 0, 0, axis_index_groups=PLANES, ti...  20.9 us
    all_to_all x1, starting transfers between devices, per_device(): lax.all_to_all(send, ('zh', 'zl'), 0, 0, axis_index_groups=LINES, tiled=T...  8.79 us
    all_to_all x1, waiting for transfers between devices, per_device(): lax.all_to_all(send, ('zh', 'y', 'x'), 0, 0, axis_index_groups=PLANES, ti...  8.59 us
    all_gather x1, blocking collectives, per_device(): both = lax.all_gather(given, 'c', tiled=True)  8.43 us
    pallas_call x11, Pallas kernels, call(): pl.pallas_call(kernel, out_shape=out_shape, in_specs=[VMEM] * len(args),...  7.89 us
    ppermute x2, starting transfers between devices, per_device(): near = lax.ppermute(inner, ROWS, NEAR_ROWS)  5.02 us
    all_gather x1, blocking collectives, per_device(): shares = lax.all_gather(shares, 'c', tiled=True)  3.31 us
    ppermute x1, waiting for transfers between devices, per_device(): beyond = lax.ppermute(given, TM, BEYOND)  2.98 us
  transfers between devices with their start and end apart: 12, of which 5 were waited for; matrix products, arithmetic and copies ran while one was open for 2% of the time, Pallas kernels for 5%

profile of v9, /device:TPU:1, one launch (start us, length us, event | category | flops | bytes accessed | tf_op | source)
XLA Modules:
  0.0 81.8 jit_solution(3366545862941579238)
XLA Ops:
  0.6 1.0 %broadcast_select_fusion.1 = (bf16[2,2,64,128]{3,2,1,0:T(8,128)(2,1)S(1)}, bf16[2,2,64,128]{3,2,1,0:T(8,128)(2,1)S(1)}) fusion(bf16[2,2,64,128]{3,2,1,0:T(8,128)(2,1)} %param.4, bf16[2,2,64,128]{3,2,1,0:T(8,128)(2,1)} %cot_ref.1, pred[]{:T(512)S(6)} %eq.2), kind=kLoop, calls=%fused_computation.1 | loop fusion | flops 65536 | bytes 262145 | tf_op jit(solution)/shard_map/jit(_where)/select_n | solution.py:358
  1.6 8.4 %all_gather.9.both_ref = bf16[4,2,64,128]{3,2,1,0:T(8,128)(2,1)S(1)} all-gather(bf16[2,2,64,128]{3,2,1,0:T(8,128)(2,1)S(1)} %get-tuple-element.37), channel_id=1, replica_groups=mesh['zh'=2,'y'=4,'c'=2,'x'=4,'zl'=8] {'c'}, dimensions={0}, use_global_device_ids=true | all-gather | bytes 196608 | tf_op jit(solution)/shard_map/all_gather | solution.py:360
  10.0 1.9 %collective-permute-start = (bf16[2,2,64,128]{3,2,1,0:T(8,128)(2,1)S(1)}, bf16[2,2,64,128]{3,2,1,0:T(8,128)(2,1)S(1)}, u32[]{:S(2)}, u32[]{:S(2)}) collective-permute-start(bf16[2,2,64,128]{3,2,1,0:T(8,128)(2,1)S(1)} %get-tuple-element.37), channel_id=1, source_target_pairs={{32,64},{64,32},{96,128},{128,96},{160,192},{192,160},{288,320},{3... | collective-permute-start | bytes 196616 | tf_op jit(solution)/shard_map/ppermute | solution.py:363
  12.0 0.7 collective-permute-start.1
  12.6 3.0 %collective-permute-done.beyond_ref = bf16[2,2,64,128]{3,2,1,0:T(8,128)(2,1)S(1)} collective-permute-done((bf16[2,2,64,128]{3,2,1,0:T(8,128)(2,1)S(1)}, bf16[2,2,64,128]{3,2,1,0:T(8,128)(2,1)S(1)}, u32[]{:S(2)}, u32[]{:S(2)}) %collective-permute-start) | collective-permute-done | bytes 65568 | tf_op jit(solution)/shard_map/ppermute | solution.py:363
  16.3 0.7 collective-permute-start.3
  17.7 1.9 %collective-permute-start.4 = (bf16[6,64,128]{2,1,0:T(8,128)(2,1)S(1)}, bf16[6,64,128]{2,1,0:T(8,128)(2,1)S(1)}, u32[]{:S(2)}, u32[]{:S(2)}) collective-permute-start(bf16[6,64,128]{2,1,0:T(8,128)(2,1)S(1)} %get-tuple-element.47), channel_id=1, source_target_pairs={{0,1},{1,0},{2,3},{3,2},{4,5},{5,4},{6,7},{7,6},{8,9},{9,8},{10,11... | collective-permute-start | bytes 294920 | tf_op jit(solution)/shard_map/ppermute | solution.py:378
  19.7 1.3 %broadcast_select_fusion.kernel_ref = bf16[3456,128]{1,0:T(8,128)(2,1)S(1)} fusion(bf16[3456,128]{1,0:T(8,128)(2,1)} %bitcast.4, pred[]{:T(512)S(6)} %eq.2, bf16[3,3,3,128,128]{4,3,2,1,0:T(8,128)(2,1)S(1)} %copy-done), kind=kLoop, calls=%fused_computation | loop fusion | flops 442368 | bytes 2654209 | tf_op jit(solution)/shard_map/jit(_where)/select_n | solution.py:377
  20.9 1.5 %shard_map.61 = (f32[2,256,128]{2,1,0:T(8,128)S(1)}, bf16[6,4,64,384]{3,2,1,0:T(8,128)(2,1)S(1)}, bf16[9,384,128]{2,1,0:T(8,128)(2,1)S(1)}) custom-call(bf16[6,2,64,128]{3,2,1,0:T(8,128)(2,1)S(1)} %get-tuple-element.39.src_ref, bf16[3456,128]{1,0:T(8,128)(2,1)S(1)} %broadcast_select_fusion.kernel_ref), custom_call_target="tpu_custom_call" | custom-call | flops 300000000 | tf_op jit(solution)/shard_map/pallas_call | solution.py:336
  22.5 0.9 %collective-permute-done.4.near_ref = bf16[6,64,128]{2,1,0:T(8,128)(2,1)S(1)} collective-permute-done((bf16[6,64,128]{2,1,0:T(8,128)(2,1)S(1)}, bf16[6,64,128]{2,1,0:T(8,128)(2,1)S(1)}, u32[]{:S(2)}, u32[]{:S(2)}) %collective-permute-start.4) | collective-permute-done | bytes 98336 | tf_op jit(solution)/shard_map/ppermute | solution.py:378
  23.3 0.7 shard_map.62
  24.1 2.2 %all_gather.10.both_ref = f32[1024,128]{1,0:T(8,128)S(1)} all-gather(f32[512,128]{1,0:T(8,128)S(1)} %get-tuple-element.49), channel_id=1, replica_groups=mesh['zh'=2,'y'=4,'c'=2,'x'=4,'zl'=8] {'c'}, dimensions={0}, use_global_device_ids=true | all-gather | bytes 786432 | tf_op jit(solution)/shard_map/all_gather | solution.py:393
  26.3 2.5 %shard_map.63 = (bf16[16,216,128]{2,1,0:T(8,128)(2,1)}, bf16[4,2,64,128]{3,2,1,0:T(8,128)(2,1)S(1)}, bf16[4,64,128]{2,1,0:T(8,128)(2,1)S(1)}, bf16[2,2,64,128]{3,2,1,0:T(8,128)(2,1)S(1)}) custom-call(f32[1024,128]{1,0:T(8,128)S(1)} %all_gather.10.both_ref, bf16[6,4,64,384]{3,2,1,0:T(8,128)(2,1)S(1)} %get-tuple-element.50.triples_ref), custom_call_target="tpu_custom_call" | custom-call | tf_op jit(solution)/shard_map/pallas_call | solution.py:336
  28.8 20.9 %all-to-all-start = ((bf16[16,216,128]{2,1,0:T(8,128)(2,1)}), bf16[16,216,128]{2,1,0:T(8,128)(2,1)S(1)}, u32[]{:S(2)}, u32[]{:S(2)}) async-start(bf16[16,216,128]{2,1,0:T(8,128)(2,1)} %get-tuple-element.51), calls=%async_computation | async-start | bytes 1769472 | tf_op jit(solution)/shard_map/all_to_all | solution.py:403
  49.7 1.3 %collective-permute-start.6 = (bf16[2,2,64,128]{3,2,1,0:T(8,128)(2,1)S(1)}, bf16[2,2,64,128]{3,2,1,0:T(8,128)(2,1)S(1)}, u32[]{:S(2)}, u32[]{:S(2)}) collective-permute-start(bf16[2,2,64,128]{3,2,1,0:T(8,128)(2,1)S(1)} %get-tuple-element.53), channel_id=1, source_target_pairs={{64,32},{65,33},{66,34},{67,35},{68,36},{69,37},{70,38},{71,39},{7... | collective-permute-start | bytes 196616 | tf_op jit(solution)/shard_map/ppermute | solution.py:404
  51.0 0.8 collective-permute-start.7
  51.8 8.6 %all-to-all-done.got_ref = bf16[16,216,128]{2,1,0:T(8,128)(2,1)S(1)} async-done(((bf16[16,216,128]{2,1,0:T(8,128)(2,1)}), bf16[16,216,128]{2,1,0:T(8,128)(2,1)S(1)}, u32[]{:S(2)}, u32[]{:S(2)}) %all-to-all-start) | async-done | bytes 884768 | tf_op jit(solution)/shard_map/all_to_all | solution.py:403
  60.4 0.9 %shard_map.64 = bf16[16,16,128]{2,1,0:T(8,128)(2,1)} custom-call(bf16[16,216,128]{2,1,0:T(8,128)(2,1)S(1)} %all-to-all-done.got_ref), custom_call_target="tpu_custom_call" | custom-call | tf_op jit(solution)/shard_map/pallas_call | solution.py:336
  61.2 8.8 %all-to-all-start.1 = ((bf16[16,16,128]{2,1,0:T(8,128)(2,1)}), bf16[16,16,128]{2,1,0:T(8,128)(2,1)S(1)}, u32[]{:S(2)}, u32[]{:S(2)}) async-start(bf16[16,16,128]{2,1,0:T(8,128)(2,1)} %shard_map.64), calls=%async_computation.1 | async-start | bytes 131072 | tf_op jit(solution)/shard_map/all_to_all | solution.py:407
  70.1 3.1 %collective-permute-start.9 = (bf16[4,64,128]{2,1,0:T(8,128)(2,1)S(1)}, bf16[4,64,128]{2,1,0:T(8,128)(2,1)S(1)}, u32[]{:S(2)}, u32[]{:S(2)}) collective-permute-start(bf16[4,64,128]{2,1,0:T(8,128)(2,1)S(1)} %get-tuple-element.61), channel_id=1, source_target_pairs={{0,1},{1,0},{2,3},{3,2},{4,5},{5,4},{6,7},{7,6},{8,9},{9,8},{10,11... | collective-permute-start | bytes 196616 | tf_op jit(solution)/shard_map/ppermute | solution.py:414
  74.5 1.3 %collective-permute-done.9.near_ref = bf16[4,64,128]{2,1,0:T(8,128)(2,1)S(1)} collective-permute-done((bf16[4,64,128]{2,1,0:T(8,128)(2,1)S(1)}, bf16[4,64,128]{2,1,0:T(8,128)(2,1)S(1)}, u32[]{:S(2)}, u32[]{:S(2)}) %collective-permute-start.9) | collective-permute-done | bytes 65568 | tf_op jit(solution)/shard_map/ppermute | solution.py:414
  75.8 1.0 %shard_map.67 = (bf16[2,2,64,128]{3,2,1,0:T(8,128)(2,1)}, bf16[4,4,64,384]{3,2,1,0:T(8,128)(2,1)S(1)}) custom-call(f32[2,128,128]{2,1,0:T(8,128)S(1)} %get-tuple-element.58.inner_ref, bf16[9,384,128]{2,1,0:T(8,128)(2,1)S(1)} %get-tuple-element.59.taps_ref, bf16[4,64,128]{2,1,0:T(8,128)(2,1)S(1)} %collective-permute-done.7.far_ref, ...), custom_call_target="tpu_custom_call", output_to_operand_aliasing={{1}: (6, {})} | custom-call | flops 1600000000 | tf_op jit(solution)/shard_map/pallas_call | solution.py:336
  76.7 1.1 %all-to-all-done.1.got_ref = bf16[16,16,128]{2,1,0:T(8,128)(2,1)S(1)} async-done(((bf16[16,16,128]{2,1,0:T(8,128)(2,1)}), bf16[16,16,128]{2,1,0:T(8,128)(2,1)S(1)}, u32[]{:S(2)}, u32[]{:S(2)}) %all-to-all-start.1) | async-done | bytes 65568 | tf_op jit(solution)/shard_map/all_to_all | solution.py:407
  77.9 3.3 %all_gather.11.refs_0_ = f32[32,128]{1,0:T(8,128)S(1)} all-gather(f32[16,128]{1,0:T(8,128)S(1)} %shard_map.68), channel_id=1, replica_groups=mesh['zh'=2,'y'=4,'c'=2,'x'=4,'zl'=8] {'c'}, dimensions={0}, use_global_device_ids=true | all-gather | bytes 24576 | tf_op jit(solution)/shard_map/all_gather | solution.py:433
  (20 shorter events, 3.3 us)
Async XLA Ops:
  0.6 19.0 %copy-start = (bf16[3,3,3,128,128]{4,3,2,1,0:T(8,128)(2,1)S(1)}, bf16[3,3,3,128,128]{4,3,2,1,0:T(8,128)(2,1)}, u32[]{:S(2)}) copy-start(bf16[3,3,3,128,128]{4,3,2,1,0:T(8,128)(2,1)} %param.5) | copy-start | bytes 2654212
  10.0 5.6 %collective-permute-start = (bf16[2,2,64,128]{3,2,1,0:T(8,128)(2,1)S(1)}, bf16[2,2,64,128]{3,2,1,0:T(8,128)(2,1)S(1)}, u32[]{:S(2)}, u32[]{:S(2)}) collective-permute-start(bf16[2,2,64,128]{3,2,1,0:T(8,128)(2,1)S(1)} %get-tuple-element.37), channel_id=1, source_target_pairs={{32,64},{64,32},{96,128},{128,96},{160,192},{192,160},{288,320},{3... | collective-permute-start | bytes 196616 | tf_op jit(solution)/shard_map/ppermute | solution.py:363
  12.0 5.0 %collective-permute-start.1 = (bf16[2,2,64,128]{3,2,1,0:T(8,128)(2,1)S(1)}, bf16[2,2,64,128]{3,2,1,0:T(8,128)(2,1)S(1)}, u32[]{:S(2)}, u32[]{:S(2)}) collective-permute-start(bf16[2,2,64,128]{3,2,1,0:T(8,128)(2,1)S(1)} %get-tuple-element.37), channel_id=1, source_target_pairs={{224,256},{256,224},{225,257},{257,225},{226,258},{258,226},{227,2... | collective-permute-start | bytes 196616 | tf_op jit(solution)/shard_map/ppermute | solution.py:362
  15.6 1.4 %collective-permute-start.2 = (bf16[2,64,128]{2,1,0:T(8,128)(2,1)S(1)}, bf16[2,64,128]{2,1,0:T(8,128)(2,1)S(1)}, u32[]{:S(2)}, u32[]{:S(2)}) collective-permute-start(bf16[2,64,128]{2,1,0:T(8,128)(2,1)S(1)} %get-tuple-element.38), channel_id=1, source_target_pairs={{199,296},{207,304},{215,312},{200,295},{208,303},{216,311},{295,2... | collective-permute-start | bytes 98312 | tf_op jit(solution)/shard_map/ppermute | solution.py:370
  16.3 6.2 %collective-permute-start.3 = (bf16[6,64,128]{2,1,0:T(8,128)(2,1)S(1)}, bf16[6,64,128]{2,1,0:T(8,128)(2,1)S(1)}, u32[]{:S(2)}, u32[]{:S(2)}) collective-permute-start(bf16[6,64,128]{2,1,0:T(8,128)(2,1)S(1)} %get-tuple-element.46), channel_id=1, source_target_pairs={{1,2},{3,4},{5,6},{7,8},{9,10},{11,12},{13,14},{15,16},{17,18},{19... | collective-permute-start | bytes 294920 | tf_op jit(solution)/shard_map/ppermute | solution.py:369
  17.1 5.4 %collective-permute-start.5 = (bf16[2,64,128]{2,1,0:T(8,128)(2,1)S(1)}, bf16[2,64,128]{2,1,0:T(8,128)(2,1)S(1)}, u32[]{:S(2)}, u32[]{:S(2)}) collective-permute-start(bf16[2,64,128]{2,1,0:T(8,128)(2,1)S(1)} %get-tuple-element.48), channel_id=1, source_target_pairs={{225,226},{227,228},{229,230},{233,234},{235,236},{237,238},{241,2... | collective-permute-start | bytes 98312 | tf_op jit(solution)/shard_map/ppermute | solution.py:379
  17.7 5.6 %collective-permute-start.4 = (bf16[6,64,128]{2,1,0:T(8,128)(2,1)S(1)}, bf16[6,64,128]{2,1,0:T(8,128)(2,1)S(1)}, u32[]{:S(2)}, u32[]{:S(2)}) collective-permute-start(bf16[6,64,128]{2,1,0:T(8,128)(2,1)S(1)} %get-tuple-element.47), channel_id=1, source_target_pairs={{0,1},{1,0},{2,3},{3,2},{4,5},{5,4},{6,7},{7,6},{8,9},{9,8},{10,11... | collective-permute-start | bytes 294920 | tf_op jit(solution)/shard_map/ppermute | solution.py:378
  28.8 31.6 %all-to-all-start = ((bf16[16,216,128]{2,1,0:T(8,128)(2,1)}), bf16[16,216,128]{2,1,0:T(8,128)(2,1)S(1)}, u32[]{:S(2)}, u32[]{:S(2)}) async-start(bf16[16,216,128]{2,1,0:T(8,128)(2,1)} %get-tuple-element.51), calls=%async_computation | async-start | bytes 1769472 | tf_op jit(solution)/shard_map/all_to_all | solution.py:403
  49.7 20.3 %collective-permute-start.6 = (bf16[2,2,64,128]{3,2,1,0:T(8,128)(2,1)S(1)}, bf16[2,2,64,128]{3,2,1,0:T(8,128)(2,1)S(1)}, u32[]{:S(2)}, u32[]{:S(2)}) collective-permute-start(bf16[2,2,64,128]{3,2,1,0:T(8,128)(2,1)S(1)} %get-tuple-element.53), channel_id=1, source_target_pairs={{64,32},{65,33},{66,34},{67,35},{68,36},{69,37},{70,38},{71,39},{7... | collective-permute-start | bytes 196616 | tf_op jit(solution)/shard_map/ppermute | solution.py:404
  51.0 24.8 %copy-start.1 = (bf16[2,2,64,128]{3,2,1,0:T(8,128)(2,1)S(1)}, bf16[2,2,64,128]{3,2,1,0:T(8,128)(2,1)}, u32[]{:S(2)}) copy-start(bf16[2,2,64,128]{3,2,1,0:T(8,128)(2,1)} %cot_ref.1) | copy-start | bytes 196612
  51.0 19.0 %collective-permute-start.7 = (bf16[4,64,128]{2,1,0:T(8,128)(2,1)S(1)}, bf16[4,64,128]{2,1,0:T(8,128)(2,1)S(1)}, u32[]{:S(2)}, u32[]{:S(2)}) collective-permute-start(bf16[4,64,128]{2,1,0:T(8,128)(2,1)S(1)} %get-tuple-element.54), channel_id=1, source_target_pairs={{1,2},{3,4},{5,6},{7,8},{9,10},{11,12},{13,14},{15,16},{17,18},{19... | collective-permute-start | bytes 196616 | tf_op jit(solution)/shard_map/ppermute | solution.py:405
  61.2 16.6 %all-to-all-start.1 = ((bf16[16,16,128]{2,1,0:T(8,128)(2,1)}), bf16[16,16,128]{2,1,0:T(8,128)(2,1)S(1)}, u32[]{:S(2)}, u32[]{:S(2)}) async-start(bf16[16,16,128]{2,1,0:T(8,128)(2,1)} %shard_map.64), calls=%async_computation.1 | async-start | bytes 131072 | tf_op jit(solution)/shard_map/all_to_all | solution.py:407
  70.1 5.7 %collective-permute-start.9 = (bf16[4,64,128]{2,1,0:T(8,128)(2,1)S(1)}, bf16[4,64,128]{2,1,0:T(8,128)(2,1)S(1)}, u32[]{:S(2)}, u32[]{:S(2)}) collective-permute-start(bf16[4,64,128]{2,1,0:T(8,128)(2,1)S(1)} %get-tuple-element.61), channel_id=1, source_target_pairs={{0,1},{1,0},{2,3},{3,2},{4,5},{5,4},{6,7},{7,6},{8,9},{9,8},{10,11... | collective-permute-start | bytes 196616 | tf_op jit(solution)/shard_map/ppermute | solution.py:414
  73.2 1.3 %collective-permute-start.8 = (bf16[2,64,128]{2,1,0:T(8,128)(2,1)S(1)}, bf16[2,64,128]{2,1,0:T(8,128)(2,1)S(1)}, u32[]{:S(2)}, u32[]{:S(2)}) collective-permute-start(bf16[2,64,128]{2,1,0:T(8,128)(2,1)S(1)} %get-tuple-element.60), channel_id=1, source_target_pairs={{33,34},{35,36},{37,38},{41,42},{43,44},{45,46},{49,50},{51,52},{5... | collective-permute-start | bytes 98312 | tf_op jit(solution)/shard_map/ppermute | solution.py:415

commit v10 on v9

--- a/solution.py
+++ b/solution.py
@@ -21,7 +21,7 @@
 
 
 PLANES = [
-    [half * 16 + (y + 2) % 4 * 4 + (x + 2) % 4 for y in range(4) for x in range(4)] for half in range(2)
+    [half * 16 + (2 - y) % 4 * 4 + (2 - x) % 4 for y in range(4) for x in range(4)] for half in range(2)
 ]
 
 

time: 82.4 us -> 82.8 us (level)
  no operation moved by 1% of the time
where the time goes in v10:
time: 82.8 us; the launch traced here: 82.2 us
  starting transfers between devices  42.2 us (51%)
  waiting for transfers between devices  14.9 us (18%)
  blocking collectives  14.1 us (17%)
  Pallas kernels  7.89 us (10%)
  other arithmetic  2.23 us (3%)
  between operations  0.85 us (1%)
    all_to_all x1, starting transfers between devices, per_device(): lax.all_to_all(send, ('zh', 'y', 'x'), 0, 0, axis_index_groups=PLANES, ti...  20.9 us
    all_to_all x1, starting transfers between devices, per_device(): lax.all_to_all(send, ('zh', 'zl'), 0, 0, axis_index_groups=LINES, tiled=T...  8.93 us
    all_to_all x1, waiting for transfers between devices, per_device(): lax.all_to_all(send, ('zh', 'y', 'x'), 0, 0, axis_index_groups=PLANES, ti...  8.86 us
    all_gather x1, blocking collectives, per_device(): both = lax.all_gather(given, 'c', tiled=True)  8.43 us
    pallas_call x11, Pallas kernels, call(): pl.pallas_call(kernel, out_shape=out_shape, in_specs=[VMEM] * len(args),...  7.89 us
    ppermute x2, starting transfers between devices, per_device(): near = lax.ppermute(inner, ROWS, NEAR_ROWS)  5.02 us
    all_gather x1, blocking collectives, per_device(): shares = lax.all_gather(shares, 'c', tiled=True)  3.49 us
    ppermute x1, waiting for transfers between devices, per_device(): beyond = lax.ppermute(given, TM, BEYOND)  2.98 us
  transfers between devices with their start and end apart: 12, of which 5 were waited for; matrix products, arithmetic and copies ran while one was open for 2% of the time, Pallas kernels for 5%

profile of v10, /device:TPU:1, one launch (start us, length us, event | category | flops | bytes accessed | tf_op | source)
XLA Modules:
  0.0 82.2 jit_solution(11939040832579815503)
XLA Ops:
  0.6 1.0 %broadcast_select_fusion.1 = (bf16[2,2,64,128]{3,2,1,0:T(8,128)(2,1)S(1)}, bf16[2,2,64,128]{3,2,1,0:T(8,128)(2,1)S(1)}) fusion(bf16[2,2,64,128]{3,2,1,0:T(8,128)(2,1)} %param.4, bf16[2,2,64,128]{3,2,1,0:T(8,128)(2,1)} %cot_ref.1, pred[]{:T(512)S(6)} %eq.2), kind=kLoop, calls=%fused_computation.1 | loop fusion | flops 65536 | bytes 262145 | tf_op jit(solution)/shard_map/jit(_where)/select_n | solution.py:358
  1.6 8.4 %all_gather.9.both_ref = bf16[4,2,64,128]{3,2,1,0:T(8,128)(2,1)S(1)} all-gather(bf16[2,2,64,128]{3,2,1,0:T(8,128)(2,1)S(1)} %get-tuple-element.37), channel_id=1, replica_groups=mesh['zh'=2,'y'=4,'c'=2,'x'=4,'zl'=8] {'c'}, dimensions={0}, use_global_device_ids=true | all-gather | bytes 196608 | tf_op jit(solution)/shard_map/all_gather | solution.py:360
  10.0 1.9 %collective-permute-start = (bf16[2,2,64,128]{3,2,1,0:T(8,128)(2,1)S(1)}, bf16[2,2,64,128]{3,2,1,0:T(8,128)(2,1)S(1)}, u32[]{:S(2)}, u32[]{:S(2)}) collective-permute-start(bf16[2,2,64,128]{3,2,1,0:T(8,128)(2,1)S(1)} %get-tuple-element.37), channel_id=1, source_target_pairs={{32,64},{64,32},{96,128},{128,96},{160,192},{192,160},{288,320},{3... | collective-permute-start | bytes 196616 | tf_op jit(solution)/shard_map/ppermute | solution.py:363
  12.0 0.7 collective-permute-start.1
  12.6 3.0 %collective-permute-done.beyond_ref = bf16[2,2,64,128]{3,2,1,0:T(8,128)(2,1)S(1)} collective-permute-done((bf16[2,2,64,128]{3,2,1,0:T(8,128)(2,1)S(1)}, bf16[2,2,64,128]{3,2,1,0:T(8,128)(2,1)S(1)}, u32[]{:S(2)}, u32[]{:S(2)}) %collective-permute-start) | collective-permute-done | bytes 65568 | tf_op jit(solution)/shard_map/ppermute | solution.py:363
  15.6 0.7 collective-permute-start.2
  16.3 0.7 collective-permute-start.3
  17.7 1.9 %collective-permute-start.4 = (bf16[6,64,128]{2,1,0:T(8,128)(2,1)S(1)}, bf16[6,64,128]{2,1,0:T(8,128)(2,1)S(1)}, u32[]{:S(2)}, u32[]{:S(2)}) collective-permute-start(bf16[6,64,128]{2,1,0:T(8,128)(2,1)S(1)} %get-tuple-element.47), channel_id=1, source_target_pairs={{0,1},{1,0},{2,3},{3,2},{4,5},{5,4},{6,7},{7,6},{8,9},{9,8},{10,11... | collective-permute-start | bytes 294920 | tf_op jit(solution)/shard_map/ppermute | solution.py:378
  19.7 1.3 %broadcast_select_fusion.kernel_ref = bf16[3456,128]{1,0:T(8,128)(2,1)S(1)} fusion(bf16[3456,128]{1,0:T(8,128)(2,1)} %bitcast.4, pred[]{:T(512)S(6)} %eq.2, bf16[3,3,3,128,128]{4,3,2,1,0:T(8,128)(2,1)S(1)} %copy-done), kind=kLoop, calls=%fused_computation | loop fusion | flops 442368 | bytes 2654209 | tf_op jit(solution)/shard_map/jit(_where)/select_n | solution.py:377
  20.9 1.5 %shard_map.61 = (f32[2,256,128]{2,1,0:T(8,128)S(1)}, bf16[6,4,64,384]{3,2,1,0:T(8,128)(2,1)S(1)}, bf16[9,384,128]{2,1,0:T(8,128)(2,1)S(1)}) custom-call(bf16[6,2,64,128]{3,2,1,0:T(8,128)(2,1)S(1)} %get-tuple-element.39.src_ref, bf16[3456,128]{1,0:T(8,128)(2,1)S(1)} %broadcast_select_fusion.kernel_ref), custom_call_target="tpu_custom_call" | custom-call | flops 300000000 | tf_op jit(solution)/shard_map/pallas_call | solution.py:336
  22.5 0.9 %collective-permute-done.4.near_ref = bf16[6,64,128]{2,1,0:T(8,128)(2,1)S(1)} collective-permute-done((bf16[6,64,128]{2,1,0:T(8,128)(2,1)S(1)}, bf16[6,64,128]{2,1,0:T(8,128)(2,1)S(1)}, u32[]{:S(2)}, u32[]{:S(2)}) %collective-permute-start.4) | collective-permute-done | bytes 98336 | tf_op jit(solution)/shard_map/ppermute | solution.py:378
  23.3 0.7 shard_map.62
  24.1 2.2 %all_gather.10.both_ref = f32[1024,128]{1,0:T(8,128)S(1)} all-gather(f32[512,128]{1,0:T(8,128)S(1)} %get-tuple-element.49), channel_id=1, replica_groups=mesh['zh'=2,'y'=4,'c'=2,'x'=4,'zl'=8] {'c'}, dimensions={0}, use_global_device_ids=true | all-gather | bytes 786432 | tf_op jit(solution)/shard_map/all_gather | solution.py:393
  26.3 2.5 %shard_map.63 = (bf16[16,216,128]{2,1,0:T(8,128)(2,1)}, bf16[4,2,64,128]{3,2,1,0:T(8,128)(2,1)S(1)}, bf16[4,64,128]{2,1,0:T(8,128)(2,1)S(1)}, bf16[2,2,64,128]{3,2,1,0:T(8,128)(2,1)S(1)}) custom-call(f32[1024,128]{1,0:T(8,128)S(1)} %all_gather.10.both_ref, bf16[6,4,64,384]{3,2,1,0:T(8,128)(2,1)S(1)} %get-tuple-element.50.triples_ref), custom_call_target="tpu_custom_call" | custom-call | tf_op jit(solution)/shard_map/pallas_call | solution.py:336
  28.8 20.9 %all-to-all-start = ((bf16[16,216,128]{2,1,0:T(8,128)(2,1)}), bf16[16,216,128]{2,1,0:T(8,128)(2,1)S(1)}, u32[]{:S(2)}, u32[]{:S(2)}) async-start(bf16[16,216,128]{2,1,0:T(8,128)(2,1)} %get-tuple-element.51), calls=%async_computation | async-start | bytes 1769472 | tf_op jit(solution)/shard_map/all_to_all | solution.py:403
  49.7 1.3 %collective-permute-start.6 = (bf16[2,2,64,128]{3,2,1,0:T(8,128)(2,1)S(1)}, bf16[2,2,64,128]{3,2,1,0:T(8,128)(2,1)S(1)}, u32[]{:S(2)}, u32[]{:S(2)}) collective-permute-start(bf16[2,2,64,128]{3,2,1,0:T(8,128)(2,1)S(1)} %get-tuple-element.53), channel_id=1, source_target_pairs={{64,32},{65,33},{66,34},{67,35},{68,36},{69,37},{70,38},{71,39},{7... | collective-permute-start | bytes 196616 | tf_op jit(solution)/shard_map/ppermute | solution.py:404
  51.0 0.8 collective-permute-start.7
  51.8 8.9 %all-to-all-done.got_ref = bf16[16,216,128]{2,1,0:T(8,128)(2,1)S(1)} async-done(((bf16[16,216,128]{2,1,0:T(8,128)(2,1)}), bf16[16,216,128]{2,1,0:T(8,128)(2,1)S(1)}, u32[]{:S(2)}, u32[]{:S(2)}) %all-to-all-start) | async-done | bytes 884768 | tf_op jit(solution)/shard_map/all_to_all | solution.py:403
  60.7 0.9 %shard_map.64 = bf16[16,16,128]{2,1,0:T(8,128)(2,1)} custom-call(bf16[16,216,128]{2,1,0:T(8,128)(2,1)S(1)} %all-to-all-done.got_ref), custom_call_target="tpu_custom_call" | custom-call | tf_op jit(solution)/shard_map/pallas_call | solution.py:336
  61.5 8.9 %all-to-all-start.1 = ((bf16[16,16,128]{2,1,0:T(8,128)(2,1)}), bf16[16,16,128]{2,1,0:T(8,128)(2,1)S(1)}, u32[]{:S(2)}, u32[]{:S(2)}) async-start(bf16[16,16,128]{2,1,0:T(8,128)(2,1)} %shard_map.64), calls=%async_computation.1 | async-start | bytes 131072 | tf_op jit(solution)/shard_map/all_to_all | solution.py:407
  70.5 3.1 %collective-permute-start.9 = (bf16[4,64,128]{2,1,0:T(8,128)(2,1)S(1)}, bf16[4,64,128]{2,1,0:T(8,128)(2,1)S(1)}, u32[]{:S(2)}, u32[]{:S(2)}) collective-permute-start(bf16[4,64,128]{2,1,0:T(8,128)(2,1)S(1)} %get-tuple-element.61), channel_id=1, source_target_pairs={{0,1},{1,0},{2,3},{3,2},{4,5},{5,4},{6,7},{7,6},{8,9},{9,8},{10,11... | collective-permute-start | bytes 196616 | tf_op jit(solution)/shard_map/ppermute | solution.py:414
  74.9 1.5 %collective-permute-done.9.near_ref = bf16[4,64,128]{2,1,0:T(8,128)(2,1)S(1)} collective-permute-done((bf16[4,64,128]{2,1,0:T(8,128)(2,1)S(1)}, bf16[4,64,128]{2,1,0:T(8,128)(2,1)S(1)}, u32[]{:S(2)}, u32[]{:S(2)}) %collective-permute-start.9) | collective-permute-done | bytes 65568 | tf_op jit(solution)/shard_map/ppermute | solution.py:414
  76.4 1.0 %shard_map.67 = (bf16[2,2,64,128]{3,2,1,0:T(8,128)(2,1)}, bf16[4,4,64,384]{3,2,1,0:T(8,128)(2,1)S(1)}) custom-call(f32[2,128,128]{2,1,0:T(8,128)S(1)} %get-tuple-element.58.inner_ref, bf16[9,384,128]{2,1,0:T(8,128)(2,1)S(1)} %get-tuple-element.59.taps_ref, bf16[4,64,128]{2,1,0:T(8,128)(2,1)S(1)} %collective-permute-done.7.far_ref, ...), custom_call_target="tpu_custom_call", output_to_operand_aliasing={{1}: (6, {})} | custom-call | flops 1600000000 | tf_op jit(solution)/shard_map/pallas_call | solution.py:336
  78.1 3.5 %all_gather.11.refs_0_ = f32[32,128]{1,0:T(8,128)S(1)} all-gather(f32[16,128]{1,0:T(8,128)S(1)} %shard_map.68), channel_id=1, replica_groups=mesh['zh'=2,'y'=4,'c'=2,'x'=4,'zl'=8] {'c'}, dimensions={0}, use_global_device_ids=true | all-gather | bytes 24576 | tf_op jit(solution)/shard_map/all_gather | solution.py:433
  (20 shorter events, 3.3 us)
Async XLA Ops:
  0.6 19.0 %copy-start = (bf16[3,3,3,128,128]{4,3,2,1,0:T(8,128)(2,1)S(1)}, bf16[3,3,3,128,128]{4,3,2,1,0:T(8,128)(2,1)}, u32[]{:S(2)}) copy-start(bf16[3,3,3,128,128]{4,3,2,1,0:T(8,128)(2,1)} %param.5) | copy-start | bytes 2654212
  10.0 5.6 %collective-permute-start = (bf16[2,2,64,128]{3,2,1,0:T(8,128)(2,1)S(1)}, bf16[2,2,64,128]{3,2,1,0:T(8,128)(2,1)S(1)}, u32[]{:S(2)}, u32[]{:S(2)}) collective-permute-start(bf16[2,2,64,128]{3,2,1,0:T(8,128)(2,1)S(1)} %get-tuple-element.37), channel_id=1, source_target_pairs={{32,64},{64,32},{96,128},{128,96},{160,192},{192,160},{288,320},{3... | collective-permute-start | bytes 196616 | tf_op jit(solution)/shard_map/ppermute | solution.py:363
  12.0 5.0 %collective-permute-start.1 = (bf16[2,2,64,128]{3,2,1,0:T(8,128)(2,1)S(1)}, bf16[2,2,64,128]{3,2,1,0:T(8,128)(2,1)S(1)}, u32[]{:S(2)}, u32[]{:S(2)}) collective-permute-start(bf16[2,2,64,128]{3,2,1,0:T(8,128)(2,1)S(1)} %get-tuple-element.37), channel_id=1, source_target_pairs={{224,256},{256,224},{225,257},{257,225},{226,258},{258,226},{227,2... | collective-permute-start | bytes 196616 | tf_op jit(solution)/shard_map/ppermute | solution.py:362
  15.6 1.4 %collective-permute-start.2 = (bf16[2,64,128]{2,1,0:T(8,128)(2,1)S(1)}, bf16[2,64,128]{2,1,0:T(8,128)(2,1)S(1)}, u32[]{:S(2)}, u32[]{:S(2)}) collective-permute-start(bf16[2,64,128]{2,1,0:T(8,128)(2,1)S(1)} %get-tuple-element.38), channel_id=1, source_target_pairs={{199,296},{207,304},{215,312},{200,295},{208,303},{216,311},{295,2... | collective-permute-start | bytes 98312 | tf_op jit(solution)/shard_map/ppermute | solution.py:370
  16.3 6.2 %collective-permute-start.3 = (bf16[6,64,128]{2,1,0:T(8,128)(2,1)S(1)}, bf16[6,64,128]{2,1,0:T(8,128)(2,1)S(1)}, u32[]{:S(2)}, u32[]{:S(2)}) collective-permute-start(bf16[6,64,128]{2,1,0:T(8,128)(2,1)S(1)} %get-tuple-element.46), channel_id=1, source_target_pairs={{1,2},{3,4},{5,6},{7,8},{9,10},{11,12},{13,14},{15,16},{17,18},{19... | collective-permute-start | bytes 294920 | tf_op jit(solution)/shard_map/ppermute | solution.py:369
  17.1 5.4 %collective-permute-start.5 = (bf16[2,64,128]{2,1,0:T(8,128)(2,1)S(1)}, bf16[2,64,128]{2,1,0:T(8,128)(2,1)S(1)}, u32[]{:S(2)}, u32[]{:S(2)}) collective-permute-start(bf16[2,64,128]{2,1,0:T(8,128)(2,1)S(1)} %get-tuple-element.48), channel_id=1, source_target_pairs={{225,226},{227,228},{229,230},{233,234},{235,236},{237,238},{241,2... | collective-permute-start | bytes 98312 | tf_op jit(solution)/shard_map/ppermute | solution.py:379
  17.7 5.6 %collective-permute-start.4 = (bf16[6,64,128]{2,1,0:T(8,128)(2,1)S(1)}, bf16[6,64,128]{2,1,0:T(8,128)(2,1)S(1)}, u32[]{:S(2)}, u32[]{:S(2)}) collective-permute-start(bf16[6,64,128]{2,1,0:T(8,128)(2,1)S(1)} %get-tuple-element.47), channel_id=1, source_target_pairs={{0,1},{1,0},{2,3},{3,2},{4,5},{5,4},{6,7},{7,6},{8,9},{9,8},{10,11... | collective-permute-start | bytes 294920 | tf_op jit(solution)/shard_map/ppermute | solution.py:378
  28.8 31.9 %all-to-all-start = ((bf16[16,216,128]{2,1,0:T(8,128)(2,1)}), bf16[16,216,128]{2,1,0:T(8,128)(2,1)S(1)}, u32[]{:S(2)}, u32[]{:S(2)}) async-start(bf16[16,216,128]{2,1,0:T(8,128)(2,1)} %get-tuple-element.51), calls=%async_computation | async-start | bytes 1769472 | tf_op jit(solution)/shard_map/all_to_all | solution.py:403
  49.7 20.8 %collective-permute-start.6 = (bf16[2,2,64,128]{3,2,1,0:T(8,128)(2,1)S(1)}, bf16[2,2,64,128]{3,2,1,0:T(8,128)(2,1)S(1)}, u32[]{:S(2)}, u32[]{:S(2)}) collective-permute-start(bf16[2,2,64,128]{3,2,1,0:T(8,128)(2,1)S(1)} %get-tuple-element.53), channel_id=1, source_target_pairs={{64,32},{65,33},{66,34},{67,35},{68,36},{69,37},{70,38},{71,39},{7... | collective-permute-start | bytes 196616 | tf_op jit(solution)/shard_map/ppermute | solution.py:404
  51.0 25.5 %copy-start.1 = (bf16[2,2,64,128]{3,2,1,0:T(8,128)(2,1)S(1)}, bf16[2,2,64,128]{3,2,1,0:T(8,128)(2,1)}, u32[]{:S(2)}) copy-start(bf16[2,2,64,128]{3,2,1,0:T(8,128)(2,1)} %cot_ref.1) | copy-start | bytes 196612
  51.0 19.5 %collective-permute-start.7 = (bf16[4,64,128]{2,1,0:T(8,128)(2,1)S(1)}, bf16[4,64,128]{2,1,0:T(8,128)(2,1)S(1)}, u32[]{:S(2)}, u32[]{:S(2)}) collective-permute-start(bf16[4,64,128]{2,1,0:T(8,128)(2,1)S(1)} %get-tuple-element.54), channel_id=1, source_target_pairs={{1,2},{3,4},{5,6},{7,8},{9,10},{11,12},{13,14},{15,16},{17,18},{19... | collective-permute-start | bytes 196616 | tf_op jit(solution)/shard_map/ppermute | solution.py:405
  61.5 16.5 %all-to-all-start.1 = ((bf16[16,16,128]{2,1,0:T(8,128)(2,1)}), bf16[16,16,128]{2,1,0:T(8,128)(2,1)S(1)}, u32[]{:S(2)}, u32[]{:S(2)}) async-start(bf16[16,16,128]{2,1,0:T(8,128)(2,1)} %shard_map.64), calls=%async_computation.1 | async-start | bytes 131072 | tf_op jit(solution)/shard_map/all_to_all | solution.py:407
  70.5 5.9 %collective-permute-start.9 = (bf16[4,64,128]{2,1,0:T(8,128)(2,1)S(1)}, bf16[4,64,128]{2,1,0:T(8,128)(2,1)S(1)}, u32[]{:S(2)}, u32[]{:S(2)}) collective-permute-start(bf16[4,64,128]{2,1,0:T(8,128)(2,1)S(1)} %get-tuple-element.61), channel_id=1, source_target_pairs={{0,1},{1,0},{2,3},{3,2},{4,5},{5,4},{6,7},{7,6},{8,9},{9,8},{10,11... | collective-permute-start | bytes 196616 | tf_op jit(solution)/shard_map/ppermute | solution.py:414
  73.6 1.3 %collective-permute-start.8 = (bf16[2,64,128]{2,1,0:T(8,128)(2,1)S(1)}, bf16[2,64,128]{2,1,0:T(8,128)(2,1)S(1)}, u32[]{:S(2)}, u32[]{:S(2)}) collective-permute-start(bf16[2,64,128]{2,1,0:T(8,128)(2,1)S(1)} %get-tuple-element.60), channel_id=1, source_target_pairs={{33,34},{35,36},{37,38},{41,42},{43,44},{45,46},{49,50},{51,52},{5... | collective-permute-start | bytes 98312 | tf_op jit(solution)/shard_map/ppermute | solution.py:415

commit v11 on v9

--- a/solution.py
+++ b/solution.py
@@ -356,7 +356,8 @@
     first_kernel, second_kernel = first_kernel.reshape(3456, 128), second_kernel.reshape(3456, 128)
     given = jnp.where(core == 0, cotangent, video_clip)
     mine = jnp.where(core == 0, video_clip, cotangent)
-    given, mine = lax.optimization_barrier((given, mine))
+    given, clip, cot = lax.optimization_barrier((given, video_clip, cotangent))
+    mine = jnp.where(core == 0, clip, cot)
     both = lax.all_gather(given, "c", tiled=True)
     both, given = lax.optimization_barrier((both, given))
     beyond_far = lax.ppermute(given, TM, BEYOND_FAR)

time: 82.4 us -> 82.9 us (level)
  starting transfers between devices: 42 us -> 40.7 us
  other arithmetic: 2.23 us -> 3.07 us
    select_n x1 -> x2, other arithmetic: 0.96 us -> 1.8 us  [the longest x1 0.94 us: per_device(): given = jnp.where(core == 0, cotangent, video_clip)]
  transfers between devices with their start and end apart: 12 -> 12, of which waited for: 5 -> 5; matrix products, arithmetic and copies ran while one was open for 2% -> 3% of each run, Pallas kernels for 5% -> 5%
where the time goes in v11:
time: 82.9 us; the launch traced here: 81.9 us
  starting transfers between devices  40.7 us (49%)
  waiting for transfers between devices  15.2 us (18%)
  blocking collectives  14.2 us (17%)
  Pallas kernels  7.88 us (10%)
  other arithmetic  3.07 us (4%)
  between operations  0.85 us (1%)
    all_to_all x1, starting transfers between devices, per_device(): lax.all_to_all(send, ('zh', 'y', 'x'), 0, 0, axis_index_groups=PLANES, ti...  20.3 us
    all_to_all x1, waiting for transfers between devices, per_device(): lax.all_to_all(send, ('zh', 'y', 'x'), 0, 0, axis_index_groups=PLANES, ti...  8.66 us
    all_gather x1, blocking collectives, per_device(): both = lax.all_gather(given, 'c', tiled=True)  8.42 us
    all_to_all x1, starting transfers between devices, per_device(): lax.all_to_all(send, ('zh', 'zl'), 0, 0, axis_index_groups=LINES, tiled=T...  8 us
    pallas_call x11, Pallas kernels, call(): pl.pallas_call(kernel, out_shape=out_shape, in_specs=[VMEM] * len(args),...  7.88 us
    ppermute x2, starting transfers between devices, per_device(): near = lax.ppermute(inner, ROWS, NEAR_ROWS)  5.01 us
    all_gather x1, blocking collectives, per_device(): shares = lax.all_gather(shares, 'c', tiled=True)  3.59 us
    ppermute x2, waiting for transfers between devices, per_device(): near = lax.ppermute(inner, ROWS, NEAR_ROWS)  2.87 us
  transfers between devices with their start and end apart: 12, of which 5 were waited for; matrix products, arithmetic and copies ran while one was open for 3% of the time, Pallas kernels for 5%

profile of v11, /device:TPU:1, one launch (start us, length us, event | category | flops | bytes accessed | tf_op | source)
XLA Modules:
  0.0 81.9 jit_solution(12447231381323189993)
XLA Ops:
  0.6 0.9 %broadcast_select_fusion.2 = bf16[2,2,64,128]{3,2,1,0:T(8,128)(2,1)S(1)} fusion(bf16[2,2,64,128]{3,2,1,0:T(8,128)(2,1)} %cot_ref.1, bf16[2,2,64,128]{3,2,1,0:T(8,128)(2,1)} %param.4, pred[]{:T(512)S(6)} %eq.2), kind=kLoop, calls=%fused_computation.2 | loop fusion | flops 32768 | bytes 196609 | tf_op jit(solution)/shard_map/jit(_where)/select_n | solution.py:357
  1.6 8.4 %all_gather.9.both_ref = bf16[4,2,64,128]{3,2,1,0:T(8,128)(2,1)S(1)} all-gather(bf16[2,2,64,128]{3,2,1,0:T(8,128)(2,1)S(1)} %broadcast_select_fusion.2), channel_id=1, replica_groups=mesh['zh'=2,'y'=4,'c'=2,'x'=4,'zl'=8] {'c'}, dimensions={0}, use_global_device_ids=true | all-gather | bytes 196608 | tf_op jit(solution)/shard_map/all_gather | solution.py:361
  10.7 1.9 %collective-permute-start = (bf16[2,2,64,128]{3,2,1,0:T(8,128)(2,1)S(1)}, bf16[2,2,64,128]{3,2,1,0:T(8,128)(2,1)S(1)}, u32[]{:S(2)}, u32[]{:S(2)}) collective-permute-start(bf16[2,2,64,128]{3,2,1,0:T(8,128)(2,1)S(1)} %broadcast_select_fusion.2), channel_id=1, source_target_pairs={{32,64},{64,32},{96,128},{128,96},{160,192},{192,160},{288,320},{3... | collective-permute-start | bytes 196616 | tf_op jit(solution)/shard_map/ppermute | solution.py:364
  12.6 0.9 %broadcast_select_fusion.1.mine_ref = bf16[2,2,64,128]{3,2,1,0:T(8,128)(2,1)S(1)} fusion(bf16[2,2,64,128]{3,2,1,0:T(8,128)(2,1)} %param.4, bf16[2,2,64,128]{3,2,1,0:T(8,128)(2,1)} %cot_ref.1, pred[]{:T(512)S(6)} %eq.2), kind=kLoop, calls=%fused_computation.1 | loop fusion | flops 32768 | bytes 196609 | tf_op jit(solution)/shard_map/jit(_where)/select_n | solution.py:360
  13.5 2.8 %collective-permute-done.beyond_ref = bf16[2,2,64,128]{3,2,1,0:T(8,128)(2,1)S(1)} collective-permute-done((bf16[2,2,64,128]{3,2,1,0:T(8,128)(2,1)S(1)}, bf16[2,2,64,128]{3,2,1,0:T(8,128)(2,1)S(1)}, u32[]{:S(2)}, u32[]{:S(2)}) %collective-permute-start) | collective-permute-done | bytes 65568 | tf_op jit(solution)/shard_map/ppermute | solution.py:364
  16.9 0.7 collective-permute-start.3
  18.4 1.9 %collective-permute-start.4 = (bf16[6,64,128]{2,1,0:T(8,128)(2,1)S(1)}, bf16[6,64,128]{2,1,0:T(8,128)(2,1)S(1)}, u32[]{:S(2)}, u32[]{:S(2)}) collective-permute-start(bf16[6,64,128]{2,1,0:T(8,128)(2,1)S(1)} %get-tuple-element.49), channel_id=1, source_target_pairs={{0,1},{1,0},{2,3},{3,2},{4,5},{5,4},{6,7},{7,6},{8,9},{9,8},{10,11... | collective-permute-start | bytes 294920 | tf_op jit(solution)/shard_map/ppermute | solution.py:379
  20.3 1.3 %broadcast_select_fusion.kernel_ref = bf16[3456,128]{1,0:T(8,128)(2,1)S(1)} fusion(bf16[3456,128]{1,0:T(8,128)(2,1)} %bitcast.4, pred[]{:T(512)S(6)} %eq.2, bf16[3,3,3,128,128]{4,3,2,1,0:T(8,128)(2,1)S(1)} %copy-done), kind=kLoop, calls=%fused_computation | loop fusion | flops 442368 | bytes 2654209 | tf_op jit(solution)/shard_map/jit(_where)/select_n | solution.py:378
  21.6 1.5 %shard_map.61 = (f32[2,256,128]{2,1,0:T(8,128)S(1)}, bf16[6,4,64,384]{3,2,1,0:T(8,128)(2,1)S(1)}, bf16[9,384,128]{2,1,0:T(8,128)(2,1)S(1)}) custom-call(bf16[6,2,64,128]{3,2,1,0:T(8,128)(2,1)S(1)} %get-tuple-element.41.src_ref, bf16[3456,128]{1,0:T(8,128)(2,1)S(1)} %broadcast_select_fusion.kernel_ref), custom_call_target="tpu_custom_call" | custom-call | flops 300000000 | tf_op jit(solution)/shard_map/pallas_call | solution.py:336
  23.1 1.4 %collective-permute-done.4.near_ref = bf16[6,64,128]{2,1,0:T(8,128)(2,1)S(1)} collective-permute-done((bf16[6,64,128]{2,1,0:T(8,128)(2,1)S(1)}, bf16[6,64,128]{2,1,0:T(8,128)(2,1)S(1)}, u32[]{:S(2)}, u32[]{:S(2)}) %collective-permute-start.4) | collective-permute-done | bytes 98336 | tf_op jit(solution)/shard_map/ppermute | solution.py:379
  24.6 0.7 shard_map.62
  25.3 2.2 %all_gather.10.both_ref = f32[1024,128]{1,0:T(8,128)S(1)} all-gather(f32[512,128]{1,0:T(8,128)S(1)} %get-tuple-element.51), channel_id=1, replica_groups=mesh['zh'=2,'y'=4,'c'=2,'x'=4,'zl'=8] {'c'}, dimensions={0}, use_global_device_ids=true | all-gather | bytes 786432 | tf_op jit(solution)/shard_map/all_gather | solution.py:394
  27.5 2.5 %shard_map.63 = (bf16[16,216,128]{2,1,0:T(8,128)(2,1)}, bf16[4,2,64,128]{3,2,1,0:T(8,128)(2,1)S(1)}, bf16[4,64,128]{2,1,0:T(8,128)(2,1)S(1)}, bf16[2,2,64,128]{3,2,1,0:T(8,128)(2,1)S(1)}) custom-call(f32[1024,128]{1,0:T(8,128)S(1)} %all_gather.10.both_ref, bf16[6,4,64,384]{3,2,1,0:T(8,128)(2,1)S(1)} %get-tuple-element.52.triples_ref), custom_call_target="tpu_custom_call" | custom-call | tf_op jit(solution)/shard_map/pallas_call | solution.py:336
  30.0 20.3 %all-to-all-start = ((bf16[16,216,128]{2,1,0:T(8,128)(2,1)}), bf16[16,216,128]{2,1,0:T(8,128)(2,1)S(1)}, u32[]{:S(2)}, u32[]{:S(2)}) async-start(bf16[16,216,128]{2,1,0:T(8,128)(2,1)} %get-tuple-element.53), calls=%async_computation | async-start | bytes 1769472 | tf_op jit(solution)/shard_map/all_to_all | solution.py:404
  50.3 1.3 %collective-permute-start.6 = (bf16[2,2,64,128]{3,2,1,0:T(8,128)(2,1)S(1)}, bf16[2,2,64,128]{3,2,1,0:T(8,128)(2,1)S(1)}, u32[]{:S(2)}, u32[]{:S(2)}) collective-permute-start(bf16[2,2,64,128]{3,2,1,0:T(8,128)(2,1)S(1)} %get-tuple-element.55), channel_id=1, source_target_pairs={{64,32},{65,33},{66,34},{67,35},{68,36},{69,37},{70,38},{71,39},{7... | collective-permute-start | bytes 196616 | tf_op jit(solution)/shard_map/ppermute | solution.py:405
  51.6 0.8 collective-permute-start.7
  52.4 8.7 %all-to-all-done.got_ref = bf16[16,216,128]{2,1,0:T(8,128)(2,1)S(1)} async-done(((bf16[16,216,128]{2,1,0:T(8,128)(2,1)}), bf16[16,216,128]{2,1,0:T(8,128)(2,1)S(1)}, u32[]{:S(2)}, u32[]{:S(2)}) %all-to-all-start) | async-done | bytes 884768 | tf_op jit(solution)/shard_map/all_to_all | solution.py:404
  61.1 0.8 %shard_map.64 = bf16[16,16,128]{2,1,0:T(8,128)(2,1)} custom-call(bf16[16,216,128]{2,1,0:T(8,128)(2,1)S(1)} %all-to-all-done.got_ref), custom_call_target="tpu_custom_call" | custom-call | tf_op jit(solution)/shard_map/pallas_call | solution.py:336
  61.9 8.0 %all-to-all-start.1 = ((bf16[16,16,128]{2,1,0:T(8,128)(2,1)}), bf16[16,16,128]{2,1,0:T(8,128)(2,1)S(1)}, u32[]{:S(2)}, u32[]{:S(2)}) async-start(bf16[16,16,128]{2,1,0:T(8,128)(2,1)} %shard_map.64), calls=%async_computation.1 | async-start | bytes 131072 | tf_op jit(solution)/shard_map/all_to_all | solution.py:408
  70.0 3.1 %collective-permute-start.9 = (bf16[4,64,128]{2,1,0:T(8,128)(2,1)S(1)}, bf16[4,64,128]{2,1,0:T(8,128)(2,1)S(1)}, u32[]{:S(2)}, u32[]{:S(2)}) collective-permute-start(bf16[4,64,128]{2,1,0:T(8,128)(2,1)S(1)} %get-tuple-element.63), channel_id=1, source_target_pairs={{0,1},{1,0},{2,3},{3,2},{4,5},{5,4},{6,7},{7,6},{8,9},{9,8},{10,11... | collective-permute-start | bytes 196616 | tf_op jit(solution)/shard_map/ppermute | solution.py:415
  74.4 1.4 %collective-permute-done.9.near_ref = bf16[4,64,128]{2,1,0:T(8,128)(2,1)S(1)} collective-permute-done((bf16[4,64,128]{2,1,0:T(8,128)(2,1)S(1)}, bf16[4,64,128]{2,1,0:T(8,128)(2,1)S(1)}, u32[]{:S(2)}, u32[]{:S(2)}) %collective-permute-start.9) | collective-permute-done | bytes 65568 | tf_op jit(solution)/shard_map/ppermute | solution.py:415
  75.8 1.0 %shard_map.67 = (bf16[2,2,64,128]{3,2,1,0:T(8,128)(2,1)}, bf16[4,4,64,384]{3,2,1,0:T(8,128)(2,1)S(1)}) custom-call(f32[2,128,128]{2,1,0:T(8,128)S(1)} %get-tuple-element.60.inner_ref, bf16[9,384,128]{2,1,0:T(8,128)(2,1)S(1)} %get-tuple-element.61.taps_ref, bf16[4,64,128]{2,1,0:T(8,128)(2,1)S(1)} %collective-permute-done.7.far_ref, ...), custom_call_target="tpu_custom_call", output_to_operand_aliasing={{1}: (6, {})} | custom-call | flops 1600000000 | tf_op jit(solution)/shard_map/pallas_call | solution.py:336
  76.8 0.9 %all-to-all-done.1.got_ref = bf16[16,16,128]{2,1,0:T(8,128)(2,1)S(1)} async-done(((bf16[16,16,128]{2,1,0:T(8,128)(2,1)}), bf16[16,16,128]{2,1,0:T(8,128)(2,1)S(1)}, u32[]{:S(2)}, u32[]{:S(2)}) %all-to-all-start.1) | async-done | bytes 65568 | tf_op jit(solution)/shard_map/all_to_all | solution.py:408
  77.7 3.6 %all_gather.11.refs_0_ = f32[32,128]{1,0:T(8,128)S(1)} all-gather(f32[16,128]{1,0:T(8,128)S(1)} %shard_map.68), channel_id=1, replica_groups=mesh['zh'=2,'y'=4,'c'=2,'x'=4,'zl'=8] {'c'}, dimensions={0}, use_global_device_ids=true | all-gather | bytes 24576 | tf_op jit(solution)/shard_map/all_gather | solution.py:434
  (21 shorter events, 4.0 us)
Async XLA Ops:
  0.6 19.7 %copy-start = (bf16[3,3,3,128,128]{4,3,2,1,0:T(8,128)(2,1)S(1)}, bf16[3,3,3,128,128]{4,3,2,1,0:T(8,128)(2,1)}, u32[]{:S(2)}) copy-start(bf16[3,3,3,128,128]{4,3,2,1,0:T(8,128)(2,1)} %param.5) | copy-start | bytes 2654212
  10.0 7.6 %collective-permute-start.1 = (bf16[2,2,64,128]{3,2,1,0:T(8,128)(2,1)S(1)}, bf16[2,2,64,128]{3,2,1,0:T(8,128)(2,1)S(1)}, u32[]{:S(2)}, u32[]{:S(2)}) collective-permute-start(bf16[2,2,64,128]{3,2,1,0:T(8,128)(2,1)S(1)} %broadcast_select_fusion.2), channel_id=1, source_target_pairs={{224,256},{256,224},{225,257},{257,225},{226,258},{258,226},{227,2... | collective-permute-start | bytes 196616 | tf_op jit(solution)/shard_map/ppermute | solution.py:363
  10.7 5.6 %collective-permute-start = (bf16[2,2,64,128]{3,2,1,0:T(8,128)(2,1)S(1)}, bf16[2,2,64,128]{3,2,1,0:T(8,128)(2,1)S(1)}, u32[]{:S(2)}, u32[]{:S(2)}) collective-permute-start(bf16[2,2,64,128]{3,2,1,0:T(8,128)(2,1)S(1)} %broadcast_select_fusion.2), channel_id=1, source_target_pairs={{32,64},{64,32},{96,128},{128,96},{160,192},{192,160},{288,320},{3... | collective-permute-start | bytes 196616 | tf_op jit(solution)/shard_map/ppermute | solution.py:364
  16.3 1.4 %collective-permute-start.2 = (bf16[2,64,128]{2,1,0:T(8,128)(2,1)S(1)}, bf16[2,64,128]{2,1,0:T(8,128)(2,1)S(1)}, u32[]{:S(2)}, u32[]{:S(2)}) collective-permute-start(bf16[2,64,128]{2,1,0:T(8,128)(2,1)S(1)} %get-tuple-element.40), channel_id=1, source_target_pairs={{199,296},{207,304},{215,312},{200,295},{208,303},{216,311},{295,2... | collective-permute-start | bytes 98312 | tf_op jit(solution)/shard_map/ppermute | solution.py:371
  16.9 6.2 %collective-permute-start.3 = (bf16[6,64,128]{2,1,0:T(8,128)(2,1)S(1)}, bf16[6,64,128]{2,1,0:T(8,128)(2,1)S(1)}, u32[]{:S(2)}, u32[]{:S(2)}) collective-permute-start(bf16[6,64,128]{2,1,0:T(8,128)(2,1)S(1)} %get-tuple-element.48), channel_id=1, source_target_pairs={{1,2},{3,4},{5,6},{7,8},{9,10},{11,12},{13,14},{15,16},{17,18},{19... | collective-permute-start | bytes 294920 | tf_op jit(solution)/shard_map/ppermute | solution.py:370
  17.7 5.4 %collective-permute-start.5 = (bf16[2,64,128]{2,1,0:T(8,128)(2,1)S(1)}, bf16[2,64,128]{2,1,0:T(8,128)(2,1)S(1)}, u32[]{:S(2)}, u32[]{:S(2)}) collective-permute-start(bf16[2,64,128]{2,1,0:T(8,128)(2,1)S(1)} %get-tuple-element.50), channel_id=1, source_target_pairs={{225,226},{227,228},{229,230},{233,234},{235,236},{237,238},{241,2... | collective-permute-start | bytes 98312 | tf_op jit(solution)/shard_map/ppermute | solution.py:380
  18.4 6.2 %collective-permute-start.4 = (bf16[6,64,128]{2,1,0:T(8,128)(2,1)S(1)}, bf16[6,64,128]{2,1,0:T(8,128)(2,1)S(1)}, u32[]{:S(2)}, u32[]{:S(2)}) collective-permute-start(bf16[6,64,128]{2,1,0:T(8,128)(2,1)S(1)} %get-tuple-element.49), channel_id=1, source_target_pairs={{0,1},{1,0},{2,3},{3,2},{4,5},{5,4},{6,7},{7,6},{8,9},{9,8},{10,11... | collective-permute-start | bytes 294920 | tf_op jit(solution)/shard_map/ppermute | solution.py:379
  30.0 31.1 %all-to-all-start = ((bf16[16,216,128]{2,1,0:T(8,128)(2,1)}), bf16[16,216,128]{2,1,0:T(8,128)(2,1)S(1)}, u32[]{:S(2)}, u32[]{:S(2)}) async-start(bf16[16,216,128]{2,1,0:T(8,128)(2,1)} %get-tuple-element.53), calls=%async_computation | async-start | bytes 1769472 | tf_op jit(solution)/shard_map/all_to_all | solution.py:404
  50.3 19.6 %collective-permute-start.6 = (bf16[2,2,64,128]{3,2,1,0:T(8,128)(2,1)S(1)}, bf16[2,2,64,128]{3,2,1,0:T(8,128)(2,1)S(1)}, u32[]{:S(2)}, u32[]{:S(2)}) collective-permute-start(bf16[2,2,64,128]{3,2,1,0:T(8,128)(2,1)S(1)} %get-tuple-element.55), channel_id=1, source_target_pairs={{64,32},{65,33},{66,34},{67,35},{68,36},{69,37},{70,38},{71,39},{7... | collective-permute-start | bytes 196616 | tf_op jit(solution)/shard_map/ppermute | solution.py:405
  51.6 24.2 %copy-start.1 = (bf16[2,2,64,128]{3,2,1,0:T(8,128)(2,1)S(1)}, bf16[2,2,64,128]{3,2,1,0:T(8,128)(2,1)}, u32[]{:S(2)}) copy-start(bf16[2,2,64,128]{3,2,1,0:T(8,128)(2,1)} %cot_ref.1) | copy-start | bytes 196612
  51.6 18.3 %collective-permute-start.7 = (bf16[4,64,128]{2,1,0:T(8,128)(2,1)S(1)}, bf16[4,64,128]{2,1,0:T(8,128)(2,1)S(1)}, u32[]{:S(2)}, u32[]{:S(2)}) collective-permute-start(bf16[4,64,128]{2,1,0:T(8,128)(2,1)S(1)} %get-tuple-element.56), channel_id=1, source_target_pairs={{1,2},{3,4},{5,6},{7,8},{9,10},{11,12},{13,14},{15,16},{17,18},{19... | collective-permute-start | bytes 196616 | tf_op jit(solution)/shard_map/ppermute | solution.py:406
  61.9 15.7 %all-to-all-start.1 = ((bf16[16,16,128]{2,1,0:T(8,128)(2,1)}), bf16[16,16,128]{2,1,0:T(8,128)(2,1)S(1)}, u32[]{:S(2)}, u32[]{:S(2)}) async-start(bf16[16,16,128]{2,1,0:T(8,128)(2,1)} %shard_map.64), calls=%async_computation.1 | async-start | bytes 131072 | tf_op jit(solution)/shard_map/all_to_all | solution.py:408
  70.0 5.8 %collective-permute-start.9 = (bf16[4,64,128]{2,1,0:T(8,128)(2,1)S(1)}, bf16[4,64,128]{2,1,0:T(8,128)(2,1)S(1)}, u32[]{:S(2)}, u32[]{:S(2)}) collective-permute-start(bf16[4,64,128]{2,1,0:T(8,128)(2,1)S(1)} %get-tuple-element.63), channel_id=1, source_target_pairs={{0,1},{1,0},{2,3},{3,2},{4,5},{5,4},{6,7},{7,6},{8,9},{9,8},{10,11... | collective-permute-start | bytes 196616 | tf_op jit(solution)/shard_map/ppermute | solution.py:415
  73.1 1.3 %collective-permute-start.8 = (bf16[2,64,128]{2,1,0:T(8,128)(2,1)S(1)}, bf16[2,64,128]{2,1,0:T(8,128)(2,1)S(1)}, u32[]{:S(2)}, u32[]{:S(2)}) collective-permute-start(bf16[2,64,128]{2,1,0:T(8,128)(2,1)S(1)} %get-tuple-element.62), channel_id=1, source_target_pairs={{33,34},{35,36},{37,38},{41,42},{43,44},{45,46},{49,50},{51,52},{5... | collective-permute-start | bytes 98312 | tf_op jit(solution)/shard_map/ppermute | solution.py:416

commit v12 on v10

--- a/solution.py
+++ b/solution.py
@@ -21,7 +21,7 @@
 
 
 PLANES = [
-    [half * 16 + (2 - y) % 4 * 4 + (2 - x) % 4 for y in range(4) for x in range(4)] for half in range(2)
+    [half * 16 + (2 - y) % 4 * 4 + (x + 2) % 4 for y in range(4) for x in range(4)] for half in range(2)
 ]
 
 

time: 82.8 us -> 82.8 us (level)
  no operation moved by 1% of the time
where the time goes in v12:
time: 82.8 us; the launch traced here: 82.2 us
  starting transfers between devices  42.7 us (52%)
  waiting for transfers between devices  14.6 us (18%)
  blocking collectives  13.9 us (17%)
  Pallas kernels  7.89 us (10%)
  other arithmetic  2.23 us (3%)
  between operations  0.85 us (1%)
    all_to_all x1, starting transfers between devices, per_device(): lax.all_to_all(send, ('zh', 'y', 'x'), 0, 0, axis_index_groups=PLANES, ti...  20.9 us
    all_to_all x1, starting transfers between devices, per_device(): lax.all_to_all(send, ('zh', 'zl'), 0, 0, axis_index_groups=LINES, tiled=T...  9.41 us
    all_gather x1, blocking collectives, per_device(): both = lax.all_gather(given, 'c', tiled=True)  8.43 us
    all_to_all x1, waiting for transfers between devices, per_device(): lax.all_to_all(send, ('zh', 'y', 'x'), 0, 0, axis_index_groups=PLANES, ti...  8.38 us
    pallas_call x11, Pallas kernels, call(): pl.pallas_call(kernel, out_shape=out_shape, in_specs=[VMEM] * len(args),...  7.89 us
    ppermute x2, starting transfers between devices, per_device(): near = lax.ppermute(inner, ROWS, NEAR_ROWS)  5.02 us
    all_gather x1, blocking collectives, per_device(): shares = lax.all_gather(shares, 'c', tiled=True)  3.28 us
    ppermute x1, waiting for transfers between devices, per_device(): beyond = lax.ppermute(given, TM, BEYOND)  2.98 us
  transfers between devices with their start and end apart: 12, of which 5 were waited for; matrix products, arithmetic and copies ran while one was open for 2% of the time, Pallas kernels for 5%

profile of v12, /device:TPU:1, one launch (start us, length us, event | category | flops | bytes accessed | tf_op | source)
XLA Modules:
  0.0 82.2 jit_solution(12444181383997541623)
XLA Ops:
  0.6 1.0 %broadcast_select_fusion.1 = (bf16[2,2,64,128]{3,2,1,0:T(8,128)(2,1)S(1)}, bf16[2,2,64,128]{3,2,1,0:T(8,128)(2,1)S(1)}) fusion(bf16[2,2,64,128]{3,2,1,0:T(8,128)(2,1)} %param.4, bf16[2,2,64,128]{3,2,1,0:T(8,128)(2,1)} %cot_ref.1, pred[]{:T(512)S(6)} %eq.2), kind=kLoop, calls=%fused_computation.1 | loop fusion | flops 65536 | bytes 262145 | tf_op jit(solution)/shard_map/jit(_where)/select_n | solution.py:358
  1.6 8.4 %all_gather.9.both_ref = bf16[4,2,64,128]{3,2,1,0:T(8,128)(2,1)S(1)} all-gather(bf16[2,2,64,128]{3,2,1,0:T(8,128)(2,1)S(1)} %get-tuple-element.37), channel_id=1, replica_groups=mesh['zh'=2,'y'=4,'c'=2,'x'=4,'zl'=8] {'c'}, dimensions={0}, use_global_device_ids=true | all-gather | bytes 196608 | tf_op jit(solution)/shard_map/all_gather | solution.py:360
  10.0 1.9 %collective-permute-start = (bf16[2,2,64,128]{3,2,1,0:T(8,128)(2,1)S(1)}, bf16[2,2,64,128]{3,2,1,0:T(8,128)(2,1)S(1)}, u32[]{:S(2)}, u32[]{:S(2)}) collective-permute-start(bf16[2,2,64,128]{3,2,1,0:T(8,128)(2,1)S(1)} %get-tuple-element.37), channel_id=1, source_target_pairs={{32,64},{64,32},{96,128},{128,96},{160,192},{192,160},{288,320},{3... | collective-permute-start | bytes 196616 | tf_op jit(solution)/shard_map/ppermute | solution.py:363
  12.0 0.7 collective-permute-start.1
  12.6 3.0 %collective-permute-done.beyond_ref = bf16[2,2,64,128]{3,2,1,0:T(8,128)(2,1)S(1)} collective-permute-done((bf16[2,2,64,128]{3,2,1,0:T(8,128)(2,1)S(1)}, bf16[2,2,64,128]{3,2,1,0:T(8,128)(2,1)S(1)}, u32[]{:S(2)}, u32[]{:S(2)}) %collective-permute-start) | collective-permute-done | bytes 65568 | tf_op jit(solution)/shard_map/ppermute | solution.py:363
  16.3 0.7 collective-permute-start.3
  17.7 1.9 %collective-permute-start.4 = (bf16[6,64,128]{2,1,0:T(8,128)(2,1)S(1)}, bf16[6,64,128]{2,1,0:T(8,128)(2,1)S(1)}, u32[]{:S(2)}, u32[]{:S(2)}) collective-permute-start(bf16[6,64,128]{2,1,0:T(8,128)(2,1)S(1)} %get-tuple-element.47), channel_id=1, source_target_pairs={{0,1},{1,0},{2,3},{3,2},{4,5},{5,4},{6,7},{7,6},{8,9},{9,8},{10,11... | collective-permute-start | bytes 294920 | tf_op jit(solution)/shard_map/ppermute | solution.py:378
  19.7 1.3 %broadcast_select_fusion.kernel_ref = bf16[3456,128]{1,0:T(8,128)(2,1)S(1)} fusion(bf16[3456,128]{1,0:T(8,128)(2,1)} %bitcast.4, pred[]{:T(512)S(6)} %eq.2, bf16[3,3,3,128,128]{4,3,2,1,0:T(8,128)(2,1)S(1)} %copy-done), kind=kLoop, calls=%fused_computation | loop fusion | flops 442368 | bytes 2654209 | tf_op jit(solution)/shard_map/jit(_where)/select_n | solution.py:377
  20.9 1.5 %shard_map.61 = (f32[2,256,128]{2,1,0:T(8,128)S(1)}, bf16[6,4,64,384]{3,2,1,0:T(8,128)(2,1)S(1)}, bf16[9,384,128]{2,1,0:T(8,128)(2,1)S(1)}) custom-call(bf16[6,2,64,128]{3,2,1,0:T(8,128)(2,1)S(1)} %get-tuple-element.39.src_ref, bf16[3456,128]{1,0:T(8,128)(2,1)S(1)} %broadcast_select_fusion.kernel_ref), custom_call_target="tpu_custom_call" | custom-call | flops 300000000 | tf_op jit(solution)/shard_map/pallas_call | solution.py:336
  22.5 0.9 %collective-permute-done.4.near_ref = bf16[6,64,128]{2,1,0:T(8,128)(2,1)S(1)} collective-permute-done((bf16[6,64,128]{2,1,0:T(8,128)(2,1)S(1)}, bf16[6,64,128]{2,1,0:T(8,128)(2,1)S(1)}, u32[]{:S(2)}, u32[]{:S(2)}) %collective-permute-start.4) | collective-permute-done | bytes 98336 | tf_op jit(solution)/shard_map/ppermute | solution.py:378
  23.3 0.7 shard_map.62
  24.1 2.2 %all_gather.10.both_ref = f32[1024,128]{1,0:T(8,128)S(1)} all-gather(f32[512,128]{1,0:T(8,128)S(1)} %get-tuple-element.49), channel_id=1, replica_groups=mesh['zh'=2,'y'=4,'c'=2,'x'=4,'zl'=8] {'c'}, dimensions={0}, use_global_device_ids=true | all-gather | bytes 786432 | tf_op jit(solution)/shard_map/all_gather | solution.py:393
  26.3 2.5 %shard_map.63 = (bf16[16,216,128]{2,1,0:T(8,128)(2,1)}, bf16[4,2,64,128]{3,2,1,0:T(8,128)(2,1)S(1)}, bf16[4,64,128]{2,1,0:T(8,128)(2,1)S(1)}, bf16[2,2,64,128]{3,2,1,0:T(8,128)(2,1)S(1)}) custom-call(f32[1024,128]{1,0:T(8,128)S(1)} %all_gather.10.both_ref, bf16[6,4,64,384]{3,2,1,0:T(8,128)(2,1)S(1)} %get-tuple-element.50.triples_ref), custom_call_target="tpu_custom_call" | custom-call | tf_op jit(solution)/shard_map/pallas_call | solution.py:336
  28.8 20.9 %all-to-all-start = ((bf16[16,216,128]{2,1,0:T(8,128)(2,1)}), bf16[16,216,128]{2,1,0:T(8,128)(2,1)S(1)}, u32[]{:S(2)}, u32[]{:S(2)}) async-start(bf16[16,216,128]{2,1,0:T(8,128)(2,1)} %get-tuple-element.51), calls=%async_computation | async-start | bytes 1769472 | tf_op jit(solution)/shard_map/all_to_all | solution.py:403
  49.7 1.3 %collective-permute-start.6 = (bf16[2,2,64,128]{3,2,1,0:T(8,128)(2,1)S(1)}, bf16[2,2,64,128]{3,2,1,0:T(8,128)(2,1)S(1)}, u32[]{:S(2)}, u32[]{:S(2)}) collective-permute-start(bf16[2,2,64,128]{3,2,1,0:T(8,128)(2,1)S(1)} %get-tuple-element.53), channel_id=1, source_target_pairs={{64,32},{65,33},{66,34},{67,35},{68,36},{69,37},{70,38},{71,39},{7... | collective-permute-start | bytes 196616 | tf_op jit(solution)/shard_map/ppermute | solution.py:404
  51.0 0.8 collective-permute-start.7
  51.8 8.4 %all-to-all-done.got_ref = bf16[16,216,128]{2,1,0:T(8,128)(2,1)S(1)} async-done(((bf16[16,216,128]{2,1,0:T(8,128)(2,1)}), bf16[16,216,128]{2,1,0:T(8,128)(2,1)S(1)}, u32[]{:S(2)}, u32[]{:S(2)}) %all-to-all-start) | async-done | bytes 884768 | tf_op jit(solution)/shard_map/all_to_all | solution.py:403
  60.2 0.9 %shard_map.64 = bf16[16,16,128]{2,1,0:T(8,128)(2,1)} custom-call(bf16[16,216,128]{2,1,0:T(8,128)(2,1)S(1)} %all-to-all-done.got_ref), custom_call_target="tpu_custom_call" | custom-call | tf_op jit(solution)/shard_map/pallas_call | solution.py:336
  61.0 9.4 %all-to-all-start.1 = ((bf16[16,16,128]{2,1,0:T(8,128)(2,1)}), bf16[16,16,128]{2,1,0:T(8,128)(2,1)S(1)}, u32[]{:S(2)}, u32[]{:S(2)}) async-start(bf16[16,16,128]{2,1,0:T(8,128)(2,1)} %shard_map.64), calls=%async_computation.1 | async-start | bytes 131072 | tf_op jit(solution)/shard_map/all_to_all | solution.py:407
  70.5 3.1 %collective-permute-start.9 = (bf16[4,64,128]{2,1,0:T(8,128)(2,1)S(1)}, bf16[4,64,128]{2,1,0:T(8,128)(2,1)S(1)}, u32[]{:S(2)}, u32[]{:S(2)}) collective-permute-start(bf16[4,64,128]{2,1,0:T(8,128)(2,1)S(1)} %get-tuple-element.61), channel_id=1, source_target_pairs={{0,1},{1,0},{2,3},{3,2},{4,5},{5,4},{6,7},{7,6},{8,9},{9,8},{10,11... | collective-permute-start | bytes 196616 | tf_op jit(solution)/shard_map/ppermute | solution.py:414
  74.9 1.3 %collective-permute-done.9.near_ref = bf16[4,64,128]{2,1,0:T(8,128)(2,1)S(1)} collective-permute-done((bf16[4,64,128]{2,1,0:T(8,128)(2,1)S(1)}, bf16[4,64,128]{2,1,0:T(8,128)(2,1)S(1)}, u32[]{:S(2)}, u32[]{:S(2)}) %collective-permute-start.9) | collective-permute-done | bytes 65568 | tf_op jit(solution)/shard_map/ppermute | solution.py:414
  76.2 1.0 %shard_map.67 = (bf16[2,2,64,128]{3,2,1,0:T(8,128)(2,1)}, bf16[4,4,64,384]{3,2,1,0:T(8,128)(2,1)S(1)}) custom-call(f32[2,128,128]{2,1,0:T(8,128)S(1)} %get-tuple-element.58.inner_ref, bf16[9,384,128]{2,1,0:T(8,128)(2,1)S(1)} %get-tuple-element.59.taps_ref, bf16[4,64,128]{2,1,0:T(8,128)(2,1)S(1)} %collective-permute-done.7.far_ref, ...), custom_call_target="tpu_custom_call", output_to_operand_aliasing={{1}: (6, {})} | custom-call | flops 1600000000 | tf_op jit(solution)/shard_map/pallas_call | solution.py:336
  77.1 1.1 %all-to-all-done.1.got_ref = bf16[16,16,128]{2,1,0:T(8,128)(2,1)S(1)} async-done(((bf16[16,16,128]{2,1,0:T(8,128)(2,1)}), bf16[16,16,128]{2,1,0:T(8,128)(2,1)S(1)}, u32[]{:S(2)}, u32[]{:S(2)}) %all-to-all-start.1) | async-done | bytes 65568 | tf_op jit(solution)/shard_map/all_to_all | solution.py:407
  78.3 3.3 %all_gather.11.refs_0_ = f32[32,128]{1,0:T(8,128)S(1)} all-gather(f32[16,128]{1,0:T(8,128)S(1)} %shard_map.68), channel_id=1, replica_groups=mesh['zh'=2,'y'=4,'c'=2,'x'=4,'zl'=8] {'c'}, dimensions={0}, use_global_device_ids=true | all-gather | bytes 24576 | tf_op jit(solution)/shard_map/all_gather | solution.py:433
  (20 shorter events, 3.3 us)
Async XLA Ops:
  0.6 19.0 %copy-start = (bf16[3,3,3,128,128]{4,3,2,1,0:T(8,128)(2,1)S(1)}, bf16[3,3,3,128,128]{4,3,2,1,0:T(8,128)(2,1)}, u32[]{:S(2)}) copy-start(bf16[3,3,3,128,128]{4,3,2,1,0:T(8,128)(2,1)} %param.5) | copy-start | bytes 2654212
  10.0 5.6 %collective-permute-start = (bf16[2,2,64,128]{3,2,1,0:T(8,128)(2,1)S(1)}, bf16[2,2,64,128]{3,2,1,0:T(8,128)(2,1)S(1)}, u32[]{:S(2)}, u32[]{:S(2)}) collective-permute-start(bf16[2,2,64,128]{3,2,1,0:T(8,128)(2,1)S(1)} %get-tuple-element.37), channel_id=1, source_target_pairs={{32,64},{64,32},{96,128},{128,96},{160,192},{192,160},{288,320},{3... | collective-permute-start | bytes 196616 | tf_op jit(solution)/shard_map/ppermute | solution.py:363
  12.0 5.0 %collective-permute-start.1 = (bf16[2,2,64,128]{3,2,1,0:T(8,128)(2,1)S(1)}, bf16[2,2,64,128]{3,2,1,0:T(8,128)(2,1)S(1)}, u32[]{:S(2)}, u32[]{:S(2)}) collective-permute-start(bf16[2,2,64,128]{3,2,1,0:T(8,128)(2,1)S(1)} %get-tuple-element.37), channel_id=1, source_target_pairs={{224,256},{256,224},{225,257},{257,225},{226,258},{258,226},{227,2... | collective-permute-start | bytes 196616 | tf_op jit(solution)/shard_map/ppermute | solution.py:362
  15.6 1.4 %collective-permute-start.2 = (bf16[2,64,128]{2,1,0:T(8,128)(2,1)S(1)}, bf16[2,64,128]{2,1,0:T(8,128)(2,1)S(1)}, u32[]{:S(2)}, u32[]{:S(2)}) collective-permute-start(bf16[2,64,128]{2,1,0:T(8,128)(2,1)S(1)} %get-tuple-element.38), channel_id=1, source_target_pairs={{199,296},{207,304},{215,312},{200,295},{208,303},{216,311},{295,2... | collective-permute-start | bytes 98312 | tf_op jit(solution)/shard_map/ppermute | solution.py:370
  16.3 6.2 %collective-permute-start.3 = (bf16[6,64,128]{2,1,0:T(8,128)(2,1)S(1)}, bf16[6,64,128]{2,1,0:T(8,128)(2,1)S(1)}, u32[]{:S(2)}, u32[]{:S(2)}) collective-permute-start(bf16[6,64,128]{2,1,0:T(8,128)(2,1)S(1)} %get-tuple-element.46), channel_id=1, source_target_pairs={{1,2},{3,4},{5,6},{7,8},{9,10},{11,12},{13,14},{15,16},{17,18},{19... | collective-permute-start | bytes 294920 | tf_op jit(solution)/shard_map/ppermute | solution.py:369
  17.1 5.4 %collective-permute-start.5 = (bf16[2,64,128]{2,1,0:T(8,128)(2,1)S(1)}, bf16[2,64,128]{2,1,0:T(8,128)(2,1)S(1)}, u32[]{:S(2)}, u32[]{:S(2)}) collective-permute-start(bf16[2,64,128]{2,1,0:T(8,128)(2,1)S(1)} %get-tuple-element.48), channel_id=1, source_target_pairs={{225,226},{227,228},{229,230},{233,234},{235,236},{237,238},{241,2... | collective-permute-start | bytes 98312 | tf_op jit(solution)/shard_map/ppermute | solution.py:379
  17.7 5.6 %collective-permute-start.4 = (bf16[6,64,128]{2,1,0:T(8,128)(2,1)S(1)}, bf16[6,64,128]{2,1,0:T(8,128)(2,1)S(1)}, u32[]{:S(2)}, u32[]{:S(2)}) collective-permute-start(bf16[6,64,128]{2,1,0:T(8,128)(2,1)S(1)} %get-tuple-element.47), channel_id=1, source_target_pairs={{0,1},{1,0},{2,3},{3,2},{4,5},{5,4},{6,7},{7,6},{8,9},{9,8},{10,11... | collective-permute-start | bytes 294920 | tf_op jit(solution)/shard_map/ppermute | solution.py:378
  28.8 31.4 %all-to-all-start = ((bf16[16,216,128]{2,1,0:T(8,128)(2,1)}), bf16[16,216,128]{2,1,0:T(8,128)(2,1)S(1)}, u32[]{:S(2)}, u32[]{:S(2)}) async-start(bf16[16,216,128]{2,1,0:T(8,128)(2,1)} %get-tuple-element.51), calls=%async_computation | async-start | bytes 1769472 | tf_op jit(solution)/shard_map/all_to_all | solution.py:403
  49.7 20.8 %collective-permute-start.6 = (bf16[2,2,64,128]{3,2,1,0:T(8,128)(2,1)S(1)}, bf16[2,2,64,128]{3,2,1,0:T(8,128)(2,1)S(1)}, u32[]{:S(2)}, u32[]{:S(2)}) collective-permute-start(bf16[2,2,64,128]{3,2,1,0:T(8,128)(2,1)S(1)} %get-tuple-element.53), channel_id=1, source_target_pairs={{64,32},{65,33},{66,34},{67,35},{68,36},{69,37},{70,38},{71,39},{7... | collective-permute-start | bytes 196616 | tf_op jit(solution)/shard_map/ppermute | solution.py:404
  51.0 25.2 %copy-start.1 = (bf16[2,2,64,128]{3,2,1,0:T(8,128)(2,1)S(1)}, bf16[2,2,64,128]{3,2,1,0:T(8,128)(2,1)}, u32[]{:S(2)}) copy-start(bf16[2,2,64,128]{3,2,1,0:T(8,128)(2,1)} %cot_ref.1) | copy-start | bytes 196612
  51.0 19.5 %collective-permute-start.7 = (bf16[4,64,128]{2,1,0:T(8,128)(2,1)S(1)}, bf16[4,64,128]{2,1,0:T(8,128)(2,1)S(1)}, u32[]{:S(2)}, u32[]{:S(2)}) collective-permute-start(bf16[4,64,128]{2,1,0:T(8,128)(2,1)S(1)} %get-tuple-element.54), channel_id=1, source_target_pairs={{1,2},{3,4},{5,6},{7,8},{9,10},{11,12},{13,14},{15,16},{17,18},{19... | collective-permute-start | bytes 196616 | tf_op jit(solution)/shard_map/ppermute | solution.py:405
  61.0 17.2 %all-to-all-start.1 = ((bf16[16,16,128]{2,1,0:T(8,128)(2,1)}), bf16[16,16,128]{2,1,0:T(8,128)(2,1)S(1)}, u32[]{:S(2)}, u32[]{:S(2)}) async-start(bf16[16,16,128]{2,1,0:T(8,128)(2,1)} %shard_map.64), calls=%async_computation.1 | async-start | bytes 131072 | tf_op jit(solution)/shard_map/all_to_all | solution.py:407
  70.5 5.7 %collective-permute-start.9 = (bf16[4,64,128]{2,1,0:T(8,128)(2,1)S(1)}, bf16[4,64,128]{2,1,0:T(8,128)(2,1)S(1)}, u32[]{:S(2)}, u32[]{:S(2)}) collective-permute-start(bf16[4,64,128]{2,1,0:T(8,128)(2,1)S(1)} %get-tuple-element.61), channel_id=1, source_target_pairs={{0,1},{1,0},{2,3},{3,2},{4,5},{5,4},{6,7},{7,6},{8,9},{9,8},{10,11... | collective-permute-start | bytes 196616 | tf_op jit(solution)/shard_map/ppermute | solution.py:414
  73.6 1.3 %collective-permute-start.8 = (bf16[2,64,128]{2,1,0:T(8,128)(2,1)S(1)}, bf16[2,64,128]{2,1,0:T(8,128)(2,1)S(1)}, u32[]{:S(2)}, u32[]{:S(2)}) collective-permute-start(bf16[2,64,128]{2,1,0:T(8,128)(2,1)S(1)} %get-tuple-element.60), channel_id=1, source_target_pairs={{33,34},{35,36},{37,38},{41,42},{43,44},{45,46},{49,50},{51,52},{5... | collective-permute-start | bytes 98312 | tf_op jit(solution)/shard_map/ppermute | solution.py:415
